TPU v7x, 256 devices: a whole 4x4x8 slice. The times are simulated.
256 devices in a mesh: lon: 16 (over y_hi, z), lat: 16 (over x, y_lo, core).
Axes of the slice: x: 4, y: 4 (y_hi: 2, y_lo: 2; y = y_hi * 2 + y_lo), z: 8, core: 2. Of those that a mesh axis runs over, the one named last changes fastest.
Arguments:
- queries: bfloat16 [32, 1024, 512], P('lat', 'lon'), may hold values from -32 to 32
- keys: bfloat16 [32, 1024, 512], P('lat', 'lon'), may hold values from -32 to 32
- values: bfloat16 [32, 1024, 512], P('lat', 'lon'), may hold values from -6 to 6
- upstream: bfloat16 [32, 1024, 1024], P('lat', 'lon'), may hold values from -6 to 6
- out_weight: bfloat16 [512, 1024], replicated, may hold values from -0.25 to 0.25
- average: float32 [512, 1024], P('lat'), may hold values from -6 to 6
- nbr_lon: int32 [32, 16, 8], P('lat', 'lon'), may hold values from 0 to 15, as said below
- nbr_lat: int32 [32, 16, 8], P('lat', 'lon'), may hold values from 0 to 1, as said below
- counts: int32 [32, 16], P('lat', 'lon'), may hold values from 1 to 8
Outputs:
- grad_queries: bfloat16 [32, 1024, 512], P('lat', 'lon')
- grad_keys: bfloat16 [32, 1024, 512], P('lat', 'lon')
- grad_values: bfloat16 [32, 1024, 512], P('lat', 'lon')
- updated: float32 [512, 1024], P('lat')
- next_weights: bfloat16 [512, 1024], replicated
Inputs may be any that keep to these rules, and one draw needn't show every extreme that they name: `nbr_lon`: slot 0 of each list names the query's own longitude block. `nbr_lat`: rows are counted within the query's own band of 2 rows; slot 0 names the query's own row.
All inputs are finite; a program needn't handle non-finite values.
Results may differ from a plain program's by a relative error of at most 0.024.
Values may be sent and summed in bfloat16 or wider, within the bound.
No kernel may reach another device: no remote copies, remote signals or barrier semaphores. Data moves between devices by JAX's collectives and lax.ppermute only.
A program may use at most 64 MiB of HBM per device.

v0:
```python
import jax
import jax.numpy as jnp
from jax import lax
from jax.sharding import PartitionSpec as P

D = 1024
HEADS = 8
HEAD = 64
BLOCK = 64
NB = 8
ROWS = 2
HD = 512


learn_rate = 0.01
decay_rate = 0.9


def from_behind(shard, axis, by):
    size = lax.axis_size(axis)
    return lax.ppermute(shard, axis, [(i, (i + by) % size) for i in range(size)])


def fwd_next(key_tile, value_tile):
    return from_behind((key_tile, value_tile), "lon", 1)


def bwd_next(key_tile, value_tile):
    return from_behind((key_tile, value_tile), "lon", 1)


def pass_grads(key_sum, value_sum):
    return from_behind((key_sum, value_sum), "lon", 1)


def on_device(queries, keys, values, upstream, out_weight, average, nbr_lon, nbr_lat, counts):
    cycle_size = lax.axis_size("lon")
    lon_index = lax.axis_index("lon")
    cells = ROWS * BLOCK
    score_scale = HEAD ** (-0.5)
    query_cells = queries.reshape(cells, HEADS, HEAD)
    key_flat = keys.reshape(cells, HD)
    value_flat = values.reshape(cells, HD)
    upstream_flat = upstream.reshape(cells, D)
    lon_list = nbr_lon.reshape(ROWS, NB)
    lat_list = nbr_lat.reshape(ROWS, NB)
    live_slots = jnp.arange(NB)[None, :] < counts

    def visible_cells(source):
        hits = live_slots & (lon_list == source)
        allowed = jnp.any(
            hits[:, :, None] & (lat_list[:, :, None] == jnp.arange(ROWS)[None, None, :]), axis=1
        )
        return jnp.repeat(jnp.repeat(allowed, BLOCK, 0), BLOCK, 1)[None]

    def tile_scores(key_tile, source):
        key_heads = key_tile.reshape(cells, HEADS, HEAD)
        scores_now = (
            jnp.einsum("chd,ehd->hce", query_cells, key_heads, preferred_element_type=jnp.float32)
            * score_scale
        )
        return (scores_now, visible_cells(source))

    def forward_step(carried, key_tile, value_tile, source):
        running, totals, summed = carried
        scores_now, visible = tile_scores(key_tile, source)
        scores_now = jnp.where(visible, scores_now, -1e30)
        new_running = jnp.maximum(running, jnp.max(scores_now, -1))
        weights_now = jnp.where(visible, jnp.exp(scores_now - new_running[:, :, None]), 0.0)
        rescale = jnp.exp(running - new_running)
        totals = totals * rescale + jnp.sum(weights_now, -1)
        value_heads = value_tile.reshape(cells, HEADS, HEAD).astype(jnp.float32)
        summed = summed * rescale.T[:, :, None] + jnp.einsum(
            "hce,ehd->chd", weights_now, value_heads, preferred_element_type=jnp.float32
        )
        return (new_running, totals, summed)

    start_state = (
        jnp.full((HEADS, cells), -1e30, jnp.float32),
        jnp.zeros((HEADS, cells), jnp.float32),
        jnp.zeros((cells, HEADS, HEAD), jnp.float32),
    )
    start_stores = ()

    def forward_turn(step, loop_state):
        carried, key_tile, value_tile, stores = loop_state
        source = (lon_index - step) % cycle_size
        carried = forward_step(carried, key_tile, value_tile, source)
        key_tile, value_tile = fwd_next(key_tile, value_tile)
        return (carried, key_tile, value_tile, stores)

    carried, key_tile, value_tile, stores = lax.fori_loop(
        0, cycle_size - 1, forward_turn, (start_state, key_flat, value_flat, start_stores)
    )
    last_source = (lon_index - cycle_size + 1) % cycle_size
    running, totals, summed = forward_step(carried, key_tile, value_tile, last_source)
    lse = running + jnp.log(totals)
    attended = (summed / totals.T[:, :, None]).reshape(cells, HD).astype(jnp.bfloat16)
    attn_grad = jnp.einsum(
        "cd,ed->ce", upstream_flat, out_weight, preferred_element_type=jnp.float32
    ).astype(jnp.bfloat16)
    grad_heads = attn_grad.reshape(cells, HEADS, HEAD)
    delta = jnp.einsum(
        "chd,chd->hc",
        grad_heads,
        attended.reshape(cells, HEADS, HEAD),
        preferred_element_type=jnp.float32,
    )

    def fetch_tiles(key_tile, value_tile):
        return (key_tile, value_tile)

    def advance_tiles(key_tile, value_tile):
        return bwd_next(key_tile, value_tile)

    def backward_step(carried_key, carried_value, source):
        key_tile, value_tile = fetch_tiles(carried_key, carried_value)
        scores_now, visible = tile_scores(key_tile, source)
        probs = jnp.where(visible, jnp.exp(scores_now - lse[:, :, None]), 0.0)
        prob_bf = probs.astype(jnp.bfloat16)
        key_heads = key_tile.reshape(cells, HEADS, HEAD)
        value_heads = value_tile.reshape(cells, HEADS, HEAD)
        prob_grad = jnp.einsum(
            "chd,ehd->hce", grad_heads, value_heads, preferred_element_type=jnp.float32
        )
        score_grad = (probs * (prob_grad - delta[:, :, None])).astype(jnp.bfloat16)
        value_part = jnp.einsum(
            "hce,chd->ehd", prob_bf, grad_heads, preferred_element_type=jnp.float32
        )
        query_part = jnp.einsum(
            "hce,ehd->chd", score_grad, key_heads, preferred_element_type=jnp.float32
        )
        key_part = jnp.einsum(
            "hce,chd->ehd", score_grad, query_cells, preferred_element_type=jnp.float32
        )
        return (query_part, key_part, value_part)

    zero_heads = jnp.zeros((cells, HEADS, HEAD), jnp.float32)

    def backward_turn(step, loop_state):
        key_tile, value_tile, grad_q, key_sum, value_sum = loop_state
        query_part, key_part, value_part = backward_step(
            key_tile, value_tile, (lon_index - step) % cycle_size
        )
        key_sum, value_sum = pass_grads(key_sum + key_part, value_sum + value_part)
        key_tile, value_tile = advance_tiles(key_tile, value_tile)
        return (key_tile, value_tile, grad_q + query_part, key_sum, value_sum)

    key_tile, value_tile, grad_q, key_sum, value_sum = lax.fori_loop(
        0, cycle_size - 1, backward_turn, (key_flat, value_flat, zero_heads, zero_heads, zero_heads)
    )
    query_part, key_part, value_part = backward_step(key_tile, value_tile, last_source)
    grad_q = grad_q + query_part
    grad_k, grad_v = pass_grads(key_sum + key_part, value_sum + value_part)
    grad_queries = (grad_q * score_scale).reshape(ROWS, BLOCK, HD).astype(jnp.bfloat16)
    grad_keys = (grad_k * score_scale).reshape(ROWS, BLOCK, HD).astype(jnp.bfloat16)
    grad_values = grad_v.reshape(ROWS, BLOCK, HD).astype(jnp.bfloat16)
    owner_rows = HD // lax.axis_size("lat")
    band_sum = lax.psum_scatter(
        jnp.einsum("ce,cd->ed", attended, upstream_flat, preferred_element_type=jnp.float32),
        "lat",
        scatter_dimension=0,
        tiled=True,
    )
    own_weight = lax.dynamic_slice_in_dim(
        out_weight, lax.axis_index("lat") * owner_rows, owner_rows, 0
    ).astype(jnp.float32)
    weight_grad = lax.psum(band_sum, "lon")
    updated = own_weight - learn_rate * weight_grad
    averaged = decay_rate * average + (1.0 - decay_rate) * updated
    next_weights = lax.all_gather(averaged.astype(jnp.bfloat16), "lat", axis=0, tiled=True)
    return (grad_queries, grad_keys, grad_values, updated, next_weights)


def solution(mesh):
    placed = (
        P("lat", "lon", None),
        P("lat", "lon", None),
        P("lat", "lon", None),
        P("lat", "lon", None),
        P(),
        P("lat", None),
        P("lat", "lon", None),
        P("lat", "lon", None),
        P("lat", "lon"),
    )
    return jax.shard_map(
        on_device,
        mesh=mesh,
        in_specs=placed,
        out_specs=(
            P("lat", "lon", None),
            P("lat", "lon", None),
            P("lat", "lon", None),
            P("lat", None),
            P(),
        ),
        check_vma=False,
    )
```

profile of v0, /device:TPU:2, one launch (start us, length us, event | category | flops | bytes accessed | tf_op | source)
XLA Modules:
  0.0 750.3 jit_solution(8565696380295885702)
XLA Ops:
  14.5 165.0 %while.48 = (s32[]{:T(128)}, f32[8,128]{1,0:T(8,128)S(1)}, f32[8,128]{1,0:T(8,128)S(1)}, f32[128,8,64]{0,2,1:T(8,128)S(1)}, bf16[128,512]{0,1:T(8,128)(2,1)S(1)}...) while((s32[]{:T(128)}, f32[8,128]{1,0:T(8,128)S(1)}, ...), condition=%wide.region_4.5_spmd.clone, body=%wide.region_0.4_spmd.clone.sunk | while | flops 34805912 | bytes 4195870 | solution.py:92
  14.5 2.0 collective-permute-start
  16.5 2.0 collective-permute-start.1
  19.7 7.7 %collective-permute-done = bf16[128,512]{0,1:T(8,128)(2,1)S(1)} collective-permute-done((bf16[128,512]{0,1:T(8,128)(2,1)S(1)}, bf16[128,512]{0,1:T(8,128)(2,1)S(1)}, u32[]{:S(2)}, u32[]{:S(2)}) %collective-permute-start) | collective-permute-done | bytes 131104 | tf_op jit(solution)/shard_map/while/body/eval_jaxpr/ppermute | solution.py:21
  30.8 8.3 %collective-permute-done = bf16[128,512]{0,1:T(8,128)(2,1)S(1)} collective-permute-done((bf16[128,512]{0,1:T(8,128)(2,1)S(1)}, bf16[128,512]{0,1:T(8,128)(2,1)S(1)}, u32[]{:S(2)}, u32[]{:S(2)}) %collective-permute-start) | collective-permute-done | bytes 131104 | tf_op jit(solution)/shard_map/while/body/eval_jaxpr/ppermute | solution.py:21
  42.0 7.4 collective-permute-done
  52.3 7.2 collective-permute-done
  62.4 7.2 collective-permute-done
  72.4 7.2 collective-permute-done
  82.5 7.2 collective-permute-done
  89.7 2.2 collective-permute-done.1
  93.4 7.8 %collective-permute-done = bf16[128,512]{0,1:T(8,128)(2,1)S(1)} collective-permute-done((bf16[128,512]{0,1:T(8,128)(2,1)S(1)}, bf16[128,512]{0,1:T(8,128)(2,1)S(1)}, u32[]{:S(2)}, u32[]{:S(2)}) %collective-permute-start) | collective-permute-done | bytes 131104 | tf_op jit(solution)/shard_map/while/body/eval_jaxpr/ppermute | solution.py:21
  101.2 2.8 collective-permute-done.1
  105.4 8.6 %collective-permute-done = bf16[128,512]{0,1:T(8,128)(2,1)S(1)} collective-permute-done((bf16[128,512]{0,1:T(8,128)(2,1)S(1)}, bf16[128,512]{0,1:T(8,128)(2,1)S(1)}, u32[]{:S(2)}, u32[]{:S(2)}) %collective-permute-start) | collective-permute-done | bytes 131104 | tf_op jit(solution)/shard_map/while/body/eval_jaxpr/ppermute | solution.py:21
  114.1 2.5 collective-permute-done.1
  118.0 8.7 %collective-permute-done = bf16[128,512]{0,1:T(8,128)(2,1)S(1)} collective-permute-done((bf16[128,512]{0,1:T(8,128)(2,1)S(1)}, bf16[128,512]{0,1:T(8,128)(2,1)S(1)}, u32[]{:S(2)}, u32[]{:S(2)}) %collective-permute-start) | collective-permute-done | bytes 131104 | tf_op jit(solution)/shard_map/while/body/eval_jaxpr/ppermute | solution.py:21
  129.7 8.0 %collective-permute-done = bf16[128,512]{0,1:T(8,128)(2,1)S(1)} collective-permute-done((bf16[128,512]{0,1:T(8,128)(2,1)S(1)}, bf16[128,512]{0,1:T(8,128)(2,1)S(1)}, u32[]{:S(2)}, u32[]{:S(2)}) %collective-permute-start) | collective-permute-done | bytes 131104 | tf_op jit(solution)/shard_map/while/body/eval_jaxpr/ppermute | solution.py:21
  140.6 7.2 collective-permute-done
  150.7 7.2 collective-permute-done
  160.7 7.2 collective-permute-done
  170.8 7.2 collective-permute-done
  182.0 53.7 %reduce-scatter.2.cloned.1.call-done = f32[32,1024]{1,0:T(8,128)} async-done(((f32[512,1024]{1,0:T(8,128)}), f32[32,1024]{1,0:T(8,128)}) %reduce-scatter.2.cloned.1.call-update) | async-done | bytes 131088 | tf_op jit(solution)/shard_map/reduce_scatter | solution.py:159
  235.7 162.4 %all-reduce.2.cloned.1.call-done = f32[32,1024]{1,0:T(8,128)} async-done(((f32[32,1024]{1,0:T(8,128)}), f32[32,1024]{1,0:T(8,128)}) %all-reduce.2.cloned.1.call-update) | async-done | bytes 131088 | tf_op jit(solution)/shard_map/psum | solution.py:168
  399.8 327.5 %while.49 = (s32[]{:T(128)}, bf16[128,512]{0,1:T(8,128)(2,1)S(1)}, bf16[128,512]{0,1:T(8,128)(2,1)S(1)}, f32[128,8,64]{0,2,1:T(8,128)S(1)}, f32[128,8,64]{0,2,1:...) while((s32[]{:T(128)}, bf16[128,512]{0,1:T(8,128)(2,1)S(1)}, ...), condition=%wide.region_10.11_spmd.clone, body=%wide.region_8.10_spmd.clone.sunk | while | flops 85065880 | bytes 8595076 | solution.py:149
  403.0 14.3 %collective-permute-done.2 = bf16[128,512]{0,1:T(8,128)(2,1)S(1)} collective-permute-done((bf16[128,512]{0,1:T(8,128)(2,1)S(1)}, bf16[128,512]{0,1:T(8,128)(2,1)S(1)}, u32[]{:S(2)}, u32[]{:S(2)}) %collective-permute-start.2) | collective-permute-done | bytes 131104 | tf_op jit(solution)/shard_map/while/body/eval_jaxpr/ppermute | solution.py:21
  417.3 2.8 collective-permute-done.3
  423.5 15.2 %collective-permute-done.2 = bf16[128,512]{0,1:T(8,128)(2,1)S(1)} collective-permute-done((bf16[128,512]{0,1:T(8,128)(2,1)S(1)}, bf16[128,512]{0,1:T(8,128)(2,1)S(1)}, u32[]{:S(2)}, u32[]{:S(2)}) %collective-permute-start.2) | collective-permute-done | bytes 131104 | tf_op jit(solution)/shard_map/while/body/eval_jaxpr/ppermute | solution.py:21
  438.7 2.8 collective-permute-done.3
  446.4 14.8 %collective-permute-done.2 = bf16[128,512]{0,1:T(8,128)(2,1)S(1)} collective-permute-done((bf16[128,512]{0,1:T(8,128)(2,1)S(1)}, bf16[128,512]{0,1:T(8,128)(2,1)S(1)}, u32[]{:S(2)}, u32[]{:S(2)}) %collective-permute-start.2) | collective-permute-done | bytes 131104 | tf_op jit(solution)/shard_map/while/body/eval_jaxpr/ppermute | solution.py:21
  461.1 2.8 collective-permute-done.3
  466.2 2.4 collective-permute-start.3
  468.9 15.7 %collective-permute-done.2 = bf16[128,512]{0,1:T(8,128)(2,1)S(1)} collective-permute-done((bf16[128,512]{0,1:T(8,128)(2,1)S(1)}, bf16[128,512]{0,1:T(8,128)(2,1)S(1)}, u32[]{:S(2)}, u32[]{:S(2)}) %collective-permute-start.2) | collective-permute-done | bytes 131104 | tf_op jit(solution)/shard_map/while/body/eval_jaxpr/ppermute | solution.py:21
  484.7 2.8 collective-permute-done.3
  490.7 18.7 %collective-permute-done.2 = bf16[128,512]{0,1:T(8,128)(2,1)S(1)} collective-permute-done((bf16[128,512]{0,1:T(8,128)(2,1)S(1)}, bf16[128,512]{0,1:T(8,128)(2,1)S(1)}, u32[]{:S(2)}, u32[]{:S(2)}) %collective-permute-start.2) | collective-permute-done | bytes 131104 | tf_op jit(solution)/shard_map/while/body/eval_jaxpr/ppermute | solution.py:21
  509.4 2.8 collective-permute-done.3
  514.6 20.4 %collective-permute-done.2 = bf16[128,512]{0,1:T(8,128)(2,1)S(1)} collective-permute-done((bf16[128,512]{0,1:T(8,128)(2,1)S(1)}, bf16[128,512]{0,1:T(8,128)(2,1)S(1)}, u32[]{:S(2)}, u32[]{:S(2)}) %collective-permute-start.2) | collective-permute-done | bytes 131104 | tf_op jit(solution)/shard_map/while/body/eval_jaxpr/ppermute | solution.py:21
  535.0 2.7 collective-permute-done.3
  540.2 20.4 %collective-permute-done.2 = bf16[128,512]{0,1:T(8,128)(2,1)S(1)} collective-permute-done((bf16[128,512]{0,1:T(8,128)(2,1)S(1)}, bf16[128,512]{0,1:T(8,128)(2,1)S(1)}, u32[]{:S(2)}, u32[]{:S(2)}) %collective-permute-start.2) | collective-permute-done | bytes 131104 | tf_op jit(solution)/shard_map/while/body/eval_jaxpr/ppermute | solution.py:21
  564.9 20.0 %collective-permute-done.2 = bf16[128,512]{0,1:T(8,128)(2,1)S(1)} collective-permute-done((bf16[128,512]{0,1:T(8,128)(2,1)S(1)}, bf16[128,512]{0,1:T(8,128)(2,1)S(1)}, u32[]{:S(2)}, u32[]{:S(2)}) %collective-permute-start.2) | collective-permute-done | bytes 131104 | tf_op jit(solution)/shard_map/while/body/eval_jaxpr/ppermute | solution.py:21
  588.7 19.0 %collective-permute-done.2 = bf16[128,512]{0,1:T(8,128)(2,1)S(1)} collective-permute-done((bf16[128,512]{0,1:T(8,128)(2,1)S(1)}, bf16[128,512]{0,1:T(8,128)(2,1)S(1)}, u32[]{:S(2)}, u32[]{:S(2)}) %collective-permute-start.2) | collective-permute-done | bytes 131104 | tf_op jit(solution)/shard_map/while/body/eval_jaxpr/ppermute | solution.py:21
  611.6 18.1 %collective-permute-done.2 = bf16[128,512]{0,1:T(8,128)(2,1)S(1)} collective-permute-done((bf16[128,512]{0,1:T(8,128)(2,1)S(1)}, bf16[128,512]{0,1:T(8,128)(2,1)S(1)}, u32[]{:S(2)}, u32[]{:S(2)}) %collective-permute-start.2) | collective-permute-done | bytes 131104 | tf_op jit(solution)/shard_map/while/body/eval_jaxpr/ppermute | solution.py:21
  633.6 17.2 %collective-permute-done.2 = bf16[128,512]{0,1:T(8,128)(2,1)S(1)} collective-permute-done((bf16[128,512]{0,1:T(8,128)(2,1)S(1)}, bf16[128,512]{0,1:T(8,128)(2,1)S(1)}, u32[]{:S(2)}, u32[]{:S(2)}) %collective-permute-start.2) | collective-permute-done | bytes 131104 | tf_op jit(solution)/shard_map/while/body/eval_jaxpr/ppermute | solution.py:21
  654.7 16.3 %collective-permute-done.2 = bf16[128,512]{0,1:T(8,128)(2,1)S(1)} collective-permute-done((bf16[128,512]{0,1:T(8,128)(2,1)S(1)}, bf16[128,512]{0,1:T(8,128)(2,1)S(1)}, u32[]{:S(2)}, u32[]{:S(2)}) %collective-permute-start.2) | collective-permute-done | bytes 131104 | tf_op jit(solution)/shard_map/while/body/eval_jaxpr/ppermute | solution.py:21
  674.8 15.4 %collective-permute-done.2 = bf16[128,512]{0,1:T(8,128)(2,1)S(1)} collective-permute-done((bf16[128,512]{0,1:T(8,128)(2,1)S(1)}, bf16[128,512]{0,1:T(8,128)(2,1)S(1)}, u32[]{:S(2)}, u32[]{:S(2)}) %collective-permute-start.2) | collective-permute-done | bytes 131104 | tf_op jit(solution)/shard_map/while/body/eval_jaxpr/ppermute | solution.py:21
  694.0 14.4 %collective-permute-done.2 = bf16[128,512]{0,1:T(8,128)(2,1)S(1)} collective-permute-done((bf16[128,512]{0,1:T(8,128)(2,1)S(1)}, bf16[128,512]{0,1:T(8,128)(2,1)S(1)}, u32[]{:S(2)}, u32[]{:S(2)}) %collective-permute-start.2) | collective-permute-done | bytes 131104 | tf_op jit(solution)/shard_map/while/body/eval_jaxpr/ppermute | solution.py:21
  712.4 13.4 %collective-permute-done.2 = bf16[128,512]{0,1:T(8,128)(2,1)S(1)} collective-permute-done((bf16[128,512]{0,1:T(8,128)(2,1)S(1)}, bf16[128,512]{0,1:T(8,128)(2,1)S(1)}, u32[]{:S(2)}, u32[]{:S(2)}) %collective-permute-start.2) | collective-permute-done | bytes 131104 | tf_op jit(solution)/shard_map/while/body/eval_jaxpr/ppermute | solution.py:21
  729.8 9.8 %collective-permute-done.7 = bf16[128,8,64]{0,2,1:T(8,128)(2,1)S(1)} collective-permute-done((bf16[128,8,64]{0,2,1:T(8,128)(2,1)S(1)}, bf16[128,8,64]{0,2,1:T(8,128)(2,1)S(1)}, u32[]{:S(2)}, u32[]{:S(2)}) %collective-permute-start.7) | collective-permute-done | bytes 131104 | tf_op jit(solution)/shard_map/ppermute | solution.py:21
  741.5 2.3 copy.140
  (617 shorter events, 106.9 us)
Async XLA Ops:
  7.2 228.4 %reduce-scatter.2.cloned.1.call-start = ((), (), s32[]{:S(2)}) async-start(), calls=%async_computation.1 | async-start | bytes 2228224 | tf_op jit(solution)/shard_map/reduce_scatter | solution.py:159
  181.9 216.1 %all-reduce.2.cloned.1.call-start = ((), (), s32[]{:S(2)}) async-start(), calls=%async_computation.2 | async-start | bytes 262144 | tf_op jit(solution)/shard_map/psum | solution.py:168
  235.7 505.9 %all-gather.2.cloned.1.call-start = ((), (), s32[]{:S(2)}) async-start(), calls=%async_computation.3 | async-start | bytes 1114112 | tf_op jit(solution)/shard_map/all_gather | solution.py:171
  401.4 18.7 %collective-permute-start.4 = (f32[128,8,64]{0,2,1:T(8,128)S(1)}, f32[128,8,64]{0,2,1:T(8,128)S(1)}, u32[]{:S(2)}, u32[]{:S(2)}) collective-permute-start(f32[128,8,64]{0,2,1:T(8,128)S(1)} %fusion.122), channel_id=1, source_target_pairs={{0,16},{16,32},{32,48},{48,64},{64,80},{80,96},{96,112},{112,128},... | collective-permute-start | bytes 786440 | tf_op jit(solution)/shard_map/while/body/eval_jaxpr/ppermute | solution.py:21
  402.4 17.7 %collective-permute-start.5 = (f32[128,8,64]{0,2,1:T(8,128)S(1)}, f32[128,8,64]{0,2,1:T(8,128)S(1)}, u32[]{:S(2)}, u32[]{:S(2)}) collective-permute-start(f32[128,8,64]{0,2,1:T(8,128)S(1)} %fusion.123), channel_id=1, source_target_pairs={{0,16},{16,32},{32,48},{48,64},{64,80},{80,96},{96,112},{112,128},... | collective-permute-start | bytes 786440 | tf_op jit(solution)/shard_map/while/body/eval_jaxpr/ppermute | solution.py:21
  402.6 17.5 %collective-permute-start.3 = (bf16[128,512]{0,1:T(8,128)(2,1)S(1)}, bf16[128,512]{0,1:T(8,128)(2,1)S(1)}, u32[]{:S(2)}, u32[]{:S(2)}) collective-permute-start(bf16[128,512]{0,1:T(8,128)(2,1)S(1)} %copy.128), channel_id=1, source_target_pairs={{0,16},{16,32},{32,48},{48,64},{64,80},{80,96},{96,112},{112,128},... | collective-permute-start | bytes 393224 | tf_op jit(solution)/shard_map/while/body/eval_jaxpr/ppermute | solution.py:21
  421.7 19.8 %collective-permute-start.4 = (f32[128,8,64]{0,2,1:T(8,128)S(1)}, f32[128,8,64]{0,2,1:T(8,128)S(1)}, u32[]{:S(2)}, u32[]{:S(2)}) collective-permute-start(f32[128,8,64]{0,2,1:T(8,128)S(1)} %fusion.122), channel_id=1, source_target_pairs={{0,16},{16,32},{32,48},{48,64},{64,80},{80,96},{96,112},{112,128},... | collective-permute-start | bytes 786440 | tf_op jit(solution)/shard_map/while/body/eval_jaxpr/ppermute | solution.py:21
  422.0 19.5 %collective-permute-start.5 = (f32[128,8,64]{0,2,1:T(8,128)S(1)}, f32[128,8,64]{0,2,1:T(8,128)S(1)}, u32[]{:S(2)}, u32[]{:S(2)}) collective-permute-start(f32[128,8,64]{0,2,1:T(8,128)S(1)} %fusion.123), channel_id=1, source_target_pairs={{0,16},{16,32},{32,48},{48,64},{64,80},{80,96},{96,112},{112,128},... | collective-permute-start | bytes 786440 | tf_op jit(solution)/shard_map/while/body/eval_jaxpr/ppermute | solution.py:21
  423.0 18.5 %collective-permute-start.3 = (bf16[128,512]{0,1:T(8,128)(2,1)S(1)}, bf16[128,512]{0,1:T(8,128)(2,1)S(1)}, u32[]{:S(2)}, u32[]{:S(2)}) collective-permute-start(bf16[128,512]{0,1:T(8,128)(2,1)S(1)} %copy.128), channel_id=1, source_target_pairs={{0,16},{16,32},{32,48},{48,64},{64,80},{80,96},{96,112},{112,128},... | collective-permute-start | bytes 393224 | tf_op jit(solution)/shard_map/while/body/eval_jaxpr/ppermute | solution.py:21
  443.1 20.9 %collective-permute-start.4 = (f32[128,8,64]{0,2,1:T(8,128)S(1)}, f32[128,8,64]{0,2,1:T(8,128)S(1)}, u32[]{:S(2)}, u32[]{:S(2)}) collective-permute-start(f32[128,8,64]{0,2,1:T(8,128)S(1)} %fusion.122), channel_id=1, source_target_pairs={{0,16},{16,32},{32,48},{48,64},{64,80},{80,96},{96,112},{112,128},... | collective-permute-start | bytes 786440 | tf_op jit(solution)/shard_map/while/body/eval_jaxpr/ppermute | solution.py:21
  443.4 20.6 %collective-permute-start.5 = (f32[128,8,64]{0,2,1:T(8,128)S(1)}, f32[128,8,64]{0,2,1:T(8,128)S(1)}, u32[]{:S(2)}, u32[]{:S(2)}) collective-permute-start(f32[128,8,64]{0,2,1:T(8,128)S(1)} %fusion.123), channel_id=1, source_target_pairs={{0,16},{16,32},{32,48},{48,64},{64,80},{80,96},{96,112},{112,128},... | collective-permute-start | bytes 786440 | tf_op jit(solution)/shard_map/while/body/eval_jaxpr/ppermute | solution.py:21
  444.3 19.6 %collective-permute-start.3 = (bf16[128,512]{0,1:T(8,128)(2,1)S(1)}, bf16[128,512]{0,1:T(8,128)(2,1)S(1)}, u32[]{:S(2)}, u32[]{:S(2)}) collective-permute-start(bf16[128,512]{0,1:T(8,128)(2,1)S(1)} %copy.128), channel_id=1, source_target_pairs={{0,16},{16,32},{32,48},{48,64},{64,80},{80,96},{96,112},{112,128},... | collective-permute-start | bytes 393224 | tf_op jit(solution)/shard_map/while/body/eval_jaxpr/ppermute | solution.py:21
  465.5 22.0 %collective-permute-start.4 = (f32[128,8,64]{0,2,1:T(8,128)S(1)}, f32[128,8,64]{0,2,1:T(8,128)S(1)}, u32[]{:S(2)}, u32[]{:S(2)}) collective-permute-start(f32[128,8,64]{0,2,1:T(8,128)S(1)} %fusion.122), channel_id=1, source_target_pairs={{0,16},{16,32},{32,48},{48,64},{64,80},{80,96},{96,112},{112,128},... | collective-permute-start | bytes 786440 | tf_op jit(solution)/shard_map/while/body/eval_jaxpr/ppermute | solution.py:21
  465.8 21.7 %collective-permute-start.5 = (f32[128,8,64]{0,2,1:T(8,128)S(1)}, f32[128,8,64]{0,2,1:T(8,128)S(1)}, u32[]{:S(2)}, u32[]{:S(2)}) collective-permute-start(f32[128,8,64]{0,2,1:T(8,128)S(1)} %fusion.123), channel_id=1, source_target_pairs={{0,16},{16,32},{32,48},{48,64},{64,80},{80,96},{96,112},{112,128},... | collective-permute-start | bytes 786440 | tf_op jit(solution)/shard_map/while/body/eval_jaxpr/ppermute | solution.py:21
  465.9 18.7 %collective-permute-start.2 = (bf16[128,512]{0,1:T(8,128)(2,1)S(1)}, bf16[128,512]{0,1:T(8,128)(2,1)S(1)}, u32[]{:S(2)}, u32[]{:S(2)}) collective-permute-start(bf16[128,512]{0,1:T(8,128)(2,1)S(1)} %copy.127), channel_id=1, source_target_pairs={{0,16},{16,32},{32,48},{48,64},{64,80},{80,96},{96,112},{112,128},... | collective-permute-start | bytes 393224 | tf_op jit(solution)/shard_map/while/body/eval_jaxpr/ppermute | solution.py:21
  466.2 21.3 %collective-permute-start.3 = (bf16[128,512]{0,1:T(8,128)(2,1)S(1)}, bf16[128,512]{0,1:T(8,128)(2,1)S(1)}, u32[]{:S(2)}, u32[]{:S(2)}) collective-permute-start(bf16[128,512]{0,1:T(8,128)(2,1)S(1)} %copy.128), channel_id=1, source_target_pairs={{0,16},{16,32},{32,48},{48,64},{64,80},{80,96},{96,112},{112,128},... | collective-permute-start | bytes 393224 | tf_op jit(solution)/shard_map/while/body/eval_jaxpr/ppermute | solution.py:21
  489.1 23.1 %collective-permute-start.4 = (f32[128,8,64]{0,2,1:T(8,128)S(1)}, f32[128,8,64]{0,2,1:T(8,128)S(1)}, u32[]{:S(2)}, u32[]{:S(2)}) collective-permute-start(f32[128,8,64]{0,2,1:T(8,128)S(1)} %fusion.122), channel_id=1, source_target_pairs={{0,16},{16,32},{32,48},{48,64},{64,80},{80,96},{96,112},{112,128},... | collective-permute-start | bytes 786440 | tf_op jit(solution)/shard_map/while/body/eval_jaxpr/ppermute | solution.py:21
  489.4 22.8 %collective-permute-start.5 = (f32[128,8,64]{0,2,1:T(8,128)S(1)}, f32[128,8,64]{0,2,1:T(8,128)S(1)}, u32[]{:S(2)}, u32[]{:S(2)}) collective-permute-start(f32[128,8,64]{0,2,1:T(8,128)S(1)} %fusion.123), channel_id=1, source_target_pairs={{0,16},{16,32},{32,48},{48,64},{64,80},{80,96},{96,112},{112,128},... | collective-permute-start | bytes 786440 | tf_op jit(solution)/shard_map/while/body/eval_jaxpr/ppermute | solution.py:21
  489.4 19.9 %collective-permute-start.2 = (bf16[128,512]{0,1:T(8,128)(2,1)S(1)}, bf16[128,512]{0,1:T(8,128)(2,1)S(1)}, u32[]{:S(2)}, u32[]{:S(2)}) collective-permute-start(bf16[128,512]{0,1:T(8,128)(2,1)S(1)} %copy.127), channel_id=1, source_target_pairs={{0,16},{16,32},{32,48},{48,64},{64,80},{80,96},{96,112},{112,128},... | collective-permute-start | bytes 393224 | tf_op jit(solution)/shard_map/while/body/eval_jaxpr/ppermute | solution.py:21
  489.5 22.6 %collective-permute-start.3 = (bf16[128,512]{0,1:T(8,128)(2,1)S(1)}, bf16[128,512]{0,1:T(8,128)(2,1)S(1)}, u32[]{:S(2)}, u32[]{:S(2)}) collective-permute-start(bf16[128,512]{0,1:T(8,128)(2,1)S(1)} %copy.128), channel_id=1, source_target_pairs={{0,16},{16,32},{32,48},{48,64},{64,80},{80,96},{96,112},{112,128},... | collective-permute-start | bytes 393224 | tf_op jit(solution)/shard_map/while/body/eval_jaxpr/ppermute | solution.py:21
  513.7 24.0 %collective-permute-start.4 = (f32[128,8,64]{0,2,1:T(8,128)S(1)}, f32[128,8,64]{0,2,1:T(8,128)S(1)}, u32[]{:S(2)}, u32[]{:S(2)}) collective-permute-start(f32[128,8,64]{0,2,1:T(8,128)S(1)} %fusion.122), channel_id=1, source_target_pairs={{0,16},{16,32},{32,48},{48,64},{64,80},{80,96},{96,112},{112,128},... | collective-permute-start | bytes 786440 | tf_op jit(solution)/shard_map/while/body/eval_jaxpr/ppermute | solution.py:21
  514.0 23.7 %collective-permute-start.5 = (f32[128,8,64]{0,2,1:T(8,128)S(1)}, f32[128,8,64]{0,2,1:T(8,128)S(1)}, u32[]{:S(2)}, u32[]{:S(2)}) collective-permute-start(f32[128,8,64]{0,2,1:T(8,128)S(1)} %fusion.123), channel_id=1, source_target_pairs={{0,16},{16,32},{32,48},{48,64},{64,80},{80,96},{96,112},{112,128},... | collective-permute-start | bytes 786440 | tf_op jit(solution)/shard_map/while/body/eval_jaxpr/ppermute | solution.py:21
  514.1 20.9 %collective-permute-start.2 = (bf16[128,512]{0,1:T(8,128)(2,1)S(1)}, bf16[128,512]{0,1:T(8,128)(2,1)S(1)}, u32[]{:S(2)}, u32[]{:S(2)}) collective-permute-start(bf16[128,512]{0,1:T(8,128)(2,1)S(1)} %copy.127), channel_id=1, source_target_pairs={{0,16},{16,32},{32,48},{48,64},{64,80},{80,96},{96,112},{112,128},... | collective-permute-start | bytes 393224 | tf_op jit(solution)/shard_map/while/body/eval_jaxpr/ppermute | solution.py:21
  514.2 23.5 %collective-permute-start.3 = (bf16[128,512]{0,1:T(8,128)(2,1)S(1)}, bf16[128,512]{0,1:T(8,128)(2,1)S(1)}, u32[]{:S(2)}, u32[]{:S(2)}) collective-permute-start(bf16[128,512]{0,1:T(8,128)(2,1)S(1)} %copy.128), channel_id=1, source_target_pairs={{0,16},{16,32},{32,48},{48,64},{64,80},{80,96},{96,112},{112,128},... | collective-permute-start | bytes 393224 | tf_op jit(solution)/shard_map/while/body/eval_jaxpr/ppermute | solution.py:21
  539.3 23.1 %collective-permute-start.4 = (f32[128,8,64]{0,2,1:T(8,128)S(1)}, f32[128,8,64]{0,2,1:T(8,128)S(1)}, u32[]{:S(2)}, u32[]{:S(2)}) collective-permute-start(f32[128,8,64]{0,2,1:T(8,128)S(1)} %fusion.122), channel_id=1, source_target_pairs={{0,16},{16,32},{32,48},{48,64},{64,80},{80,96},{96,112},{112,128},... | collective-permute-start | bytes 786440 | tf_op jit(solution)/shard_map/while/body/eval_jaxpr/ppermute | solution.py:21
  539.6 22.8 %collective-permute-start.5 = (f32[128,8,64]{0,2,1:T(8,128)S(1)}, f32[128,8,64]{0,2,1:T(8,128)S(1)}, u32[]{:S(2)}, u32[]{:S(2)}) collective-permute-start(f32[128,8,64]{0,2,1:T(8,128)S(1)} %fusion.123), channel_id=1, source_target_pairs={{0,16},{16,32},{32,48},{48,64},{64,80},{80,96},{96,112},{112,128},... | collective-permute-start | bytes 786440 | tf_op jit(solution)/shard_map/while/body/eval_jaxpr/ppermute | solution.py:21
  539.7 20.9 %collective-permute-start.2 = (bf16[128,512]{0,1:T(8,128)(2,1)S(1)}, bf16[128,512]{0,1:T(8,128)(2,1)S(1)}, u32[]{:S(2)}, u32[]{:S(2)}) collective-permute-start(bf16[128,512]{0,1:T(8,128)(2,1)S(1)} %copy.127), channel_id=1, source_target_pairs={{0,16},{16,32},{32,48},{48,64},{64,80},{80,96},{96,112},{112,128},... | collective-permute-start | bytes 393224 | tf_op jit(solution)/shard_map/while/body/eval_jaxpr/ppermute | solution.py:21
  539.8 22.6 %collective-permute-start.3 = (bf16[128,512]{0,1:T(8,128)(2,1)S(1)}, bf16[128,512]{0,1:T(8,128)(2,1)S(1)}, u32[]{:S(2)}, u32[]{:S(2)}) collective-permute-start(bf16[128,512]{0,1:T(8,128)(2,1)S(1)} %copy.128), channel_id=1, source_target_pairs={{0,16},{16,32},{32,48},{48,64},{64,80},{80,96},{96,112},{112,128},... | collective-permute-start | bytes 393224 | tf_op jit(solution)/shard_map/while/body/eval_jaxpr/ppermute | solution.py:21
  564.0 22.3 %collective-permute-start.4 = (f32[128,8,64]{0,2,1:T(8,128)S(1)}, f32[128,8,64]{0,2,1:T(8,128)S(1)}, u32[]{:S(2)}, u32[]{:S(2)}) collective-permute-start(f32[128,8,64]{0,2,1:T(8,128)S(1)} %fusion.122), channel_id=1, source_target_pairs={{0,16},{16,32},{32,48},{48,64},{64,80},{80,96},{96,112},{112,128},... | collective-permute-start | bytes 786440 | tf_op jit(solution)/shard_map/while/body/eval_jaxpr/ppermute | solution.py:21
  564.3 22.0 %collective-permute-start.5 = (f32[128,8,64]{0,2,1:T(8,128)S(1)}, f32[128,8,64]{0,2,1:T(8,128)S(1)}, u32[]{:S(2)}, u32[]{:S(2)}) collective-permute-start(f32[128,8,64]{0,2,1:T(8,128)S(1)} %fusion.123), channel_id=1, source_target_pairs={{0,16},{16,32},{32,48},{48,64},{64,80},{80,96},{96,112},{112,128},... | collective-permute-start | bytes 786440 | tf_op jit(solution)/shard_map/while/body/eval_jaxpr/ppermute | solution.py:21
  564.4 20.5 %collective-permute-start.2 = (bf16[128,512]{0,1:T(8,128)(2,1)S(1)}, bf16[128,512]{0,1:T(8,128)(2,1)S(1)}, u32[]{:S(2)}, u32[]{:S(2)}) collective-permute-start(bf16[128,512]{0,1:T(8,128)(2,1)S(1)} %copy.127), channel_id=1, source_target_pairs={{0,16},{16,32},{32,48},{48,64},{64,80},{80,96},{96,112},{112,128},... | collective-permute-start | bytes 393224 | tf_op jit(solution)/shard_map/while/body/eval_jaxpr/ppermute | solution.py:21
  564.5 21.8 %collective-permute-start.3 = (bf16[128,512]{0,1:T(8,128)(2,1)S(1)}, bf16[128,512]{0,1:T(8,128)(2,1)S(1)}, u32[]{:S(2)}, u32[]{:S(2)}) collective-permute-start(bf16[128,512]{0,1:T(8,128)(2,1)S(1)} %copy.128), channel_id=1, source_target_pairs={{0,16},{16,32},{32,48},{48,64},{64,80},{80,96},{96,112},{112,128},... | collective-permute-start | bytes 393224 | tf_op jit(solution)/shard_map/while/body/eval_jaxpr/ppermute | solution.py:21
  587.8 21.3 %collective-permute-start.4 = (f32[128,8,64]{0,2,1:T(8,128)S(1)}, f32[128,8,64]{0,2,1:T(8,128)S(1)}, u32[]{:S(2)}, u32[]{:S(2)}) collective-permute-start(f32[128,8,64]{0,2,1:T(8,128)S(1)} %fusion.122), channel_id=1, source_target_pairs={{0,16},{16,32},{32,48},{48,64},{64,80},{80,96},{96,112},{112,128},... | collective-permute-start | bytes 786440 | tf_op jit(solution)/shard_map/while/body/eval_jaxpr/ppermute | solution.py:21
  588.1 21.0 %collective-permute-start.5 = (f32[128,8,64]{0,2,1:T(8,128)S(1)}, f32[128,8,64]{0,2,1:T(8,128)S(1)}, u32[]{:S(2)}, u32[]{:S(2)}) collective-permute-start(f32[128,8,64]{0,2,1:T(8,128)S(1)} %fusion.123), channel_id=1, source_target_pairs={{0,16},{16,32},{32,48},{48,64},{64,80},{80,96},{96,112},{112,128},... | collective-permute-start | bytes 786440 | tf_op jit(solution)/shard_map/while/body/eval_jaxpr/ppermute | solution.py:21
  588.2 19.5 %collective-permute-start.2 = (bf16[128,512]{0,1:T(8,128)(2,1)S(1)}, bf16[128,512]{0,1:T(8,128)(2,1)S(1)}, u32[]{:S(2)}, u32[]{:S(2)}) collective-permute-start(bf16[128,512]{0,1:T(8,128)(2,1)S(1)} %copy.127), channel_id=1, source_target_pairs={{0,16},{16,32},{32,48},{48,64},{64,80},{80,96},{96,112},{112,128},... | collective-permute-start | bytes 393224 | tf_op jit(solution)/shard_map/while/body/eval_jaxpr/ppermute | solution.py:21
  588.3 20.8 %collective-permute-start.3 = (bf16[128,512]{0,1:T(8,128)(2,1)S(1)}, bf16[128,512]{0,1:T(8,128)(2,1)S(1)}, u32[]{:S(2)}, u32[]{:S(2)}) collective-permute-start(bf16[128,512]{0,1:T(8,128)(2,1)S(1)} %copy.128), channel_id=1, source_target_pairs={{0,16},{16,32},{32,48},{48,64},{64,80},{80,96},{96,112},{112,128},... | collective-permute-start | bytes 393224 | tf_op jit(solution)/shard_map/while/body/eval_jaxpr/ppermute | solution.py:21
  610.7 20.4 %collective-permute-start.4 = (f32[128,8,64]{0,2,1:T(8,128)S(1)}, f32[128,8,64]{0,2,1:T(8,128)S(1)}, u32[]{:S(2)}, u32[]{:S(2)}) collective-permute-start(f32[128,8,64]{0,2,1:T(8,128)S(1)} %fusion.122), channel_id=1, source_target_pairs={{0,16},{16,32},{32,48},{48,64},{64,80},{80,96},{96,112},{112,128},... | collective-permute-start | bytes 786440 | tf_op jit(solution)/shard_map/while/body/eval_jaxpr/ppermute | solution.py:21
  611.0 20.1 %collective-permute-start.5 = (f32[128,8,64]{0,2,1:T(8,128)S(1)}, f32[128,8,64]{0,2,1:T(8,128)S(1)}, u32[]{:S(2)}, u32[]{:S(2)}) collective-permute-start(f32[128,8,64]{0,2,1:T(8,128)S(1)} %fusion.123), channel_id=1, source_target_pairs={{0,16},{16,32},{32,48},{48,64},{64,80},{80,96},{96,112},{112,128},... | collective-permute-start | bytes 786440 | tf_op jit(solution)/shard_map/while/body/eval_jaxpr/ppermute | solution.py:21
  611.1 18.6 %collective-permute-start.2 = (bf16[128,512]{0,1:T(8,128)(2,1)S(1)}, bf16[128,512]{0,1:T(8,128)(2,1)S(1)}, u32[]{:S(2)}, u32[]{:S(2)}) collective-permute-start(bf16[128,512]{0,1:T(8,128)(2,1)S(1)} %copy.127), channel_id=1, source_target_pairs={{0,16},{16,32},{32,48},{48,64},{64,80},{80,96},{96,112},{112,128},... | collective-permute-start | bytes 393224 | tf_op jit(solution)/shard_map/while/body/eval_jaxpr/ppermute | solution.py:21
  611.2 19.9 %collective-permute-start.3 = (bf16[128,512]{0,1:T(8,128)(2,1)S(1)}, bf16[128,512]{0,1:T(8,128)(2,1)S(1)}, u32[]{:S(2)}, u32[]{:S(2)}) collective-permute-start(bf16[128,512]{0,1:T(8,128)(2,1)S(1)} %copy.128), channel_id=1, source_target_pairs={{0,16},{16,32},{32,48},{48,64},{64,80},{80,96},{96,112},{112,128},... | collective-permute-start | bytes 393224 | tf_op jit(solution)/shard_map/while/body/eval_jaxpr/ppermute | solution.py:21
  632.7 19.5 %collective-permute-start.4 = (f32[128,8,64]{0,2,1:T(8,128)S(1)}, f32[128,8,64]{0,2,1:T(8,128)S(1)}, u32[]{:S(2)}, u32[]{:S(2)}) collective-permute-start(f32[128,8,64]{0,2,1:T(8,128)S(1)} %fusion.122), channel_id=1, source_target_pairs={{0,16},{16,32},{32,48},{48,64},{64,80},{80,96},{96,112},{112,128},... | collective-permute-start | bytes 786440 | tf_op jit(solution)/shard_map/while/body/eval_jaxpr/ppermute | solution.py:21
  633.0 19.2 %collective-permute-start.5 = (f32[128,8,64]{0,2,1:T(8,128)S(1)}, f32[128,8,64]{0,2,1:T(8,128)S(1)}, u32[]{:S(2)}, u32[]{:S(2)}) collective-permute-start(f32[128,8,64]{0,2,1:T(8,128)S(1)} %fusion.123), channel_id=1, source_target_pairs={{0,16},{16,32},{32,48},{48,64},{64,80},{80,96},{96,112},{112,128},... | collective-permute-start | bytes 786440 | tf_op jit(solution)/shard_map/while/body/eval_jaxpr/ppermute | solution.py:21
  633.1 17.7 %collective-permute-start.2 = (bf16[128,512]{0,1:T(8,128)(2,1)S(1)}, bf16[128,512]{0,1:T(8,128)(2,1)S(1)}, u32[]{:S(2)}, u32[]{:S(2)}) collective-permute-start(bf16[128,512]{0,1:T(8,128)(2,1)S(1)} %copy.127), channel_id=1, source_target_pairs={{0,16},{16,32},{32,48},{48,64},{64,80},{80,96},{96,112},{112,128},... | collective-permute-start | bytes 393224 | tf_op jit(solution)/shard_map/while/body/eval_jaxpr/ppermute | solution.py:21
  633.2 19.0 %collective-permute-start.3 = (bf16[128,512]{0,1:T(8,128)(2,1)S(1)}, bf16[128,512]{0,1:T(8,128)(2,1)S(1)}, u32[]{:S(2)}, u32[]{:S(2)}) collective-permute-start(bf16[128,512]{0,1:T(8,128)(2,1)S(1)} %copy.128), channel_id=1, source_target_pairs={{0,16},{16,32},{32,48},{48,64},{64,80},{80,96},{96,112},{112,128},... | collective-permute-start | bytes 393224 | tf_op jit(solution)/shard_map/while/body/eval_jaxpr/ppermute | solution.py:21
  653.8 18.6 %collective-permute-start.4 = (f32[128,8,64]{0,2,1:T(8,128)S(1)}, f32[128,8,64]{0,2,1:T(8,128)S(1)}, u32[]{:S(2)}, u32[]{:S(2)}) collective-permute-start(f32[128,8,64]{0,2,1:T(8,128)S(1)} %fusion.122), channel_id=1, source_target_pairs={{0,16},{16,32},{32,48},{48,64},{64,80},{80,96},{96,112},{112,128},... | collective-permute-start | bytes 786440 | tf_op jit(solution)/shard_map/while/body/eval_jaxpr/ppermute | solution.py:21
  654.1 18.3 %collective-permute-start.5 = (f32[128,8,64]{0,2,1:T(8,128)S(1)}, f32[128,8,64]{0,2,1:T(8,128)S(1)}, u32[]{:S(2)}, u32[]{:S(2)}) collective-permute-start(f32[128,8,64]{0,2,1:T(8,128)S(1)} %fusion.123), channel_id=1, source_target_pairs={{0,16},{16,32},{32,48},{48,64},{64,80},{80,96},{96,112},{112,128},... | collective-permute-start | bytes 786440 | tf_op jit(solution)/shard_map/while/body/eval_jaxpr/ppermute | solution.py:21
  654.3 18.1 %collective-permute-start.3 = (bf16[128,512]{0,1:T(8,128)(2,1)S(1)}, bf16[128,512]{0,1:T(8,128)(2,1)S(1)}, u32[]{:S(2)}, u32[]{:S(2)}) collective-permute-start(bf16[128,512]{0,1:T(8,128)(2,1)S(1)} %copy.128), channel_id=1, source_target_pairs={{0,16},{16,32},{32,48},{48,64},{64,80},{80,96},{96,112},{112,128},... | collective-permute-start | bytes 393224 | tf_op jit(solution)/shard_map/while/body/eval_jaxpr/ppermute | solution.py:21
  673.9 17.6 %collective-permute-start.4 = (f32[128,8,64]{0,2,1:T(8,128)S(1)}, f32[128,8,64]{0,2,1:T(8,128)S(1)}, u32[]{:S(2)}, u32[]{:S(2)}) collective-permute-start(f32[128,8,64]{0,2,1:T(8,128)S(1)} %fusion.122), channel_id=1, source_target_pairs={{0,16},{16,32},{32,48},{48,64},{64,80},{80,96},{96,112},{112,128},... | collective-permute-start | bytes 786440 | tf_op jit(solution)/shard_map/while/body/eval_jaxpr/ppermute | solution.py:21
  (52 other events, 808.8 us)
Sparse Core Ops, SparseCore 0:
  182.1 53.5 reduce-scatter.1
  238.2 159.7 all-reduce.1
  400.7 74.1 all-gather.1
where the time goes:
time: 751 us; the launch traced here: 750 us
  waiting for transfers between devices  649 us (86%)
  matrix products  33.5 us (4%)
  local copies, waits for them, and re-layouts  20 us (3%)
  starting transfers between devices  19.2 us (3%)
  between operations  14 us (2%)
  other arithmetic  11.9 us (2%)
    ppermute x92, waiting for transfers between devices, from_behind(): lax.ppermute(shard, axis, [(i, (i + by) % size) for i in range(size)])  433 us
    psum x1, waiting for transfers between devices, on_device(): weight_grad = lax.psum(band_sum, 'lon')  162 us
    reduce_scatter x1, waiting for transfers between devices, on_device(): lax.psum_scatter(jnp.einsum('ce,cd->ed', attended, upstream_flat, preferr...  53.7 us
    ppermute x92, starting transfers between devices, from_behind(): lax.ppermute(shard, axis, [(i, (i + by) % size) for i in range(size)])  19 us
  transfers between devices with their start and end apart: 95, of which 63 were waited for; matrix products, arithmetic and copies ran while one was open for 7% of the time, Pallas kernels for 0%

commit v1 on v0

v1 whole, which is shorter than its diff:
```python
import jax
import jax.numpy as jnp
from jax import lax
from jax.experimental import pallas as pl
from jax.experimental.pallas import tpu as pltpu
from jax.sharding import PartitionSpec as P

D = 1024
HEADS = 8
HEAD = 64
BLOCK = 64
NB = 8
ROWS = 2
HD = 512
CELLS = ROWS * BLOCK
PAIR = 2 * HEAD

learn_rate = 0.01
decay_rate = 0.9

BF = jnp.bfloat16
F32 = jnp.float32
VMEM_BYTES = 56 * 2**20


def dot(a, b, dims):
    return lax.dot_general(a, b, ((dims[:1], dims[1:]), ((), ())), preferred_element_type=F32)


def pack_kernel(q_ref, k_ref, v_ref, up_ref, w_ref, allow_ref, out_ref):
    grad = dot(up_ref[...], w_ref[...], (1, 1)).astype(BF)
    for h in range(HEADS):
        feats = slice(h * HEAD, (h + 1) * HEAD)
        kv = jnp.concatenate([k_ref[:, feats], v_ref[:, feats]], axis=1)
        qg = jnp.concatenate([q_ref[:, feats], grad[:, feats]], axis=1)
        for r in range(ROWS):
            slab = r * HEADS + h
            out_ref[slab, 0:BLOCK, :] = qg[r * BLOCK : (r + 1) * BLOCK]
            out_ref[slab, BLOCK : BLOCK + CELLS, :] = kv
            out_ref[slab, BLOCK + CELLS :, :] = allow_ref[r]


def attend_kernel(in_ref, out_ref, acc_ref, tile):
    lonb = in_ref.shape[0]
    keys = lonb * CELLS
    per = tile // BLOCK
    kv = in_ref[:, BLOCK : BLOCK + CELLS, :].reshape(keys, PAIR)
    low = lax.broadcasted_iota(jnp.int32, (1, PAIR), 1) < HEAD
    zero = jnp.zeros((), BF)
    scale = HEAD**-0.5
    k_only = jnp.where(low, kv, zero) * jnp.asarray(scale, BF)
    v_only = jnp.where(low, zero, kv)
    kv_t = kv.T
    lists = in_ref[:, BLOCK + CELLS, :].astype(F32)
    acc_ref[...] = jnp.zeros_like(acc_ref)
    for t in range(lonb // per):
        x = in_ref[t * per : (t + 1) * per, 0:BLOCK, :].reshape(tile, PAIR)
        spread = (
            lax.broadcasted_iota(jnp.int32, (lonb, tile), 0)
            == t * per + lax.broadcasted_iota(jnp.int32, (lonb, tile), 1) // BLOCK
        ).astype(F32)
        seen = dot(lists, spread, (0, 0))[: lonb * ROWS]
        bias = jnp.where(seen > 0.5, 0.0, -1e30)[:, None, :]
        scores = dot(k_only, x, (1, 1)).reshape(lonb * ROWS, BLOCK, tile) + bias
        scores = scores.reshape(keys, tile)
        top = jnp.max(scores, axis=0, keepdims=True)
        probs = jnp.exp(scores - top)
        probs = probs * (1.0 / jnp.sum(probs, axis=0, keepdims=True))
        prob_bf = probs.astype(BF)
        x_t = x.T
        att_t = dot(kv_t, prob_bf, (1, 0)).astype(BF)
        delta = jnp.sum((x_t.astype(F32) * att_t.astype(F32))[HEAD:], axis=0, keepdims=True)
        prob_grad = dot(v_only, x, (1, 1))
        score_grad = (probs * (prob_grad - delta)).astype(BF)
        grad_q_t = (dot(kv_t[:HEAD], score_grad, (1, 0)) * scale).astype(BF)
        mine = jnp.concatenate([grad_q_t, att_t[HEAD:]], axis=0).T
        out_ref[t * per : (t + 1) * per, 0:BLOCK, :] = mine.reshape(per, BLOCK, PAIR)
        acc_ref[...] += jnp.where(low, dot(score_grad, x, (1, 0)) * scale, dot(prob_bf, x, (1, 0)))
    out_ref[:, BLOCK : BLOCK + CELLS, :] = acc_ref[...].astype(BF).reshape(lonb, CELLS, PAIR)


def unpack_kernel(in_ref, up_ref, gq_ref, gk_ref, gv_ref, weight_ref):
    att = []
    for h in range(HEADS):
        feats = slice(h * HEAD, (h + 1) * HEAD)
        mine = jnp.concatenate([in_ref[r * HEADS + h, 0:BLOCK, :] for r in range(ROWS)], axis=0)
        gq_ref[:, feats] = mine[:, :HEAD]
        att.append(mine[:, HEAD:])
        kv = sum(in_ref[r * HEADS + h, BLOCK : BLOCK + CELLS, :].astype(F32) for r in range(ROWS)).astype(BF)
        gk_ref[:, feats] = kv[:, :HEAD]
        gv_ref[:, feats] = kv[:, HEAD:]
    att = jnp.concatenate(att, axis=1)
    weight_ref[...] = dot(att, up_ref[...], (0, 0)).astype(weight_ref.dtype)


def call(kernel, outs, *args, scratch=()):
    return pl.pallas_call(
        kernel,
        out_shape=outs,
        scratch_shapes=scratch,
        compiler_params=pltpu.CompilerParams(vmem_limit_bytes=VMEM_BYTES),
    )(*args)


def summed(parts, rows):
    return jnp.sum(parts.reshape(-1, rows, D).astype(F32), axis=0)


def spread(shard, axis):
    copies = jnp.broadcast_to(shard[None], (lax.axis_size(axis), *shard.shape))
    return lax.all_to_all(copies, axis, 0, 0, tiled=True).reshape(-1, D)


def on_device(queries, keys, values, upstream, out_weight, average, nbr_lon, nbr_lat, counts):
    lonb = lax.axis_size("lon")
    up = upstream.reshape(CELLS, D)
    live = jnp.arange(NB)[None, :] < counts
    block = nbr_lon.reshape(ROWS, NB) * ROWS + nbr_lat.reshape(ROWS, NB)
    allow = jnp.any(live[:, :, None] & (block[:, :, None] == jnp.arange(PAIR)[None, None, :]), axis=1)
    allow = jnp.broadcast_to(allow.astype(BF)[:, None, :], (ROWS, 16, PAIR))
    slabs = call(
        pack_kernel,
        jax.ShapeDtypeStruct((lonb, BLOCK + CELLS + 16, PAIR), BF),
        queries.reshape(CELLS, HD),
        keys.reshape(CELLS, HD),
        values.reshape(CELLS, HD),
        up,
        out_weight,
        allow,
    )
    slabs = lax.all_to_all(slabs, "lon", 0, 0, tiled=True)
    done = call(
        lambda i, o, a: attend_kernel(i, o, a, 256),
        jax.ShapeDtypeStruct((lonb, BLOCK + CELLS, PAIR), BF),
        slabs,
        scratch=[pltpu.VMEM((lonb * CELLS, PAIR), F32)],
    )
    done = lax.all_to_all(done, "lon", 0, 0, tiled=True)
    cell_grads = jax.ShapeDtypeStruct((CELLS, HD), BF)
    gq, gk, gv, weight_part = call(
        unpack_kernel,
        (cell_grads, cell_grads, cell_grads, jax.ShapeDtypeStruct((HD, D), BF)),
        done,
        up,
    )
    rows = HD // lax.axis_size("lat")
    share = rows // lonb
    band_sum = summed(lax.all_to_all(weight_part, "lat", 0, 0, tiled=True), rows).astype(BF)
    grid_sum = summed(lax.all_to_all(band_sum, "lon", 0, 0, tiled=True), share).astype(BF)
    weight_grad = spread(grid_sum, "lon").astype(F32)
    own_weight = lax.dynamic_slice_in_dim(out_weight, lax.axis_index("lat") * rows, rows, 0).astype(F32)
    updated = own_weight - learn_rate * weight_grad
    averaged = decay_rate * average + (1.0 - decay_rate) * updated
    next_weights = spread(averaged.astype(BF), "lat")
    own = (ROWS, BLOCK, HD)
    return (gq.reshape(own), gk.reshape(own), gv.reshape(own), updated, next_weights)


def solution(mesh):
    cells = P("lat", "lon", None)
    return jax.shard_map(
        on_device,
        mesh=mesh,
        in_specs=(cells, cells, cells, cells, P(), P("lat", None), cells, cells, P("lat", "lon")),
        out_specs=(cells, cells, cells, P("lat", None), P()),
        check_vma=False,
    )
```

time: 751 us -> 158 us (0.21)
  the two profiles are of different devices: /device:TPU:2 before, /device:TPU:1 now
where the time goes in v1:
time: 158 us; the launch traced here: 157 us
  blocking collectives  119 us (75%)
  Pallas kernels  18.4 us (12%)
  waiting for transfers between devices  8.83 us (6%)
  local copies, waits for them, and re-layouts  4.52 us (3%)
  starting transfers between devices  3.5 us (2%)
  other arithmetic  2.03 us (1%)
    all_to_all x1, blocking collectives, on_device(): slabs = lax.all_to_all(slabs, 'lon', 0, 0, tiled=True)  34.5 us
    all_to_all x1, blocking collectives, on_device(): done = lax.all_to_all(done, 'lon', 0, 0, tiled=True)  26.9 us
    all_to_all x1, blocking collectives, on_device(): lax.all_to_all(weight_part, 'lat', 0, 0, tiled=True)  22.4 us
    all_to_all x1, blocking collectives, spread(): return lax.all_to_all(copies, axis, 0, 0, tiled=True).reshape(-1, D)  21.7 us
    pallas_call x3, Pallas kernels, call(): pl.pallas_call(kernel, out_shape=outs, scratch_shapes=scratch, compiler_p...  18.4 us
    all_to_all x1, blocking collectives, on_device(): lax.all_to_all(band_sum, 'lon', 0, 0, tiled=True)  13.6 us
    all_to_all x1, waiting for transfers between devices, spread(): return lax.all_to_all(copies, axis, 0, 0, tiled=True).reshape(-1, D)  8.83 us
    all_to_all x1, starting transfers between devices, spread(): return lax.all_to_all(copies, axis, 0, 0, tiled=True).reshape(-1, D)  3.5 us
  transfers between devices with their start and end apart: 1, of which 1 were waited for; matrix products, arithmetic and copies ran while one was open for 0% of the time, Pallas kernels for 0%

profile of v1, /device:TPU:1, one launch (start us, length us, event | category | flops | bytes accessed | tf_op | source)
XLA Modules:
  0.0 157.1 jit_solution(6483227486410532574)
XLA Ops:
  0.6 0.0 copy-start.3
  0.6 0.0 copy-start.2
  0.7 0.6 copy-done.3
  1.3 0.0 copy-start.1
  1.3 0.1 iota_compare_fusion.1
  1.4 0.0 copy-done.2
  1.4 0.6 copy-done.1
  2.0 0.1 fusion.1
  2.1 0.6 broadcast_in_dim.6.allow_ref
  2.7 3.0 %shard_map.131 = bf16[16,208,128]{2,1,0:T(8,128)(2,1)} custom-call(bf16[128,512]{1,0:T(8,128)(2,1)} %bitcast.15, bf16[128,512]{1,0:T(8,128)(2,1)} %bitcast.16, bf16[128,512]{1,0:T(8,128)(2,1)} %bitcast.17, bf16[128,1024]{1,0:T(8,128)(2,1)} %bitcast.13, bf16[512,1024]{1,0:T(8,128)(2,1)} %w_ref.1, bf16[2,16,128]{2,1,0:T(8,128)(2,1)} %broadcast_in_dim.6.allow_ref), custom_call_target="tpu_custom_call" | custom-call | tf_op jit(solution)/shard_map/pallas_call | solution.py:97
  5.6 34.5 %all_to_all.38.i = bf16[16,208,128]{2,1,0:T(8,128)(2,1)} all-to-all(bf16[16,208,128]{2,1,0:T(8,128)(2,1)} %shard_map.131), channel_id=1, replica_groups=mesh['lon'=16,'lat'=16] {'lon'}, dimensions={0} | all-to-all | bytes 1703936 | tf_op jit(solution)/shard_map/all_to_all | solution.py:131
  40.1 12.7 %shard_map.132 = bf16[16,192,128]{2,1,0:T(8,128)(2,1)} custom-call(bf16[16,208,128]{2,1,0:T(8,128)(2,1)} %all_to_all.38.i), custom_call_target="tpu_custom_call" | custom-call | tf_op jit(solution)/shard_map/pallas_call | solution.py:97
  52.8 26.9 %all_to_all.39.in_ref = bf16[16,192,128]{2,1,0:T(8,128)(2,1)} all-to-all(bf16[16,192,128]{2,1,0:T(8,128)(2,1)} %shard_map.132), channel_id=1, replica_groups=mesh['lon'=16,'lat'=16] {'lon'}, dimensions={0} | all-to-all | bytes 1572864 | tf_op jit(solution)/shard_map/all_to_all | solution.py:138
  79.7 2.8 %shard_map.133 = (bf16[128,512]{1,0:T(8,128)(2,1)}, bf16[128,512]{1,0:T(8,128)(2,1)}, bf16[128,512]{1,0:T(8,128)(2,1)}, bf16[512,1024]{1,0:T(8,128)(2,1)}) custom-call(bf16[16,192,128]{2,1,0:T(8,128)(2,1)} %all_to_all.39.in_ref, bf16[128,1024]{1,0:T(8,128)(2,1)} %bitcast.14), custom_call_target="tpu_custom_call" | custom-call | tf_op jit(solution)/shard_map/pallas_call | solution.py:97
  82.4 22.4 %all_to_all.40 = bf16[16,32,1024]{2,1,0:T(8,128)(2,1)S(1)} all-to-all(bf16[16,32,1024]{2,1,0:T(8,128)(2,1)} %bitcast.12), channel_id=1, replica_groups=mesh['lon'=16,'lat'=16] {'lat'}, dimensions={0} | all-to-all | bytes 2097152 | tf_op jit(solution)/shard_map/all_to_all | solution.py:148
  104.9 0.2 reduce_sum.24
  105.1 13.6 %all_to_all.41 = bf16[16,2,1024]{2,1,0:T(2,128)(2,1)S(1)} all-to-all(bf16[16,2,1024]{2,1,0:T(2,128)(2,1)S(1)} %all_to_all.28), channel_id=1, replica_groups=mesh['lon'=16,'lat'=16] {'lon'}, dimensions={0} | all-to-all | bytes 131072 | tf_op jit(solution)/shard_map/all_to_all | solution.py:149
  118.8 0.1 reduce_sum.25
  118.8 0.7 broadcast_in_dim.7
  119.5 3.5 %all-to-all-start.4 = ((bf16[16,2,1024]{2,1,0:T(2,128)(2,1)}), bf16[16,2,1024]{2,1,0:T(2,128)(2,1)S(1)}, u32[]{:S(2)}, u32[]{:S(2)}) async-start(bf16[16,2,1024]{2,1,0:T(2,128)(2,1)} %broadcast_in_dim.7), calls=%async_computation.4 | async-start | bytes 131072 | tf_op jit(solution)/shard_map/all_to_all | solution.py:111
  123.0 8.8 %all-to-all-done.4 = bf16[16,2,1024]{2,1,0:T(2,128)(2,1)S(1)} async-done(((bf16[16,2,1024]{2,1,0:T(2,128)(2,1)}), bf16[16,2,1024]{2,1,0:T(2,128)(2,1)S(1)}, u32[]{:S(2)}, u32[]{:S(2)}) %all-to-all-start.4) | async-done | bytes 65568 | tf_op jit(solution)/shard_map/all_to_all | solution.py:111
  131.9 0.1 convert_multiply_fusion
  131.9 0.0 copy-start
  131.9 0.1 mul.36
  132.0 0.8 copy-done
  132.8 1.5 add_convert_fusion
  134.4 0.1 broadcast_in_dim.8
  134.5 21.7 %all_to_all.42 = bf16[16,32,1024]{2,1,0:T(8,128)(2,1)S(1)} all-to-all(bf16[16,32,1024]{2,1,0:T(8,128)(2,1)S(1)} %broadcast_in_dim.8), channel_id=1, replica_groups=mesh['lon'=16,'lat'=16] {'lat'}, dimensions={0} | all-to-all | bytes 2097152 | tf_op jit(solution)/shard_map/all_to_all | solution.py:111
  156.1 1.0 copy.17
  (3 shorter events, 0.0 us)
Async XLA Ops:
  0.6 0.7 copy-start.3
  0.6 0.7 copy-start.2
  1.3 0.7 copy-start.1
  119.5 12.3 %all-to-all-start.4 = ((bf16[16,2,1024]{2,1,0:T(2,128)(2,1)}), bf16[16,2,1024]{2,1,0:T(2,128)(2,1)S(1)}, u32[]{:S(2)}, u32[]{:S(2)}) async-start(bf16[16,2,1024]{2,1,0:T(2,128)(2,1)} %broadcast_in_dim.7), calls=%async_computation.4 | async-start | bytes 131072 | tf_op jit(solution)/shard_map/all_to_all | solution.py:111
  131.9 0.9 copy-start

commit v2 on v1

v2 whole, which is shorter than its diff:
```python
import jax
import jax.numpy as jnp
from jax import lax
from jax.experimental import pallas as pl
from jax.experimental.pallas import tpu as pltpu
from jax.sharding import PartitionSpec as P

D = 1024
HEADS = 8
HEAD = 64
BLOCK = 64
NB = 8
ROWS = 2
HD = 512
CELLS = ROWS * BLOCK
PAIR = 2 * HEAD
HALF = BLOCK // 2
LISTS = 16
TILE = 256

learn_rate = 0.01
decay_rate = 0.9

BF = jnp.bfloat16
F32 = jnp.float32
VMEM_BYTES = 56 * 2**20
SCALE = HEAD**-0.5


def dot(a, b, dims):
    return lax.dot_general(a, b, ((dims[:1], dims[1:]), ((), ())), preferred_element_type=F32)


def low_lanes():
    return lax.broadcasted_iota(jnp.int32, (1, PAIR), 1) < HEAD


def swap(x):
    return jnp.concatenate([x[:, HEAD:], x[:, :HEAD]], axis=1)


def fold(x):
    top, bottom = x[:HALF], x[HALF:]
    low = low_lanes()
    return jnp.where(low, top, swap(bottom)), jnp.where(low, swap(top), bottom)


def unfold(first, second):
    low = low_lanes()
    return jnp.concatenate([jnp.where(low, first, swap(second)), jnp.where(low, swap(first), second)], axis=0)


def pack_kernel(lon_ref, lat_ref, count_ref, q_ref, k_ref, v_ref, up_ref, w_ref, out_ref):
    grad = dot(up_ref[...], w_ref[...], (1, 1)).astype(BF)
    for h in range(HEADS):
        feats = slice(h * HEAD, (h + 1) * HEAD)
        kv = jnp.concatenate([k_ref[:, feats], v_ref[:, feats]], axis=1)
        qg = jnp.concatenate([q_ref[:, feats], grad[:, feats]], axis=1)
        for r in range(ROWS):
            slab = r * HEADS + h
            out_ref[slab, 0:BLOCK, :] = qg[r * BLOCK : (r + 1) * BLOCK]
            out_ref[slab, BLOCK : BLOCK + CELLS, :] = kv
    block = lax.broadcasted_iota(jnp.int32, (LISTS, PAIR), 1)
    for r in range(ROWS):
        seen = jnp.zeros((LISTS, PAIR), F32)
        for t in range(NB):
            named = jnp.where(t < count_ref[r, 0], lon_ref[r, 0, t] * ROWS + lat_ref[r, 0, t], -1)
            seen = jnp.where(block == named, 1.0, seen)
        for h in range(HEADS):
            out_ref[r * HEADS + h, BLOCK + CELLS :, :] = seen.astype(BF)


def forward_kernel(in_ref, att_ref, prob_ref, delta_ref):
    lonb = in_ref.shape[0]
    keys = lonb * CELLS
    per = TILE // BLOCK
    kv = in_ref[:, BLOCK : BLOCK + CELLS, :].reshape(keys, PAIR)
    k_only = jnp.where(low_lanes(), kv * jnp.asarray(SCALE, BF), jnp.zeros((), BF))
    v_t = kv.T[HEAD:]
    lists = in_ref[:, BLOCK + CELLS, :].astype(F32)
    for t in range(lonb // per):
        x = in_ref[t * per : (t + 1) * per, 0:BLOCK, :].reshape(TILE, PAIR)
        spread = (
            lax.broadcasted_iota(jnp.int32, (lonb, TILE), 0)
            == t * per + lax.broadcasted_iota(jnp.int32, (lonb, TILE), 1) // BLOCK
        ).astype(F32)
        seen = dot(lists, spread, (0, 0))[: lonb * ROWS]
        bias = jnp.where(seen > 0.5, 0.0, -1e30)[:, None, :]
        scores = dot(k_only, x, (1, 1)).reshape(lonb * ROWS, BLOCK, TILE) + bias
        scores = scores.reshape(keys, TILE)
        top = jnp.max(scores, axis=0, keepdims=True)
        probs = jnp.exp(scores - top)
        probs = (probs * (1.0 / jnp.sum(probs, axis=0, keepdims=True))).astype(BF)
        prob_ref[t] = probs
        att_t = dot(v_t, probs, (1, 0)).astype(BF)
        grad_t = x.T[HEAD:].astype(F32)
        delta_ref[t] = jnp.broadcast_to(jnp.sum(grad_t * att_t.astype(F32), axis=0, keepdims=True), (8, TILE))
        for i in range(0, per, 2):
            att_ref[t * per + i], att_ref[t * per + i + 1] = fold(att_t[:, i * BLOCK : (i + 2) * BLOCK])


def backward_kernel(in_ref, prob_ref, delta_ref, out_ref, acc_ref):
    lonb = in_ref.shape[0]
    keys = lonb * CELLS
    per = TILE // BLOCK
    kv = in_ref[:, BLOCK : BLOCK + CELLS, :].reshape(keys, PAIR)
    low = low_lanes()
    v_only = jnp.where(low, jnp.zeros((), BF), kv)
    k_t = kv.T[:HEAD]
    for t in range(lonb // per):
        x = in_ref[t * per : (t + 1) * per, 0:BLOCK, :].reshape(TILE, PAIR)
        probs = prob_ref[t]
        prob_grad = dot(v_only, x, (1, 1))
        score_grad = (probs.astype(F32) * (prob_grad - delta_ref[t, 0:1, :])).astype(BF)
        grad_q = (dot(k_t, score_grad, (1, 0)) * SCALE).astype(BF)
        for i in range(0, per, 2):
            pieces = fold(grad_q[:, i * BLOCK : (i + 2) * BLOCK])
            out_ref[t * per + i, 0:HALF, :] = pieces[0]
            out_ref[t * per + i + 1, 0:HALF, :] = pieces[1]
        part = jnp.where(low, dot(score_grad, x, (1, 0)) * SCALE, dot(probs, x, (1, 0)))
        if t == 0:
            acc_ref[...] = part
        else:
            acc_ref[...] += part
    out_ref[:, HALF:, :] = acc_ref[...].astype(BF).reshape(lonb, CELLS, PAIR)


def weight_kernel(place_ref, att_ref, up_ref, keep_ref, send_ref, att_t):
    for h in range(HEADS):
        piece = unfold(att_ref[h], att_ref[HEADS + h])
        att_t[2 * h] = piece[:HALF]
        att_t[2 * h + 1] = piece[HALF:]
    place = place_ref[0]
    for ref, core in ((send_ref, 1), (keep_ref, 0)):
        rows = [att_t[place ^ (4 * dx + 2 * dy + core)] for dy in range(2) for dx in range(HEADS // 2)]
        part = dot(jnp.concatenate(rows, axis=0), up_ref[...], (1, 0))
        ref[...] = part.astype(BF).reshape(ref.shape)


def unpack_kernel(in_ref, gq_ref, gk_ref, gv_ref):
    gq_t = []
    for h in range(HEADS):
        feats = slice(h * HEAD, (h + 1) * HEAD)
        gq_t.append(unfold(in_ref[h, 0:HALF, :], in_ref[HEADS + h, 0:HALF, :]))
        kv = sum(in_ref[r * HEADS + h, HALF:, :].astype(F32) for r in range(ROWS)).astype(BF)
        gk_ref[:, feats] = kv[:, :HEAD]
        gv_ref[:, feats] = kv[:, HEAD:]
    gq_ref[...] = jnp.concatenate(gq_t, axis=0).T


def call(kernel, outs, *args, scratch=(), scalars=0):
    on_chip = [pl.BlockSpec(memory_space=pltpu.SMEM if i < scalars else pltpu.VMEM) for i in range(len(args))]
    return pl.pallas_call(
        kernel,
        out_shape=outs,
        in_specs=on_chip,
        scratch_shapes=scratch,
        compiler_params=pltpu.CompilerParams(vmem_limit_bytes=VMEM_BYTES),
    )(*args)


def shape(*dims, dtype=BF):
    return jax.ShapeDtypeStruct(dims, dtype)


def pairwise(x, axis, bit):
    return lax.ppermute(x, axis, [(i, i ^ bit) for i in range(lax.axis_size(axis))])


def plus(*parts):
    total = parts[0].astype(F32)
    for part in parts[1:]:
        total = total + part.astype(F32)
    return total


def quad_sum(x, a, b):
    x = x.astype(BF)
    return plus(x, pairwise(x, "lon", a)) + plus(pairwise(x, "lon", b), pairwise(x, "lon", a ^ b))


def on_device(queries, keys, values, upstream, out_weight, average, nbr_lon, nbr_lat, counts):
    lonb = lax.axis_size("lon")
    lats = lax.axis_size("lat")
    same_core = [[c + 2 * i for i in range(lats // 2)] for c in range(2)]
    up = upstream.reshape(CELLS, D)
    slabs = call(
        pack_kernel,
        shape(lonb, BLOCK + CELLS + LISTS, PAIR),
        nbr_lon,
        nbr_lat,
        counts,
        queries.reshape(CELLS, HD),
        keys.reshape(CELLS, HD),
        values.reshape(CELLS, HD),
        up,
        out_weight,
        scalars=3,
    )
    slabs = lax.all_to_all(slabs, "lon", 0, 0, tiled=True)
    tiles = lonb * BLOCK // TILE
    att, probs, delta = call(
        forward_kernel,
        (
            shape(lonb, HALF, PAIR),
            shape(tiles, lonb * CELLS, TILE),
            shape(tiles, 8, TILE, dtype=F32),
        ),
        slabs,
    )
    att = lax.all_to_all(att, "lon", 0, 0, tiled=True)
    grads = call(
        backward_kernel,
        shape(lonb, HALF + CELLS, PAIR),
        slabs,
        probs,
        delta,
        scratch=[pltpu.VMEM((lonb * CELLS, PAIR), F32)],
    )
    att, grads = lax.optimization_barrier((att, grads))
    rows = HD // lats
    half = shape(2, lats // 4, rows, D)
    place = lax.axis_index("lat")
    keep, send = call(
        weight_kernel,
        (half, half),
        place.reshape(1),
        att,
        up,
        scratch=[pltpu.VMEM((2 * HEADS, HALF, CELLS), BF)],
        scalars=1,
    )
    grads = lax.all_to_all(grads, "lon", 0, 0, tiled=True)
    came = pairwise(send, "lat", 1)
    by_y = pairwise(plus(keep[1], came[1]).astype(BF), "lat", 2)
    by_x = [plus(keep[0, i], came[0, i], by_y[i]) for i in range(lats // 4)]
    by_x = by_x[:1] + [pairwise(by_x[i].astype(BF), "lat", 4 * i) for i in range(1, lats // 4)]
    total = quad_sum(plus(*by_x), 1, 8)
    total = quad_sum(total, 2, 4)
    own_weight = lax.dynamic_slice_in_dim(out_weight, place * rows, rows, 0).astype(F32)
    updated = own_weight - learn_rate * total
    averaged = decay_rate * average + (1.0 - decay_rate) * updated
    averaged, grads = lax.optimization_barrier((averaged, grads))
    copies = jnp.broadcast_to(averaged.astype(BF)[None], (lats // 2, rows, D))
    mine = lax.all_to_all(copies, "lat", 0, 0, axis_index_groups=same_core, tiled=True)
    other = pairwise(mine, "lat", 1)
    first = place % 2 == 0
    next_weights = jnp.stack([jnp.where(first, mine, other), jnp.where(first, other, mine)], axis=1).reshape(HD, D)
    cell_grads = shape(CELLS, HD)
    gq, gk, gv = call(unpack_kernel, (cell_grads, cell_grads, cell_grads), grads)
    own = (ROWS, BLOCK, HD)
    return (gq.reshape(own), gk.reshape(own), gv.reshape(own), updated, next_weights)


def solution(mesh):
    cells = P("lat", "lon", None)
    return jax.shard_map(
        on_device,
        mesh=mesh,
        in_specs=(cells, cells, cells, cells, P(), P("lat", None), cells, cells, P("lat", "lon")),
        out_specs=(cells, cells, cells, P("lat", None), P()),
        check_vma=False,
    )
```

time: 158 us -> 135 us (0.85)
  blocking collectives: 119 us -> 46.1 us
  starting transfers between devices: 3.5 us -> 35 us
  waiting for transfers between devices: 8.83 us -> 19.2 us
  Pallas kernels: 18.4 us -> 25.2 us
  other arithmetic: 2.03 us -> 5.62 us
  local copies, waits for them, and re-layouts: 4.52 us -> 2.01 us
    all_to_all x4 -> x1, blocking collectives: 84.6 us -> 11.6 us  [on_device(): lax.all_to_all(copies, 'lat', 0, 0, axis_index_groups=same_core, tiled=True)]
    ppermute x0 -> x12, starting transfers between devices: none -> 20.8 us  [pairwise(): lax.ppermute(x, axis, [(i, i ^ bit) for i in range(lax.axis_size(axis))])]
    ppermute x0 -> x12, waiting for transfers between devices: none -> 18.8 us  [pairwise(): lax.ppermute(x, axis, [(i, i ^ bit) for i in range(lax.axis_size(axis))])]
    all_to_all x1 -> x2, starting transfers between devices: 3.5 us -> 14.3 us  [the longest x1 8.41 us: on_device(): grads = lax.all_to_all(grads, 'lon', 0, 0, tiled=True)]
    all_to_all x1 -> x2, waiting for transfers between devices: 8.83 us -> 0.47 us  [the longest x1 0.47 us: on_device(): att = lax.all_to_all(att, 'lon', 0, 0, tiled=True)]
    pallas_call x3 -> x5, Pallas kernels: 18.4 us -> 25.2 us  [call(): pl.pallas_call(kernel, out_shape=outs, in_specs=on_chip, scratch_shapes=s...]
  transfers between devices with their start and end apart: 1 -> 14, of which waited for: 1 -> 9; matrix products, arithmetic and copies ran while one was open for 0% -> 3% of each run, Pallas kernels for 0% -> 8%
where the time goes in v2:
time: 135 us; the launch traced here: 134 us
  blocking collectives  46.1 us (34%)
  starting transfers between devices  35 us (26%)
  Pallas kernels  25.2 us (19%)
  waiting for transfers between devices  19.2 us (14%)
  other arithmetic  5.62 us (4%)
  local copies, waits for them, and re-layouts  2.01 us (1%)
    all_to_all x1, blocking collectives, on_device(): slabs = lax.all_to_all(slabs, 'lon', 0, 0, tiled=True)  34.5 us
    pallas_call x5, Pallas kernels, call(): pl.pallas_call(kernel, out_shape=outs, in_specs=on_chip, scratch_shapes=s...  25.2 us
    ppermute x12, starting transfers between devices, pairwise(): lax.ppermute(x, axis, [(i, i ^ bit) for i in range(lax.axis_size(axis))])  20.8 us
    ppermute x12, waiting for transfers between devices, pairwise(): lax.ppermute(x, axis, [(i, i ^ bit) for i in range(lax.axis_size(axis))])  18.8 us
    all_to_all x1, blocking collectives, on_device(): lax.all_to_all(copies, 'lat', 0, 0, axis_index_groups=same_core, tiled=True)  11.6 us
    all_to_all x1, starting transfers between devices, on_device(): grads = lax.all_to_all(grads, 'lon', 0, 0, tiled=True)  8.41 us
    all_to_all x1, starting transfers between devices, on_device(): att = lax.all_to_all(att, 'lon', 0, 0, tiled=True)  5.84 us
  transfers between devices with their start and end apart: 14, of which 9 were waited for; matrix products, arithmetic and copies ran while one was open for 3% of the time, Pallas kernels for 8%

profile of v2, /device:TPU:1, one launch (start us, length us, event | category | flops | bytes accessed | tf_op | source)
XLA Modules:
  0.0 133.9 jit_solution(12463599390415021083)
XLA Ops:
  0.6 1.3 copy.14.count_ref
  1.9 3.0 %shard_map.128 = bf16[16,208,128]{2,1,0:T(8,128)(2,1)} custom-call(s32[2,1,8]{2,1,0:T(1,128)} %lon_ref.1, s32[2,1,8]{2,1,0:T(1,128)} %lat_ref.1, s32[2,1]{1,0:T(2,128)} %copy.14.count_ref, bf16[128,512]{1,0:T(8,128)(2,1)} %bitcast.48, bf16[128,512]{1,0:T(8,128)(2,1)} %bitcast.49, bf16[128,512]{1,0:T(8,128)(2,1)} %bitcast.50, bf16[128,1024]{1,0:T(8,128)(2,1)} %bitcast.46, ...), custom_call_target="tpu_custom_call" | custom-call | tf_op jit(solution)/shard_map/pallas_call | solution.py:153
  4.9 34.5 %all_to_all.20.in_ref = bf16[16,208,128]{2,1,0:T(8,128)(2,1)} all-to-all(bf16[16,208,128]{2,1,0:T(8,128)(2,1)} %shard_map.128), channel_id=1, replica_groups=mesh['lon'=16,'lat'=16] {'lon'}, dimensions={0} | all-to-all | bytes 1703936 | tf_op jit(solution)/shard_map/all_to_all | solution.py:200
  39.3 9.3 %shard_map.129 = (bf16[16,32,128]{2,1,0:T(8,128)(2,1)}, bf16[4,2048,256]{2,1,0:T(8,128)(2,1)}, f32[4,8,256]{2,1,0:T(8,128)}) custom-call(bf16[16,208,128]{2,1,0:T(8,128)(2,1)} %all_to_all.20.in_ref), custom_call_target="tpu_custom_call" | custom-call | tf_op jit(solution)/shard_map/pallas_call | solution.py:153
  48.7 5.8 %all-to-all-start.1 = ((bf16[16,32,128]{2,1,0:T(8,128)(2,1)}), bf16[16,32,128]{2,1,0:T(8,128)(2,1)S(1)}, u32[]{:S(2)}, u32[]{:S(2)}) async-start(bf16[16,32,128]{2,1,0:T(8,128)(2,1)} %get-tuple-element.17), calls=%async_computation.1 | async-start | bytes 262144 | tf_op jit(solution)/shard_map/all_to_all | solution.py:211
  54.5 0.0 copy-start.2
  54.5 8.5 %shard_map.130 = bf16[16,160,128]{2,1,0:T(8,128)(2,1)} custom-call(bf16[16,208,128]{2,1,0:T(8,128)(2,1)} %all_to_all.20.in_ref, bf16[4,2048,256]{2,1,0:T(8,128)(2,1)} %get-tuple-element.18.prob_ref, f32[4,8,256]{2,1,0:T(8,128)} %get-tuple-element.19.delta_ref), custom_call_target="tpu_custom_call" | custom-call | tf_op jit(solution)/shard_map/pallas_call | solution.py:153
  63.0 0.5 all-to-all-done.1.att_ref
  63.5 0.0 copy-start.1
  63.5 0.7 copy-done.1
  64.2 2.4 %shard_map.131 = (bf16[2,4,32,1024]{3,2,1,0:T(8,128)(2,1)}, bf16[2,4,32,1024]{3,2,1,0:T(8,128)(2,1)}) custom-call(s32[1]{0:T(128)} %bitcast.place_ref, bf16[16,32,128]{2,1,0:T(8,128)(2,1)} %copy-done.1, bf16[128,1024]{1,0:T(8,128)(2,1)} %bitcast.47), custom_call_target="tpu_custom_call" | custom-call | tf_op jit(solution)/shard_map/pallas_call | solution.py:153
  66.6 2.3 %collective-permute-start = (bf16[2,4,32,1024]{3,2,1,0:T(8,128)(2,1)}, bf16[2,4,32,1024]{3,2,1,0:T(8,128)(2,1)S(1)}, u32[]{:S(2)}, u32[]{:S(2)}) collective-permute-start(bf16[2,4,32,1024]{3,2,1,0:T(8,128)(2,1)} %get-tuple-element.22), channel_id=1, source_target_pairs={{0,1},{1,0},{2,3},{3,2},{4,5},{5,4},{6,7},{7,6},{8,9},{9,8},{10,11... | collective-permute-start | bytes 1572872 | tf_op jit(solution)/shard_map/ppermute | solution.py:167
  68.9 1.7 %collective-permute-done = bf16[2,4,32,1024]{3,2,1,0:T(8,128)(2,1)S(1)} collective-permute-done((bf16[2,4,32,1024]{3,2,1,0:T(8,128)(2,1)}, bf16[2,4,32,1024]{3,2,1,0:T(8,128)(2,1)S(1)}, u32[]{:S(2)}, u32[]{:S(2)}) %collective-permute-start) | collective-permute-done | bytes 524320 | tf_op jit(solution)/shard_map/ppermute | solution.py:167
  70.7 1.0 fusion
  71.7 0.5 collective-permute-start.1
  72.2 8.4 %all-to-all-start.2 = ((bf16[16,160,128]{2,1,0:T(8,128)(2,1)}), bf16[16,160,128]{2,1,0:T(8,128)(2,1)S(1)}, u32[]{:S(2)}, u32[]{:S(2)}) async-start(bf16[16,160,128]{2,1,0:T(8,128)(2,1)} %shard_map.130), calls=%async_computation.2 | async-start | bytes 1310720 | tf_op jit(solution)/shard_map/all_to_all | solution.py:233
  80.6 0.0 collective-permute-done.1
  80.6 1.0 fusion.3
  81.6 1.3 collective-permute-start.2
  82.9 2.5 %collective-permute-start.3 = (bf16[32,1024]{1,0:T(8,128)(2,1)S(1)}, bf16[32,1024]{1,0:T(8,128)(2,1)S(1)}, u32[]{:S(2)}, u32[]{:S(2)}) collective-permute-start(bf16[32,1024]{1,0:T(8,128)(2,1)S(1)} %get-tuple-element.33), channel_id=1, source_target_pairs={{0,8},{1,9},{2,10},{3,11},{4,12},{5,13},{6,14},{7,15},{8,0},{9,1},... | collective-permute-start | bytes 196616 | tf_op jit(solution)/shard_map/ppermute | solution.py:167
  85.3 0.2 collective-permute-start.4
  85.5 0.0 collective-permute-done.2
  85.5 2.2 %collective-permute-done.3 = bf16[32,1024]{1,0:T(8,128)(2,1)S(1)} collective-permute-done((bf16[32,1024]{1,0:T(8,128)(2,1)S(1)}, bf16[32,1024]{1,0:T(8,128)(2,1)S(1)}, u32[]{:S(2)}, u32[]{:S(2)}) %collective-permute-start.3) | collective-permute-done | bytes 65568 | tf_op jit(solution)/shard_map/ppermute | solution.py:167
  87.7 2.5 %collective-permute-done.4 = bf16[32,1024]{1,0:T(8,128)(2,1)S(1)} collective-permute-done((bf16[32,1024]{1,0:T(8,128)(2,1)S(1)}, bf16[32,1024]{1,0:T(8,128)(2,1)S(1)}, u32[]{:S(2)}, u32[]{:S(2)}) %collective-permute-start.4) | collective-permute-done | bytes 65568 | tf_op jit(solution)/shard_map/ppermute | solution.py:167
  90.2 0.9 fusion.7
  91.1 1.7 %collective-permute-start.5 = (bf16[32,1024]{1,0:T(8,128)(2,1)S(1)}, bf16[32,1024]{1,0:T(8,128)(2,1)S(1)}, u32[]{:S(2)}, u32[]{:S(2)}) collective-permute-start(bf16[32,1024]{1,0:T(8,128)(2,1)S(1)} %fusion.7), channel_id=1, source_target_pairs={{0,16},{16,0},{32,48},{48,32},{64,80},{80,64},{96,112},{112,96},{1... | collective-permute-start | bytes 196616 | tf_op jit(solution)/shard_map/ppermute | solution.py:167
  92.8 2.7 %collective-permute-start.6 = (bf16[32,1024]{1,0:T(8,128)(2,1)S(1)}, bf16[32,1024]{1,0:T(8,128)(2,1)S(1)}, u32[]{:S(2)}, u32[]{:S(2)}) collective-permute-start(bf16[32,1024]{1,0:T(8,128)(2,1)S(1)} %fusion.7), channel_id=1, source_target_pairs={{0,128},{16,144},{32,160},{48,176},{64,192},{80,208},{96,224},{112... | collective-permute-start | bytes 196616 | tf_op jit(solution)/shard_map/ppermute | solution.py:167
  95.5 0.1 collective-permute-start.7
  95.6 2.1 %collective-permute-done.5 = bf16[32,1024]{1,0:T(8,128)(2,1)S(1)} collective-permute-done((bf16[32,1024]{1,0:T(8,128)(2,1)S(1)}, bf16[32,1024]{1,0:T(8,128)(2,1)S(1)}, u32[]{:S(2)}, u32[]{:S(2)}) %collective-permute-start.5) | collective-permute-done | bytes 65568 | tf_op jit(solution)/shard_map/ppermute | solution.py:167
  97.7 1.0 collective-permute-done.6
  98.7 3.3 %collective-permute-done.7 = bf16[32,1024]{1,0:T(8,128)(2,1)S(1)} collective-permute-done((bf16[32,1024]{1,0:T(8,128)(2,1)S(1)}, bf16[32,1024]{1,0:T(8,128)(2,1)S(1)}, u32[]{:S(2)}, u32[]{:S(2)}) %collective-permute-start.7) | collective-permute-done | bytes 65568 | tf_op jit(solution)/shard_map/ppermute | solution.py:167
  102.0 2.3 %collective-permute-start.10 = (bf16[32,1024]{1,0:T(8,128)(2,1)S(1)}, bf16[32,1024]{1,0:T(8,128)(2,1)S(1)}, u32[]{:S(2)}, u32[]{:S(2)}) collective-permute-start(bf16[32,1024]{1,0:T(8,128)(2,1)S(1)} %add_convert_fusion.1), channel_id=1, source_target_pairs={{0,96},{16,112},{32,64},{48,80},{64,32},{80,48},{96,0},{112,16},{1... | collective-permute-start | bytes 196616 | tf_op jit(solution)/shard_map/ppermute | solution.py:167
  104.2 2.0 %collective-permute-start.8 = (bf16[32,1024]{1,0:T(8,128)(2,1)S(1)}, bf16[32,1024]{1,0:T(8,128)(2,1)S(1)}, u32[]{:S(2)}, u32[]{:S(2)}) collective-permute-start(bf16[32,1024]{1,0:T(8,128)(2,1)S(1)} %add_convert_fusion.1), channel_id=1, source_target_pairs={{0,32},{16,48},{32,0},{48,16},{64,96},{80,112},{96,64},{112,80},{1... | collective-permute-start | bytes 196616 | tf_op jit(solution)/shard_map/ppermute | solution.py:167
  106.3 1.5 %collective-permute-start.9 = (bf16[32,1024]{1,0:T(8,128)(2,1)S(1)}, bf16[32,1024]{1,0:T(8,128)(2,1)S(1)}, u32[]{:S(2)}, u32[]{:S(2)}) collective-permute-start(bf16[32,1024]{1,0:T(8,128)(2,1)S(1)} %add_convert_fusion.1), channel_id=1, source_target_pairs={{0,64},{16,80},{32,96},{48,112},{64,0},{80,16},{96,32},{112,48},{1... | collective-permute-start | bytes 196616 | tf_op jit(solution)/shard_map/ppermute | solution.py:167
  107.7 0.0 collective-permute-done.10
  107.7 0.5 collective-permute-done.8
  108.3 5.5 %collective-permute-done.9 = bf16[32,1024]{1,0:T(8,128)(2,1)S(1)} collective-permute-done((bf16[32,1024]{1,0:T(8,128)(2,1)S(1)}, bf16[32,1024]{1,0:T(8,128)(2,1)S(1)}, u32[]{:S(2)}, u32[]{:S(2)}) %collective-permute-start.9) | collective-permute-done | bytes 65568 | tf_op jit(solution)/shard_map/ppermute | solution.py:167
  113.8 0.0 copy-done.2
  113.8 1.6 %multiply_add_fusion = (bf16[32,1024]{1,0:T(8,128)(2,1)S(1)}, f32[32,1024]{1,0:T(8,128)}) fusion(f32[32,1024]{1,0:T(8,128)S(1)} %copy-done.2, bf16[32,1024]{1,0:T(8,128)(2,1)S(1)} %collective-permute-done.10, bf16[32,1024]{1,0:T(8,128)(2,1)S(1)} %collective-permute-done.9, bf16[32,1024]{1,0:T(8,128)(2,1)S(1)} %collective-permute-done.8, ...), kind=kLoop, calls=%fused_computation.16 | loop fusion | flops 458752 | bytes 655364 | tf_op jit(solution)/shard_map/add | solution.py:242
  115.3 0.0 all-to-all-done.2.in_ref
  115.3 0.0 copy-start
  115.4 11.6 %all_to_all.21 = bf16[8,32,1024]{2,1,0:T(8,128)(2,1)S(1)} all-to-all(bf16[8,32,1024]{2,1,0:T(8,128)(2,1)S(1)} %broadcast_in_dim.2), channel_id=1, replica_groups={{0,2,4,6,8,10,12,14},{1,3,5,7,9,11,13,15},{16,18,20,22,24,26,28,30},{17..., dimensions={0} | all-to-all | bytes 1048576 | tf_op jit(solution)/shard_map/all_to_all | solution.py:245
  127.0 3.7 %collective-permute-start.11 = (bf16[8,32,1024]{2,1,0:T(8,128)(2,1)S(1)}, bf16[8,32,1024]{2,1,0:T(8,128)(2,1)S(1)}, u32[]{:S(2)}, u32[]{:S(2)}) collective-permute-start(bf16[8,32,1024]{2,1,0:T(8,128)(2,1)S(1)} %all_to_all.21), channel_id=1, source_target_pairs={{0,1},{1,0},{2,3},{3,2},{4,5},{5,4},{6,7},{7,6},{8,9},{9,8},{10,11... | collective-permute-start | bytes 1572872 | tf_op jit(solution)/shard_map/ppermute | solution.py:167
  130.7 0.0 copy-done
  130.7 2.1 %shard_map.132 = (bf16[128,512]{1,0:T(8,128)(2,1)}, bf16[128,512]{1,0:T(8,128)(2,1)}, bf16[128,512]{1,0:T(8,128)(2,1)}) custom-call(bf16[16,160,128]{2,1,0:T(8,128)(2,1)} %copy-done), custom_call_target="tpu_custom_call" | custom-call | tf_op jit(solution)/shard_map/pallas_call | solution.py:153
  132.8 0.0 collective-permute-done.11
  132.8 0.1 select_bitcast_fusion.1
  132.8 1.1 pad_maximum_fusion
  (2 shorter events, 0.1 us)
Async XLA Ops:
  48.7 14.9 %all-to-all-start.1 = ((bf16[16,32,128]{2,1,0:T(8,128)(2,1)}), bf16[16,32,128]{2,1,0:T(8,128)(2,1)S(1)}, u32[]{:S(2)}, u32[]{:S(2)}) async-start(bf16[16,32,128]{2,1,0:T(8,128)(2,1)} %get-tuple-element.17), calls=%async_computation.1 | async-start | bytes 262144 | tf_op jit(solution)/shard_map/all_to_all | solution.py:211
  54.5 59.3 %copy-start.2 = (f32[32,1024]{1,0:T(8,128)S(1)}, f32[32,1024]{1,0:T(8,128)}, u32[]{:S(2)}) copy-start(f32[32,1024]{1,0:T(8,128)} %param.14) | copy-start | bytes 393220
  63.5 0.7 copy-start.1
  66.6 4.1 %collective-permute-start = (bf16[2,4,32,1024]{3,2,1,0:T(8,128)(2,1)}, bf16[2,4,32,1024]{3,2,1,0:T(8,128)(2,1)S(1)}, u32[]{:S(2)}, u32[]{:S(2)}) collective-permute-start(bf16[2,4,32,1024]{3,2,1,0:T(8,128)(2,1)} %get-tuple-element.22), channel_id=1, source_target_pairs={{0,1},{1,0},{2,3},{3,2},{4,5},{5,4},{6,7},{7,6},{8,9},{9,8},{10,11... | collective-permute-start | bytes 1572872 | tf_op jit(solution)/shard_map/ppermute | solution.py:167
  71.7 8.9 %collective-permute-start.1 = (bf16[4,32,1024]{2,1,0:T(8,128)(2,1)S(1)}, bf16[4,32,1024]{2,1,0:T(8,128)(2,1)S(1)}, u32[]{:S(2)}, u32[]{:S(2)}) collective-permute-start(bf16[4,32,1024]{2,1,0:T(8,128)(2,1)S(1)} %fusion), channel_id=1, source_target_pairs={{0,2},{1,3},{2,0},{3,1},{4,6},{5,7},{6,4},{7,5},{8,10},{9,11},{10,... | collective-permute-start | bytes 786440 | tf_op jit(solution)/shard_map/ppermute | solution.py:167
  72.2 43.2 %all-to-all-start.2 = ((bf16[16,160,128]{2,1,0:T(8,128)(2,1)}), bf16[16,160,128]{2,1,0:T(8,128)(2,1)S(1)}, u32[]{:S(2)}, u32[]{:S(2)}) async-start(bf16[16,160,128]{2,1,0:T(8,128)(2,1)} %shard_map.130), calls=%async_computation.2 | async-start | bytes 1310720 | tf_op jit(solution)/shard_map/all_to_all | solution.py:233
  81.6 3.9 %collective-permute-start.2 = (bf16[32,1024]{1,0:T(8,128)(2,1)S(1)}, bf16[32,1024]{1,0:T(8,128)(2,1)S(1)}, u32[]{:S(2)}, u32[]{:S(2)}) collective-permute-start(bf16[32,1024]{1,0:T(8,128)(2,1)S(1)} %get-tuple-element.31), channel_id=1, source_target_pairs={{0,4},{1,5},{2,6},{3,7},{4,0},{5,1},{6,2},{7,3},{8,12},{9,13},{10,... | collective-permute-start | bytes 196616 | tf_op jit(solution)/shard_map/ppermute | solution.py:167
  82.9 4.8 %collective-permute-start.3 = (bf16[32,1024]{1,0:T(8,128)(2,1)S(1)}, bf16[32,1024]{1,0:T(8,128)(2,1)S(1)}, u32[]{:S(2)}, u32[]{:S(2)}) collective-permute-start(bf16[32,1024]{1,0:T(8,128)(2,1)S(1)} %get-tuple-element.33), channel_id=1, source_target_pairs={{0,8},{1,9},{2,10},{3,11},{4,12},{5,13},{6,14},{7,15},{8,0},{9,1},... | collective-permute-start | bytes 196616 | tf_op jit(solution)/shard_map/ppermute | solution.py:167
  85.3 4.8 %collective-permute-start.4 = (bf16[32,1024]{1,0:T(8,128)(2,1)S(1)}, bf16[32,1024]{1,0:T(8,128)(2,1)S(1)}, u32[]{:S(2)}, u32[]{:S(2)}) collective-permute-start(bf16[32,1024]{1,0:T(8,128)(2,1)S(1)} %get-tuple-element.32), channel_id=1, source_target_pairs={{0,12},{1,13},{2,14},{3,15},{4,8},{5,9},{6,10},{7,11},{8,4},{9,5},... | collective-permute-start | bytes 196616 | tf_op jit(solution)/shard_map/ppermute | solution.py:167
  91.1 6.6 %collective-permute-start.5 = (bf16[32,1024]{1,0:T(8,128)(2,1)S(1)}, bf16[32,1024]{1,0:T(8,128)(2,1)S(1)}, u32[]{:S(2)}, u32[]{:S(2)}) collective-permute-start(bf16[32,1024]{1,0:T(8,128)(2,1)S(1)} %fusion.7), channel_id=1, source_target_pairs={{0,16},{16,0},{32,48},{48,32},{64,80},{80,64},{96,112},{112,96},{1... | collective-permute-start | bytes 196616 | tf_op jit(solution)/shard_map/ppermute | solution.py:167
  92.8 5.9 %collective-permute-start.6 = (bf16[32,1024]{1,0:T(8,128)(2,1)S(1)}, bf16[32,1024]{1,0:T(8,128)(2,1)S(1)}, u32[]{:S(2)}, u32[]{:S(2)}) collective-permute-start(bf16[32,1024]{1,0:T(8,128)(2,1)S(1)} %fusion.7), channel_id=1, source_target_pairs={{0,128},{16,144},{32,160},{48,176},{64,192},{80,208},{96,224},{112... | collective-permute-start | bytes 196616 | tf_op jit(solution)/shard_map/ppermute | solution.py:167
  95.5 6.5 %collective-permute-start.7 = (bf16[32,1024]{1,0:T(8,128)(2,1)S(1)}, bf16[32,1024]{1,0:T(8,128)(2,1)S(1)}, u32[]{:S(2)}, u32[]{:S(2)}) collective-permute-start(bf16[32,1024]{1,0:T(8,128)(2,1)S(1)} %fusion.7), channel_id=1, source_target_pairs={{0,144},{16,128},{32,176},{48,160},{64,208},{80,192},{96,240},{112... | collective-permute-start | bytes 196616 | tf_op jit(solution)/shard_map/ppermute | solution.py:167
  102.0 5.7 %collective-permute-start.10 = (bf16[32,1024]{1,0:T(8,128)(2,1)S(1)}, bf16[32,1024]{1,0:T(8,128)(2,1)S(1)}, u32[]{:S(2)}, u32[]{:S(2)}) collective-permute-start(bf16[32,1024]{1,0:T(8,128)(2,1)S(1)} %add_convert_fusion.1), channel_id=1, source_target_pairs={{0,96},{16,112},{32,64},{48,80},{64,32},{80,48},{96,0},{112,16},{1... | collective-permute-start | bytes 196616 | tf_op jit(solution)/shard_map/ppermute | solution.py:167
  104.2 4.0 %collective-permute-start.8 = (bf16[32,1024]{1,0:T(8,128)(2,1)S(1)}, bf16[32,1024]{1,0:T(8,128)(2,1)S(1)}, u32[]{:S(2)}, u32[]{:S(2)}) collective-permute-start(bf16[32,1024]{1,0:T(8,128)(2,1)S(1)} %add_convert_fusion.1), channel_id=1, source_target_pairs={{0,32},{16,48},{32,0},{48,16},{64,96},{80,112},{96,64},{112,80},{1... | collective-permute-start | bytes 196616 | tf_op jit(solution)/shard_map/ppermute | solution.py:167
  106.3 7.5 %collective-permute-start.9 = (bf16[32,1024]{1,0:T(8,128)(2,1)S(1)}, bf16[32,1024]{1,0:T(8,128)(2,1)S(1)}, u32[]{:S(2)}, u32[]{:S(2)}) collective-permute-start(bf16[32,1024]{1,0:T(8,128)(2,1)S(1)} %add_convert_fusion.1), channel_id=1, source_target_pairs={{0,64},{16,80},{32,96},{48,112},{64,0},{80,16},{96,32},{112,48},{1... | collective-permute-start | bytes 196616 | tf_op jit(solution)/shard_map/ppermute | solution.py:167
  115.3 15.4 %copy-start = (bf16[16,160,128]{2,1,0:T(8,128)(2,1)}, bf16[16,160,128]{2,1,0:T(8,128)(2,1)S(1)}, u32[]{:S(2)}) copy-start(bf16[16,160,128]{2,1,0:T(8,128)(2,1)S(1)} %all-to-all-done.2.in_ref) | copy-start | bytes 1966084
  127.0 5.8 %collective-permute-start.11 = (bf16[8,32,1024]{2,1,0:T(8,128)(2,1)S(1)}, bf16[8,32,1024]{2,1,0:T(8,128)(2,1)S(1)}, u32[]{:S(2)}, u32[]{:S(2)}) collective-permute-start(bf16[8,32,1024]{2,1,0:T(8,128)(2,1)S(1)} %all_to_all.21), channel_id=1, source_target_pairs={{0,1},{1,0},{2,3},{3,2},{4,5},{5,4},{6,7},{7,6},{8,9},{9,8},{10,11... | collective-permute-start | bytes 1572872 | tf_op jit(solution)/shard_map/ppermute | solution.py:167

commit v3 on v2

v3 whole, which is shorter than its diff:
```python
import jax
import jax.numpy as jnp
from jax import lax
from jax.experimental import pallas as pl
from jax.experimental.pallas import tpu as pltpu
from jax.sharding import PartitionSpec as P

D = 1024
HEADS = 8
HEAD = 64
BLOCK = 64
NB = 8
ROWS = 2
HD = 512
CELLS = ROWS * BLOCK
PAIR = 2 * HEAD
HALF = BLOCK // 2
LISTS = 16
GROUP = 512

learn_rate = 0.01
decay_rate = 0.9

BF = jnp.bfloat16
F32 = jnp.float32
VMEM_BYTES = 56 * 2**20
SMALL_BYTES = 24 * 2**20
SCALE = HEAD**-0.5


def dot(a, b, dims):
    return lax.dot_general(a, b, ((dims[:1], dims[1:]), ((), ())), preferred_element_type=F32)


def low_lanes():
    return lax.broadcasted_iota(jnp.int32, (1, PAIR), 1) < HEAD


def swap(x):
    return jnp.concatenate([x[:, HEAD:], x[:, :HEAD]], axis=1)


def fold(x):
    top, bottom = x[:HALF], x[HALF:]
    low = low_lanes()
    return jnp.where(low, top, swap(bottom)), jnp.where(low, swap(top), bottom)


def unfold(first, second):
    low = low_lanes()
    return jnp.concatenate([jnp.where(low, first, swap(second)), jnp.where(low, swap(first), second)], axis=0)


def pack_kernel(lon_ref, lat_ref, count_ref, q_ref, k_ref, v_ref, up_ref, w_ref, out_ref):
    grad = dot(up_ref[...], w_ref[...], (1, 1)).astype(BF)
    for h in range(HEADS):
        feats = slice(h * HEAD, (h + 1) * HEAD)
        kv = jnp.concatenate([k_ref[:, feats], v_ref[:, feats]], axis=1)
        qg = jnp.concatenate([q_ref[:, feats], grad[:, feats]], axis=1)
        for r in range(ROWS):
            slab = r * HEADS + h
            out_ref[slab, 0:BLOCK, :] = qg[r * BLOCK : (r + 1) * BLOCK]
            out_ref[slab, BLOCK : BLOCK + CELLS, :] = kv
    block = lax.broadcasted_iota(jnp.int32, (LISTS, PAIR), 1)
    for r in range(ROWS):
        seen = jnp.zeros((LISTS, PAIR), F32)
        for t in range(NB):
            named = jnp.where(t < count_ref[r], lon_ref[r, 0, t] * ROWS + lat_ref[r, 0, t], -1)
            seen = jnp.where(block == named, 1.0, seen)
        for h in range(HEADS):
            out_ref[r * HEADS + h, BLOCK + CELLS :, :] = seen.astype(BF)


def seen_blocks(in_ref):
    lonb = in_ref.shape[0]
    tile = (lonb, lonb * BLOCK)
    spread = lax.broadcasted_iota(jnp.int32, tile, 0) == lax.broadcasted_iota(jnp.int32, tile, 1) // BLOCK
    return dot(in_ref[:, BLOCK + CELLS, :].astype(F32), spread.astype(F32), (0, 0))[: lonb * ROWS] > 0.5


def tiles_of(in_ref):
    lonb = in_ref.shape[0]
    x = in_ref[:, 0:BLOCK, :].reshape(lonb * BLOCK, PAIR)
    return x, in_ref[:, BLOCK : BLOCK + CELLS, :].reshape(lonb * CELLS, PAIR)


def forward_kernel(in_ref, att_ref, stat_ref, score_ref):
    x, kv = tiles_of(in_ref)
    keys, cells = score_ref.shape
    k_only = jnp.where(low_lanes(), kv * jnp.asarray(SCALE, BF), jnp.zeros((), BF))
    v_t = kv.T[HEAD:]
    seen = seen_blocks(in_ref)
    tops = []
    for g in range(0, keys, GROUP):
        scores = dot(k_only[g : g + GROUP], x, (1, 1))
        score_ref[g : g + GROUP, :] = scores
        tops += [jnp.max(scores[j : j + BLOCK], axis=0, keepdims=True) for j in range(0, GROUP, BLOCK)]
    top = jnp.max(jnp.where(seen, jnp.concatenate(tops, axis=0), -1e30), axis=0, keepdims=True)
    shift = jnp.where(seen, top, 1e30)
    att = jnp.zeros((HEAD, cells), F32)
    total = jnp.zeros((8, cells), F32)
    for g in range(0, keys, GROUP):
        probs = []
        for j in range(g, g + GROUP, BLOCK):
            prob = jnp.exp(score_ref[j : j + BLOCK, :] - shift[j // BLOCK : j // BLOCK + 1])
            total = total + jnp.sum(prob.reshape(BLOCK // 8, 8, cells), axis=0)
            probs.append(prob.astype(BF))
        att = att + dot(v_t[:, g : g + GROUP], jnp.concatenate(probs, axis=0), (1, 0))
    total = jnp.sum(total, axis=0, keepdims=True)
    att = (att * (1.0 / total)).astype(BF)
    delta = jnp.sum(x.T[HEAD:].astype(F32) * att.astype(F32), axis=0, keepdims=True)
    row = lax.broadcasted_iota(jnp.int32, stat_ref.shape, 0)
    stat_ref[...] = jnp.where(row == 0, top + jnp.log(total), delta)
    for i in range(0, cells, PAIR):
        b = i // BLOCK
        att_ref[b], att_ref[b + 1] = fold(att[:, i : i + PAIR])


def backward_kernel(in_ref, stat_ref, out_ref):
    x, kv = tiles_of(in_ref)
    keys, cells = kv.shape[0], x.shape[0]
    low = low_lanes()
    zero = jnp.zeros((), BF)
    k_only = jnp.where(low, kv * jnp.asarray(SCALE, BF), zero)
    v_only = jnp.where(low, zero, kv)
    k_t = kv.T[:HEAD]
    shift = jnp.where(seen_blocks(in_ref), stat_ref[0:1, :], 1e30)
    delta = stat_ref[1:2, :]
    grad_q = jnp.zeros((HEAD, cells), F32)
    for g in range(0, keys, GROUP):
        scores = dot(k_only[g : g + GROUP], x, (1, 1))
        prob_grad = dot(v_only[g : g + GROUP], x, (1, 1))
        probs, score_grads = [], []
        for j in range(0, GROUP, BLOCK):
            b = (g + j) // BLOCK
            prob = jnp.exp(scores[j : j + BLOCK] - shift[b : b + 1])
            probs.append(prob.astype(BF))
            score_grads.append((prob * (prob_grad[j : j + BLOCK] - delta)).astype(BF))
        probs = jnp.concatenate(probs, axis=0)
        score_grads = jnp.concatenate(score_grads, axis=0)
        grad_q = grad_q + dot(k_t[:, g : g + GROUP], score_grads, (1, 0))
        grad_kv = jnp.where(low, dot(score_grads, x, (1, 0)) * SCALE, dot(probs, x, (1, 0)))
        out_ref[g // CELLS : (g + GROUP) // CELLS, HALF:, :] = grad_kv.astype(BF).reshape(GROUP // CELLS, CELLS, PAIR)
    grad_q = (grad_q * SCALE).astype(BF)
    for i in range(0, cells, PAIR):
        b = i // BLOCK
        out_ref[b, 0:HALF, :], out_ref[b + 1, 0:HALF, :] = fold(grad_q[:, i : i + PAIR])


def weight_kernel(place_ref, att_ref, up_ref, out_ref, att_t):
    for h in range(HEADS):
        piece = unfold(att_ref[h], att_ref[HEADS + h])
        att_t[2 * h] = piece[:HALF]
        att_t[2 * h + 1] = piece[HALF:]
    place = place_ref[0]
    rows = [att_t[place ^ (4 * dx + 2 * dy)] for dy in range(2) for dx in range(HEADS // 2)]
    part = dot(jnp.concatenate(rows, axis=0), up_ref[...], (1, 0))
    out_ref[...] = part.astype(BF).reshape(out_ref.shape)


def unpack_kernel(in_ref, gq_ref, gk_ref, gv_ref):
    gq_t = []
    for h in range(HEADS):
        feats = slice(h * HEAD, (h + 1) * HEAD)
        gq_t.append(unfold(in_ref[h, 0:HALF, :], in_ref[HEADS + h, 0:HALF, :]))
        kv = sum(in_ref[r * HEADS + h, HALF:, :].astype(F32) for r in range(ROWS)).astype(BF)
        gk_ref[:, feats] = kv[:, :HEAD]
        gv_ref[:, feats] = kv[:, HEAD:]
    gq_ref[...] = jnp.concatenate(gq_t, axis=0).T


def call(kernel, outs, *args, scratch=(), scalars=0, vmem=VMEM_BYTES):
    on_chip = [pl.BlockSpec(memory_space=pltpu.SMEM if i < scalars else pltpu.VMEM) for i in range(len(args))]
    return pl.pallas_call(
        kernel,
        out_shape=outs,
        in_specs=on_chip,
        scratch_shapes=scratch,
        compiler_params=pltpu.CompilerParams(vmem_limit_bytes=vmem),
    )(*args)


def shape(*dims, dtype=BF):
    return jax.ShapeDtypeStruct(dims, dtype)


def pairwise(x, axis, bit):
    return lax.ppermute(x, axis, [(i, i ^ bit) for i in range(lax.axis_size(axis))])


def plus(*parts):
    total = parts[0].astype(F32)
    for part in parts[1:]:
        total = total + part.astype(F32)
    return total


def quad_sum(x, a, b):
    x = x.astype(BF)
    return plus(x, pairwise(x, "lon", a)) + plus(pairwise(x, "lon", b), pairwise(x, "lon", a ^ b))


def on_device(queries, keys, values, upstream, out_weight, average, nbr_lon, nbr_lat, counts):
    lonb = lax.axis_size("lon")
    lats = lax.axis_size("lat")
    same_core = [[c + 2 * i for i in range(lats // 2)] for c in range(2)]
    up = upstream.reshape(CELLS, D)
    slabs = call(
        pack_kernel,
        shape(lonb, BLOCK + CELLS + LISTS, PAIR),
        nbr_lon,
        nbr_lat,
        counts.reshape(ROWS),
        queries.reshape(CELLS, HD),
        keys.reshape(CELLS, HD),
        values.reshape(CELLS, HD),
        up,
        out_weight,
        scalars=3,
    )
    slabs = lax.all_to_all(slabs, "lon", 0, 0, tiled=True)
    cells = lonb * BLOCK
    att, stats = call(
        forward_kernel,
        (shape(lonb, HALF, PAIR), shape(8, cells, dtype=F32)),
        slabs,
        scratch=[pltpu.VMEM((lonb * CELLS, cells), F32)],
    )
    att = lax.all_to_all(att, "lon", 0, 0, tiled=True)
    grads = call(backward_kernel, shape(lonb, HALF + CELLS, PAIR), slabs, stats)
    att, grads = lax.optimization_barrier((att, grads))
    rows = HD // lats
    half = shape(2, lats // 4, rows, D)
    place = lax.axis_index("lat")
    send, keep = (
        call(
            weight_kernel,
            half,
            (place ^ core).reshape(1),
            att,
            up,
            scratch=[pltpu.VMEM((2 * HEADS, HALF, CELLS), BF)],
            scalars=1,
            vmem=SMALL_BYTES,
        )
        for core in (1, 0)
    )
    grads = lax.all_to_all(grads, "lon", 0, 0, tiled=True)
    came = pairwise(send, "lat", 1)
    by_y = pairwise(plus(keep[1], came[1]).astype(BF), "lat", 2)
    by_x = [plus(keep[0, i], came[0, i], by_y[i]) for i in range(lats // 4)]
    by_x = by_x[:1] + [pairwise(by_x[i].astype(BF), "lat", 4 * i) for i in range(1, lats // 4)]
    total = quad_sum(plus(*by_x), 1, 8)
    total = quad_sum(total, 2, 4)
    own_weight = lax.dynamic_slice_in_dim(out_weight, place * rows, rows, 0).astype(F32)
    updated = own_weight - learn_rate * total
    averaged = decay_rate * average + (1.0 - decay_rate) * updated
    cell_grads = shape(CELLS, HD)
    gq, gk, gv = call(unpack_kernel, (cell_grads, cell_grads, cell_grads), grads, vmem=SMALL_BYTES)
    averaged, gq, gk, gv = lax.optimization_barrier((averaged, gq, gk, gv))
    copies = jnp.broadcast_to(averaged.astype(BF)[None], (lats // 2, rows, D))
    mine = lax.all_to_all(copies, "lat", 0, 0, axis_index_groups=same_core, tiled=True)
    other = pairwise(mine, "lat", 1)
    first = place % 2 == 0
    next_weights = jnp.stack([jnp.where(first, mine, other), jnp.where(first, other, mine)], axis=1).reshape(HD, D)
    own = (ROWS, BLOCK, HD)
    return (gq.reshape(own), gk.reshape(own), gv.reshape(own), updated, next_weights)


def solution(mesh):
    cells = P("lat", "lon", None)
    return jax.shard_map(
        on_device,
        mesh=mesh,
        in_specs=(cells, cells, cells, cells, P(), P("lat", None), cells, cells, P("lat", "lon")),
        out_specs=(cells, cells, cells, P("lat", None), P()),
        check_vma=False,
    )
```

time: 135 us -> 123 us (0.911)
  Pallas kernels: 25.2 us -> 17.2 us
  other arithmetic: 5.62 us -> 2.94 us
  local copies, waits for them, and re-layouts: 2.01 us -> 0.06 us
    pallas_call x5 -> x6, Pallas kernels: 25.2 us -> 17.2 us  [call(): pl.pallas_call(kernel, out_shape=outs, in_specs=on_chip, scratch_shapes=s...]
    unnamed x7 -> x4, local copies, waits for them, and re-layouts: 1.96 us -> 0.01 us
  transfers between devices with their start and end apart: 14 -> 14, of which waited for: 9 -> 7; matrix products, arithmetic and copies ran while one was open for 3% -> 1% of each run, Pallas kernels for 8% -> 6%
where the time goes in v3:
time: 123 us
  blocking collectives  46.4 us (38%)
  starting transfers between devices  34.9 us (28%)
  waiting for transfers between devices  20.3 us (17%)
  Pallas kernels  17.2 us (14%)
  other arithmetic  2.94 us (2%)
    all_to_all x1, blocking collectives, on_device(): slabs = lax.all_to_all(slabs, 'lon', 0, 0, tiled=True)  34.5 us
    ppermute x12, starting transfers between devices, pairwise(): lax.ppermute(x, axis, [(i, i ^ bit) for i in range(lax.axis_size(axis))])  21.6 us
    ppermute x12, waiting for transfers between devices, pairwise(): lax.ppermute(x, axis, [(i, i ^ bit) for i in range(lax.axis_size(axis))])  18.9 us
    pallas_call x6, Pallas kernels, call(): pl.pallas_call(kernel, out_shape=outs, in_specs=on_chip, scratch_shapes=s...  17.2 us
    all_to_all x1, blocking collectives, on_device(): lax.all_to_all(copies, 'lat', 0, 0, axis_index_groups=same_core, tiled=True)  11.9 us
    all_to_all x1, starting transfers between devices, on_device(): grads = lax.all_to_all(grads, 'lon', 0, 0, tiled=True)  7.49 us
    all_to_all x1, starting transfers between devices, on_device(): att = lax.all_to_all(att, 'lon', 0, 0, tiled=True)  5.82 us
  transfers between devices with their start and end apart: 14, of which 7 were waited for; matrix products, arithmetic and copies ran while one was open for 1% of the time, Pallas kernels for 6%

profile of v3, /device:TPU:1, one launch (start us, length us, event | category | flops | bytes accessed | tf_op | source)
XLA Modules:
  0.0 122.5 jit_solution(5810029824249984406)
XLA Ops:
  0.6 3.0 %shard_map.128 = bf16[16,208,128]{2,1,0:T(8,128)(2,1)} custom-call(s32[2,1,8]{2,1,0:T(1,128)} %lon_ref.1, s32[2,1,8]{2,1,0:T(1,128)} %lat_ref.1, s32[2]{0:T(128)} %bitcast.54, bf16[128,512]{1,0:T(8,128)(2,1)} %bitcast.51, bf16[128,512]{1,0:T(8,128)(2,1)} %bitcast.52, bf16[128,512]{1,0:T(8,128)(2,1)} %bitcast.53, bf16[128,1024]{1,0:T(8,128)(2,1)} %bitcast.47, ...), custom_call_target="tpu_custom_call" | custom-call | tf_op jit(solution)/shard_map/pallas_call | solution.py:174
  3.6 34.5 %all_to_all.20.in_ref = bf16[16,208,128]{2,1,0:T(8,128)(2,1)} all-to-all(bf16[16,208,128]{2,1,0:T(8,128)(2,1)} %shard_map.128), channel_id=1, replica_groups=mesh['lon'=16,'lat'=16] {'lon'}, dimensions={0} | all-to-all | bytes 1703936 | tf_op jit(solution)/shard_map/all_to_all | solution.py:221
  38.1 4.9 %shard_map.129 = (bf16[16,32,128]{2,1,0:T(8,128)(2,1)}, f32[8,1024]{1,0:T(8,128)}) custom-call(bf16[16,208,128]{2,1,0:T(8,128)(2,1)} %all_to_all.20.in_ref), custom_call_target="tpu_custom_call" | custom-call | tf_op jit(solution)/shard_map/pallas_call | solution.py:174
  43.0 5.8 %all-to-all-start.1 = ((bf16[16,32,128]{2,1,0:T(8,128)(2,1)}), bf16[16,32,128]{2,1,0:T(8,128)(2,1)S(1)}, u32[]{:S(2)}, u32[]{:S(2)}) async-start(bf16[16,32,128]{2,1,0:T(8,128)(2,1)} %get-tuple-element.16), calls=%async_computation.1 | async-start | bytes 262144 | tf_op jit(solution)/shard_map/all_to_all | solution.py:229
  48.8 0.0 copy-start
  48.9 7.6 %shard_map.130 = bf16[16,160,128]{2,1,0:T(8,128)(2,1)} custom-call(bf16[16,208,128]{2,1,0:T(8,128)(2,1)} %all_to_all.20.in_ref, f32[8,1024]{1,0:T(8,128)} %get-tuple-element.17.stat_ref), custom_call_target="tpu_custom_call" | custom-call | tf_op jit(solution)/shard_map/pallas_call | solution.py:174
  56.5 1.4 %all-to-all-done.1.att_ref = bf16[16,32,128]{2,1,0:T(8,128)(2,1)S(1)} async-done(((bf16[16,32,128]{2,1,0:T(8,128)(2,1)}), bf16[16,32,128]{2,1,0:T(8,128)(2,1)S(1)}, u32[]{:S(2)}, u32[]{:S(2)}) %all-to-all-start.1) | async-done | bytes 131104 | tf_op jit(solution)/shard_map/all_to_all | solution.py:229
  57.9 0.0 copy-done
  57.9 0.4 shard_map.132
  58.2 2.4 %collective-permute-start = (bf16[2,4,32,1024]{3,2,1,0:T(8,128)(2,1)S(1)}, bf16[2,4,32,1024]{3,2,1,0:T(8,128)(2,1)S(1)}, u32[]{:S(2)}, u32[]{:S(2)}) collective-permute-start(bf16[2,4,32,1024]{3,2,1,0:T(8,128)(2,1)S(1)} %shard_map.132), channel_id=1, source_target_pairs={{0,1},{1,0},{2,3},{3,2},{4,5},{5,4},{6,7},{7,6},{8,9},{9,8},{10,11... | collective-permute-start | bytes 1572872 | tf_op jit(solution)/shard_map/ppermute | solution.py:188
  60.7 0.4 shard_map.131
  61.0 1.2 collective-permute-done
  62.2 0.1 fusion
  62.3 0.5 collective-permute-start.1
  62.8 7.5 %all-to-all-start.2 = ((bf16[16,160,128]{2,1,0:T(8,128)(2,1)}), bf16[16,160,128]{2,1,0:T(8,128)(2,1)S(1)}, u32[]{:S(2)}, u32[]{:S(2)}) async-start(bf16[16,160,128]{2,1,0:T(8,128)(2,1)} %shard_map.130), calls=%async_computation.2 | async-start | bytes 1310720 | tf_op jit(solution)/shard_map/all_to_all | solution.py:248
  70.3 0.0 collective-permute-done.1
  70.3 0.1 fusion.3
  70.4 1.3 %collective-permute-start.2 = (bf16[32,1024]{1,0:T(8,128)(2,1)S(1)}, bf16[32,1024]{1,0:T(8,128)(2,1)S(1)}, u32[]{:S(2)}, u32[]{:S(2)}) collective-permute-start(bf16[32,1024]{1,0:T(8,128)(2,1)S(1)} %get-tuple-element.29), channel_id=1, source_target_pairs={{0,4},{1,5},{2,6},{3,7},{4,0},{5,1},{6,2},{7,3},{8,12},{9,13},{10,... | collective-permute-start | bytes 196616 | tf_op jit(solution)/shard_map/ppermute | solution.py:188
  71.6 1.8 %collective-permute-start.4 = (bf16[32,1024]{1,0:T(8,128)(2,1)S(1)}, bf16[32,1024]{1,0:T(8,128)(2,1)S(1)}, u32[]{:S(2)}, u32[]{:S(2)}) collective-permute-start(bf16[32,1024]{1,0:T(8,128)(2,1)S(1)} %get-tuple-element.30), channel_id=1, source_target_pairs={{0,12},{1,13},{2,14},{3,15},{4,8},{5,9},{6,10},{7,11},{8,4},{9,5},... | collective-permute-start | bytes 196616 | tf_op jit(solution)/shard_map/ppermute | solution.py:188
  73.5 0.6 collective-permute-start.3
  74.1 0.0 collective-permute-done.2
  74.1 2.2 %collective-permute-done.4 = bf16[32,1024]{1,0:T(8,128)(2,1)S(1)} collective-permute-done((bf16[32,1024]{1,0:T(8,128)(2,1)S(1)}, bf16[32,1024]{1,0:T(8,128)(2,1)S(1)}, u32[]{:S(2)}, u32[]{:S(2)}) %collective-permute-start.4) | collective-permute-done | bytes 65568 | tf_op jit(solution)/shard_map/ppermute | solution.py:188
  76.3 2.1 %collective-permute-done.3 = bf16[32,1024]{1,0:T(8,128)(2,1)S(1)} collective-permute-done((bf16[32,1024]{1,0:T(8,128)(2,1)S(1)}, bf16[32,1024]{1,0:T(8,128)(2,1)S(1)}, u32[]{:S(2)}, u32[]{:S(2)}) %collective-permute-start.3) | collective-permute-done | bytes 65568 | tf_op jit(solution)/shard_map/ppermute | solution.py:188
  78.4 0.1 fusion.7
  78.4 0.0 copy-start.1
  78.5 3.9 %collective-permute-start.7 = (bf16[32,1024]{1,0:T(8,128)(2,1)S(1)}, bf16[32,1024]{1,0:T(8,128)(2,1)S(1)}, u32[]{:S(2)}, u32[]{:S(2)}) collective-permute-start(bf16[32,1024]{1,0:T(8,128)(2,1)S(1)} %fusion.7), channel_id=1, source_target_pairs={{0,144},{16,128},{32,176},{48,160},{64,208},{80,192},{96,240},{112... | collective-permute-start | bytes 196616 | tf_op jit(solution)/shard_map/ppermute | solution.py:188
  82.3 0.3 collective-permute-start.6
  82.6 0.1 collective-permute-start.5
  82.7 6.4 %collective-permute-done.7 = bf16[32,1024]{1,0:T(8,128)(2,1)S(1)} collective-permute-done((bf16[32,1024]{1,0:T(8,128)(2,1)S(1)}, bf16[32,1024]{1,0:T(8,128)(2,1)S(1)}, u32[]{:S(2)}, u32[]{:S(2)}) %collective-permute-start.7) | collective-permute-done | bytes 65568 | tf_op jit(solution)/shard_map/ppermute | solution.py:188
  89.1 0.0 collective-permute-done.6
  89.1 0.0 collective-permute-done.5
  89.2 4.5 %collective-permute-start.10 = (bf16[32,1024]{1,0:T(8,128)(2,1)S(1)}, bf16[32,1024]{1,0:T(8,128)(2,1)S(1)}, u32[]{:S(2)}, u32[]{:S(2)}) collective-permute-start(bf16[32,1024]{1,0:T(8,128)(2,1)S(1)} %add_convert_fusion.1), channel_id=1, source_target_pairs={{0,96},{16,112},{32,64},{48,80},{64,32},{80,48},{96,0},{112,16},{1... | collective-permute-start | bytes 196616 | tf_op jit(solution)/shard_map/ppermute | solution.py:188
  93.7 1.3 %collective-permute-start.9 = (bf16[32,1024]{1,0:T(8,128)(2,1)S(1)}, bf16[32,1024]{1,0:T(8,128)(2,1)S(1)}, u32[]{:S(2)}, u32[]{:S(2)}) collective-permute-start(bf16[32,1024]{1,0:T(8,128)(2,1)S(1)} %add_convert_fusion.1), channel_id=1, source_target_pairs={{0,64},{16,80},{32,96},{48,112},{64,0},{80,16},{96,32},{112,48},{1... | collective-permute-start | bytes 196616 | tf_op jit(solution)/shard_map/ppermute | solution.py:188
  95.0 0.8 collective-permute-start.8
  95.9 0.0 collective-permute-done.10
  95.9 5.5 %collective-permute-done.9 = bf16[32,1024]{1,0:T(8,128)(2,1)S(1)} collective-permute-done((bf16[32,1024]{1,0:T(8,128)(2,1)S(1)}, bf16[32,1024]{1,0:T(8,128)(2,1)S(1)}, u32[]{:S(2)}, u32[]{:S(2)}) %collective-permute-start.9) | collective-permute-done | bytes 65568 | tf_op jit(solution)/shard_map/ppermute | solution.py:188
  101.3 0.0 collective-permute-done.8
  101.3 0.0 copy-done.1
  101.3 1.6 %multiply_add_fusion = (bf16[32,1024]{1,0:T(8,128)(2,1)S(1)}, f32[32,1024]{1,0:T(8,128)}) fusion(f32[32,1024]{1,0:T(8,128)S(1)} %copy-done.1, bf16[32,1024]{1,0:T(8,128)(2,1)S(1)} %collective-permute-done.10, bf16[32,1024]{1,0:T(8,128)(2,1)S(1)} %collective-permute-done.9, bf16[32,1024]{1,0:T(8,128)(2,1)S(1)} %collective-permute-done.8, ...), kind=kLoop, calls=%fused_computation.16 | loop fusion | flops 458752 | bytes 655364 | tf_op jit(solution)/shard_map/add | solution.py:257
  102.9 0.0 all-to-all-done.2.in_ref
  102.9 1.0 shard_map.133
  103.9 11.9 %all_to_all.21 = bf16[8,32,1024]{2,1,0:T(8,128)(2,1)S(1)} all-to-all(bf16[8,32,1024]{2,1,0:T(8,128)(2,1)S(1)} %broadcast_in_dim.2), channel_id=1, replica_groups={{0,2,4,6,8,10,12,14},{1,3,5,7,9,11,13,15},{16,18,20,22,24,26,28,30},{17..., dimensions={0} | all-to-all | bytes 1048576 | tf_op jit(solution)/shard_map/all_to_all | solution.py:262
  115.9 4.0 %collective-permute-start.11 = (bf16[8,32,1024]{2,1,0:T(8,128)(2,1)S(1)}, bf16[8,32,1024]{2,1,0:T(8,128)(2,1)S(1)}, u32[]{:S(2)}, u32[]{:S(2)}) collective-permute-start(bf16[8,32,1024]{2,1,0:T(8,128)(2,1)S(1)} %all_to_all.21), channel_id=1, source_target_pairs={{0,1},{1,0},{2,3},{3,2},{4,5},{5,4},{6,7},{7,6},{8,9},{9,8},{10,11... | collective-permute-start | bytes 1572872 | tf_op jit(solution)/shard_map/ppermute | solution.py:188
  119.9 1.5 %collective-permute-done.11 = bf16[8,32,1024]{2,1,0:T(8,128)(2,1)S(1)} collective-permute-done((bf16[8,32,1024]{2,1,0:T(8,128)(2,1)S(1)}, bf16[8,32,1024]{2,1,0:T(8,128)(2,1)S(1)}, u32[]{:S(2)}, u32[]{:S(2)}) %collective-permute-start.11) | collective-permute-done | bytes 524320 | tf_op jit(solution)/shard_map/ppermute | solution.py:188
  121.4 0.1 select_bitcast_fusion.1
  121.5 1.1 pad_maximum_fusion
  (2 shorter events, 0.1 us)
Async XLA Ops:
  43.0 14.9 %all-to-all-start.1 = ((bf16[16,32,128]{2,1,0:T(8,128)(2,1)}), bf16[16,32,128]{2,1,0:T(8,128)(2,1)S(1)}, u32[]{:S(2)}, u32[]{:S(2)}) async-start(bf16[16,32,128]{2,1,0:T(8,128)(2,1)} %get-tuple-element.16), calls=%async_computation.1 | async-start | bytes 262144 | tf_op jit(solution)/shard_map/all_to_all | solution.py:229
  48.8 9.0 %copy-start = (bf16[2,64,1024]{2,1,0:T(8,128)(2,1)S(1)}, bf16[2,64,1024]{2,1,0:T(8,128)(2,1)}, u32[]{:S(2)}) copy-start(bf16[2,64,1024]{2,1,0:T(8,128)(2,1)} %param.12) | copy-start | bytes 786436
  58.2 4.0 %collective-permute-start = (bf16[2,4,32,1024]{3,2,1,0:T(8,128)(2,1)S(1)}, bf16[2,4,32,1024]{3,2,1,0:T(8,128)(2,1)S(1)}, u32[]{:S(2)}, u32[]{:S(2)}) collective-permute-start(bf16[2,4,32,1024]{3,2,1,0:T(8,128)(2,1)S(1)} %shard_map.132), channel_id=1, source_target_pairs={{0,1},{1,0},{2,3},{3,2},{4,5},{5,4},{6,7},{7,6},{8,9},{9,8},{10,11... | collective-permute-start | bytes 1572872 | tf_op jit(solution)/shard_map/ppermute | solution.py:188
  62.3 8.0 %collective-permute-start.1 = (bf16[4,32,1024]{2,1,0:T(8,128)(2,1)S(1)}, bf16[4,32,1024]{2,1,0:T(8,128)(2,1)S(1)}, u32[]{:S(2)}, u32[]{:S(2)}) collective-permute-start(bf16[4,32,1024]{2,1,0:T(8,128)(2,1)S(1)} %fusion), channel_id=1, source_target_pairs={{0,2},{1,3},{2,0},{3,1},{4,6},{5,7},{6,4},{7,5},{8,10},{9,11},{10,... | collective-permute-start | bytes 786440 | tf_op jit(solution)/shard_map/ppermute | solution.py:188
  62.8 40.1 %all-to-all-start.2 = ((bf16[16,160,128]{2,1,0:T(8,128)(2,1)}), bf16[16,160,128]{2,1,0:T(8,128)(2,1)S(1)}, u32[]{:S(2)}, u32[]{:S(2)}) async-start(bf16[16,160,128]{2,1,0:T(8,128)(2,1)} %shard_map.130), calls=%async_computation.2 | async-start | bytes 1310720 | tf_op jit(solution)/shard_map/all_to_all | solution.py:248
  70.4 3.7 %collective-permute-start.2 = (bf16[32,1024]{1,0:T(8,128)(2,1)S(1)}, bf16[32,1024]{1,0:T(8,128)(2,1)S(1)}, u32[]{:S(2)}, u32[]{:S(2)}) collective-permute-start(bf16[32,1024]{1,0:T(8,128)(2,1)S(1)} %get-tuple-element.29), channel_id=1, source_target_pairs={{0,4},{1,5},{2,6},{3,7},{4,0},{5,1},{6,2},{7,3},{8,12},{9,13},{10,... | collective-permute-start | bytes 196616 | tf_op jit(solution)/shard_map/ppermute | solution.py:188
  71.6 4.6 %collective-permute-start.4 = (bf16[32,1024]{1,0:T(8,128)(2,1)S(1)}, bf16[32,1024]{1,0:T(8,128)(2,1)S(1)}, u32[]{:S(2)}, u32[]{:S(2)}) collective-permute-start(bf16[32,1024]{1,0:T(8,128)(2,1)S(1)} %get-tuple-element.30), channel_id=1, source_target_pairs={{0,12},{1,13},{2,14},{3,15},{4,8},{5,9},{6,10},{7,11},{8,4},{9,5},... | collective-permute-start | bytes 196616 | tf_op jit(solution)/shard_map/ppermute | solution.py:188
  73.5 4.9 %collective-permute-start.3 = (bf16[32,1024]{1,0:T(8,128)(2,1)S(1)}, bf16[32,1024]{1,0:T(8,128)(2,1)S(1)}, u32[]{:S(2)}, u32[]{:S(2)}) collective-permute-start(bf16[32,1024]{1,0:T(8,128)(2,1)S(1)} %get-tuple-element.31), channel_id=1, source_target_pairs={{0,8},{1,9},{2,10},{3,11},{4,12},{5,13},{6,14},{7,15},{8,0},{9,1},... | collective-permute-start | bytes 196616 | tf_op jit(solution)/shard_map/ppermute | solution.py:188
  78.4 22.9 %copy-start.1 = (f32[32,1024]{1,0:T(8,128)S(1)}, f32[32,1024]{1,0:T(8,128)}, u32[]{:S(2)}) copy-start(f32[32,1024]{1,0:T(8,128)} %param.14) | copy-start | bytes 393220
  78.5 10.7 %collective-permute-start.7 = (bf16[32,1024]{1,0:T(8,128)(2,1)S(1)}, bf16[32,1024]{1,0:T(8,128)(2,1)S(1)}, u32[]{:S(2)}, u32[]{:S(2)}) collective-permute-start(bf16[32,1024]{1,0:T(8,128)(2,1)S(1)} %fusion.7), channel_id=1, source_target_pairs={{0,144},{16,128},{32,176},{48,160},{64,208},{80,192},{96,240},{112... | collective-permute-start | bytes 196616 | tf_op jit(solution)/shard_map/ppermute | solution.py:188
  82.3 6.8 %collective-permute-start.6 = (bf16[32,1024]{1,0:T(8,128)(2,1)S(1)}, bf16[32,1024]{1,0:T(8,128)(2,1)S(1)}, u32[]{:S(2)}, u32[]{:S(2)}) collective-permute-start(bf16[32,1024]{1,0:T(8,128)(2,1)S(1)} %fusion.7), channel_id=1, source_target_pairs={{0,128},{16,144},{32,160},{48,176},{64,192},{80,208},{96,224},{112... | collective-permute-start | bytes 196616 | tf_op jit(solution)/shard_map/ppermute | solution.py:188
  82.6 6.5 %collective-permute-start.5 = (bf16[32,1024]{1,0:T(8,128)(2,1)S(1)}, bf16[32,1024]{1,0:T(8,128)(2,1)S(1)}, u32[]{:S(2)}, u32[]{:S(2)}) collective-permute-start(bf16[32,1024]{1,0:T(8,128)(2,1)S(1)} %fusion.7), channel_id=1, source_target_pairs={{0,16},{16,0},{32,48},{48,32},{64,80},{80,64},{96,112},{112,96},{1... | collective-permute-start | bytes 196616 | tf_op jit(solution)/shard_map/ppermute | solution.py:188
  89.2 6.7 %collective-permute-start.10 = (bf16[32,1024]{1,0:T(8,128)(2,1)S(1)}, bf16[32,1024]{1,0:T(8,128)(2,1)S(1)}, u32[]{:S(2)}, u32[]{:S(2)}) collective-permute-start(bf16[32,1024]{1,0:T(8,128)(2,1)S(1)} %add_convert_fusion.1), channel_id=1, source_target_pairs={{0,96},{16,112},{32,64},{48,80},{64,32},{80,48},{96,0},{112,16},{1... | collective-permute-start | bytes 196616 | tf_op jit(solution)/shard_map/ppermute | solution.py:188
  93.7 7.7 %collective-permute-start.9 = (bf16[32,1024]{1,0:T(8,128)(2,1)S(1)}, bf16[32,1024]{1,0:T(8,128)(2,1)S(1)}, u32[]{:S(2)}, u32[]{:S(2)}) collective-permute-start(bf16[32,1024]{1,0:T(8,128)(2,1)S(1)} %add_convert_fusion.1), channel_id=1, source_target_pairs={{0,64},{16,80},{32,96},{48,112},{64,0},{80,16},{96,32},{112,48},{1... | collective-permute-start | bytes 196616 | tf_op jit(solution)/shard_map/ppermute | solution.py:188
  95.0 6.3 %collective-permute-start.8 = (bf16[32,1024]{1,0:T(8,128)(2,1)S(1)}, bf16[32,1024]{1,0:T(8,128)(2,1)S(1)}, u32[]{:S(2)}, u32[]{:S(2)}) collective-permute-start(bf16[32,1024]{1,0:T(8,128)(2,1)S(1)} %add_convert_fusion.1), channel_id=1, source_target_pairs={{0,32},{16,48},{32,0},{48,16},{64,96},{80,112},{96,64},{112,80},{1... | collective-permute-start | bytes 196616 | tf_op jit(solution)/shard_map/ppermute | solution.py:188
  115.9 5.5 %collective-permute-start.11 = (bf16[8,32,1024]{2,1,0:T(8,128)(2,1)S(1)}, bf16[8,32,1024]{2,1,0:T(8,128)(2,1)S(1)}, u32[]{:S(2)}, u32[]{:S(2)}) collective-permute-start(bf16[8,32,1024]{2,1,0:T(8,128)(2,1)S(1)} %all_to_all.21), channel_id=1, source_target_pairs={{0,1},{1,0},{2,3},{3,2},{4,5},{5,4},{6,7},{7,6},{8,9},{9,8},{10,11... | collective-permute-start | bytes 1572872 | tf_op jit(solution)/shard_map/ppermute | solution.py:188

commit v4 on v3

--- a/solution.py
+++ b/solution.py
@@ -147,15 +147,19 @@
         out_ref[b, 0:HALF, :], out_ref[b + 1, 0:HALF, :] = fold(grad_q[:, i : i + PAIR])
 
 
-def weight_kernel(place_ref, att_ref, up_ref, out_ref, att_t):
+def weight_kernel(place_ref, att_ref, other_att_ref, up_ref, other_up_ref, *refs):
+    *out_refs, att_t = refs
     for h in range(HEADS):
-        piece = unfold(att_ref[h], att_ref[HEADS + h])
-        att_t[2 * h] = piece[:HALF]
-        att_t[2 * h + 1] = piece[HALF:]
+        mine = unfold(att_ref[h], att_ref[HEADS + h])
+        other = unfold(other_att_ref[h], other_att_ref[HEADS + h])
+        for half in range(2):
+            rows = slice(half * HALF, (half + 1) * HALF)
+            att_t[2 * h + half] = jnp.concatenate([mine[rows], other[rows]], axis=1)
     place = place_ref[0]
-    rows = [att_t[place ^ (4 * dx + 2 * dy)] for dy in range(2) for dx in range(HEADS // 2)]
-    part = dot(jnp.concatenate(rows, axis=0), up_ref[...], (1, 0))
-    out_ref[...] = part.astype(BF).reshape(out_ref.shape)
+    up = jnp.concatenate([up_ref[...], other_up_ref[...]], axis=0)
+    for dx, out_ref in enumerate(out_refs):
+        rows = jnp.concatenate([att_t[place ^ (4 * dx + 2 * dy)] for dy in range(2)], axis=0)
+        out_ref[...] = dot(rows, up, (1, 0)).astype(BF).reshape(out_ref.shape)
 
 
 def unpack_kernel(in_ref, gq_ref, gk_ref, gv_ref):
@@ -195,9 +199,15 @@
     return total
 
 
-def quad_sum(x, a, b):
+def joined(x, *bits):
     x = x.astype(BF)
-    return plus(x, pairwise(x, "lon", a)) + plus(pairwise(x, "lon", b), pairwise(x, "lon", a ^ b))
+    one, two, three = (pairwise(x, "lon", bit) for bit in bits)
+    return plus(x, one) + plus(two, three)
+
+
+def paired(x, bit):
+    x = x.astype(BF)
+    return plus(x, pairwise(x, "lon", bit))
 
 
 def on_device(queries, keys, values, upstream, out_weight, average, nbr_lon, nbr_lat, counts):
@@ -205,6 +215,7 @@
     lats = lax.axis_size("lat")
     same_core = [[c + 2 * i for i in range(lats // 2)] for c in range(2)]
     up = upstream.reshape(CELLS, D)
+    other_up = pairwise(up, "lat", 1)
     slabs = call(
         pack_kernel,
         shape(lonb, BLOCK + CELLS + LISTS, PAIR),
@@ -230,39 +241,38 @@
     grads = call(backward_kernel, shape(lonb, HALF + CELLS, PAIR), slabs, stats)
     att, grads = lax.optimization_barrier((att, grads))
     rows = HD // lats
-    half = shape(2, lats // 4, rows, D)
+    quarters = lats // 4
     place = lax.axis_index("lat")
-    send, keep = (
-        call(
-            weight_kernel,
-            half,
-            (place ^ core).reshape(1),
-            att,
-            up,
-            scratch=[pltpu.VMEM((2 * HEADS, HALF, CELLS), BF)],
-            scalars=1,
-            vmem=SMALL_BYTES,
-        )
-        for core in (1, 0)
+    parts = call(
+        weight_kernel,
+        [shape(2, rows, D)] * quarters,
+        place.reshape(1),
+        att,
+        pairwise(att, "lat", 1),
+        up,
+        other_up,
+        scratch=[pltpu.VMEM((2 * HEADS, HALF, 2 * CELLS), BF)],
+        scalars=1,
+        vmem=SMALL_BYTES,
     )
     grads = lax.all_to_all(grads, "lon", 0, 0, tiled=True)
-    came = pairwise(send, "lat", 1)
-    by_y = pairwise(plus(keep[1], came[1]).astype(BF), "lat", 2)
-    by_x = [plus(keep[0, i], came[0, i], by_y[i]) for i in range(lats // 4)]
-    by_x = by_x[:1] + [pairwise(by_x[i].astype(BF), "lat", 4 * i) for i in range(1, lats // 4)]
-    total = quad_sum(plus(*by_x), 1, 8)
-    total = quad_sum(total, 2, 4)
+    parts = [parts[0]] + [pairwise(parts[i], "lat", 4 * i) for i in range(1, quarters)]
+    near, far = (plus(*(part[i] for part in parts)).astype(BF) for i in range(2))
+    both = [(i, j) for i in range(lonb) for j in range(lats)]
+    across = lax.ppermute(far, ("lon", "lat"), [(i * lats + j, (i ^ 8) * lats + (j ^ 2)) for i, j in both])
+    total = plus(near, pairwise(near, "lon", 8)) + plus(pairwise(far, "lat", 2), across)
+    total = paired(joined(total, 1, 2, 3), 6)
     own_weight = lax.dynamic_slice_in_dim(out_weight, place * rows, rows, 0).astype(F32)
     updated = own_weight - learn_rate * total
     averaged = decay_rate * average + (1.0 - decay_rate) * updated
-    cell_grads = shape(CELLS, HD)
-    gq, gk, gv = call(unpack_kernel, (cell_grads, cell_grads, cell_grads), grads, vmem=SMALL_BYTES)
-    averaged, gq, gk, gv = lax.optimization_barrier((averaged, gq, gk, gv))
+    averaged, grads = lax.optimization_barrier((averaged, grads))
     copies = jnp.broadcast_to(averaged.astype(BF)[None], (lats // 2, rows, D))
     mine = lax.all_to_all(copies, "lat", 0, 0, axis_index_groups=same_core, tiled=True)
     other = pairwise(mine, "lat", 1)
     first = place % 2 == 0
     next_weights = jnp.stack([jnp.where(first, mine, other), jnp.where(first, other, mine)], axis=1).reshape(HD, D)
+    cell_grads = shape(CELLS, HD)
+    gq, gk, gv = call(unpack_kernel, (cell_grads, cell_grads, cell_grads), grads, vmem=SMALL_BYTES)
     own = (ROWS, BLOCK, HD)
     return (gq.reshape(own), gk.reshape(own), gv.reshape(own), updated, next_weights)
 

time: 123 us -> 121 us (0.984)
  starting transfers between devices: 34.9 us -> 33.3 us
    ppermute x12, starting transfers between devices: 21.6 us -> 19.1 us  [pairwise(): lax.ppermute(x, axis, [(i, i ^ bit) for i in range(lax.axis_size(axis))])]
    ppermute x0 -> x1, waiting for transfers between devices: none -> 1.53 us  [on_device(): lax.ppermute(far, ('lon', 'lat'), [(i * lats + j, (i ^ 8) * lats + (j ^ 2...]
    all_to_all x1, waiting for transfers between devices: 1.41 us -> 0.08 us  [on_device(): att = lax.all_to_all(att, 'lon', 0, 0, tiled=True)]
    pallas_call x6 -> x5, Pallas kernels: 17.2 us -> 17 us  [call(): pl.pallas_call(kernel, out_shape=outs, in_specs=on_chip, scratch_shapes=s...]
  transfers between devices with their start and end apart: 14 -> 15, of which waited for: 7 -> 10; matrix products, arithmetic and copies ran while one was open for 1% -> 1% of each run, Pallas kernels for 6% -> 7%
where the time goes in v4:
time: 121 us; the launch traced here: 120 us
  blocking collectives  45.4 us (38%)
  starting transfers between devices  33.3 us (28%)
  waiting for transfers between devices  20.7 us (17%)
  Pallas kernels  17 us (14%)
  other arithmetic  2.82 us (2%)
    all_to_all x1, blocking collectives, on_device(): slabs = lax.all_to_all(slabs, 'lon', 0, 0, tiled=True)  34.5 us
    ppermute x12, starting transfers between devices, pairwise(): lax.ppermute(x, axis, [(i, i ^ bit) for i in range(lax.axis_size(axis))])  19.1 us
    ppermute x12, waiting for transfers between devices, pairwise(): lax.ppermute(x, axis, [(i, i ^ bit) for i in range(lax.axis_size(axis))])  19 us
    pallas_call x5, Pallas kernels, call(): pl.pallas_call(kernel, out_shape=outs, in_specs=on_chip, scratch_shapes=s...  17 us
    all_to_all x1, blocking collectives, on_device(): lax.all_to_all(copies, 'lat', 0, 0, axis_index_groups=same_core, tiled=True)  10.9 us
    all_to_all x1, starting transfers between devices, on_device(): grads = lax.all_to_all(grads, 'lon', 0, 0, tiled=True)  7.27 us
    all_to_all x1, starting transfers between devices, on_device(): att = lax.all_to_all(att, 'lon', 0, 0, tiled=True)  5.96 us
  transfers between devices with their start and end apart: 15, of which 10 were waited for; matrix products, arithmetic and copies ran while one was open for 1% of the time, Pallas kernels for 7%

profile of v4, /device:TPU:1, one launch (start us, length us, event | category | flops | bytes accessed | tf_op | source)
XLA Modules:
  0.0 120.0 jit_solution(7286380482633183046)
XLA Ops:
  0.6 3.0 %shard_map.128 = bf16[16,208,128]{2,1,0:T(8,128)(2,1)} custom-call(s32[2,1,8]{2,1,0:T(1,128)} %lon_ref.1, s32[2,1,8]{2,1,0:T(1,128)} %lat_ref.1, s32[2]{0:T(128)} %bitcast.27, bf16[128,512]{1,0:T(8,128)(2,1)} %bitcast.24, bf16[128,512]{1,0:T(8,128)(2,1)} %bitcast.25, bf16[128,512]{1,0:T(8,128)(2,1)} %bitcast.26, bf16[128,1024]{1,0:T(8,128)(2,1)} %bitcast.20, ...), custom_call_target="tpu_custom_call" | custom-call | tf_op jit(solution)/shard_map/pallas_call | solution.py:178
  3.6 34.5 %all_to_all.20.in_ref = bf16[16,208,128]{2,1,0:T(8,128)(2,1)} all-to-all(bf16[16,208,128]{2,1,0:T(8,128)(2,1)} %shard_map.128), channel_id=1, replica_groups=mesh['lon'=16,'lat'=16] {'lon'}, dimensions={0} | all-to-all | bytes 1703936 | tf_op jit(solution)/shard_map/all_to_all | solution.py:232
  38.1 4.9 %shard_map.129 = (bf16[16,32,128]{2,1,0:T(8,128)(2,1)}, f32[8,1024]{1,0:T(8,128)}) custom-call(bf16[16,208,128]{2,1,0:T(8,128)(2,1)} %all_to_all.20.in_ref), custom_call_target="tpu_custom_call" | custom-call | tf_op jit(solution)/shard_map/pallas_call | solution.py:178
  43.0 0.0 copy-start
  43.0 6.0 %all-to-all-start.1 = ((bf16[16,32,128]{2,1,0:T(8,128)(2,1)}), bf16[16,32,128]{2,1,0:T(8,128)(2,1)S(1)}, u32[]{:S(2)}, u32[]{:S(2)}) async-start(bf16[16,32,128]{2,1,0:T(8,128)(2,1)} %get-tuple-element.18), calls=%async_computation.1 | async-start | bytes 262144 | tf_op jit(solution)/shard_map/all_to_all | solution.py:240
  49.0 0.0 copy-done
  49.0 1.4 %collective-permute-start.1 = (bf16[128,1024]{1,0:T(8,128)(2,1)S(1)}, bf16[128,1024]{1,0:T(8,128)(2,1)S(1)}, u32[]{:S(2)}, u32[]{:S(2)}) collective-permute-start(bf16[128,1024]{1,0:T(8,128)(2,1)S(1)} %bitcast.21), channel_id=1, source_target_pairs={{0,1},{1,0},{2,3},{3,2},{4,5},{5,4},{6,7},{7,6},{8,9},{9,8},{10,11... | collective-permute-start | bytes 786440 | tf_op jit(solution)/shard_map/ppermute | solution.py:192
  50.4 7.6 %shard_map.130 = bf16[16,160,128]{2,1,0:T(8,128)(2,1)} custom-call(bf16[16,208,128]{2,1,0:T(8,128)(2,1)} %all_to_all.20.in_ref, f32[8,1024]{1,0:T(8,128)} %get-tuple-element.19.stat_ref), custom_call_target="tpu_custom_call" | custom-call | tf_op jit(solution)/shard_map/pallas_call | solution.py:178
  57.9 0.1 all-to-all-done.1.att_ref
  58.0 2.3 %collective-permute-start = (bf16[16,32,128]{2,1,0:T(8,128)(2,1)S(1)}, bf16[16,32,128]{2,1,0:T(8,128)(2,1)S(1)}, u32[]{:S(2)}, u32[]{:S(2)}) collective-permute-start(bf16[16,32,128]{2,1,0:T(8,128)(2,1)S(1)} %all-to-all-done.1.att_ref), channel_id=1, source_target_pairs={{0,1},{1,0},{2,3},{3,2},{4,5},{5,4},{6,7},{7,6},{8,9},{9,8},{10,11... | collective-permute-start | bytes 393224 | tf_op jit(solution)/shard_map/ppermute | solution.py:192
  60.3 0.0 collective-permute-done.1.other_up_ref
  60.3 1.0 collective-permute-done.other_att_ref
  61.3 0.6 shard_map.131
  61.9 1.3 %collective-permute-start.2 = (bf16[2,32,1024]{2,1,0:T(8,128)(2,1)S(1)}, bf16[2,32,1024]{2,1,0:T(8,128)(2,1)S(1)}, u32[]{:S(2)}, u32[]{:S(2)}) collective-permute-start(bf16[2,32,1024]{2,1,0:T(8,128)(2,1)S(1)} %get-tuple-element.22), channel_id=1, source_target_pairs={{0,4},{1,5},{2,6},{3,7},{4,0},{5,1},{6,2},{7,3},{8,12},{9,13},{10,... | collective-permute-start | bytes 393224 | tf_op jit(solution)/shard_map/ppermute | solution.py:192
  63.2 2.4 %collective-permute-start.3 = (bf16[2,32,1024]{2,1,0:T(8,128)(2,1)S(1)}, bf16[2,32,1024]{2,1,0:T(8,128)(2,1)S(1)}, u32[]{:S(2)}, u32[]{:S(2)}) collective-permute-start(bf16[2,32,1024]{2,1,0:T(8,128)(2,1)S(1)} %get-tuple-element.23), channel_id=1, source_target_pairs={{0,8},{1,9},{2,10},{3,11},{4,12},{5,13},{6,14},{7,15},{8,0},{9,1},... | collective-permute-start | bytes 393224 | tf_op jit(solution)/shard_map/ppermute | solution.py:192
  65.7 0.2 collective-permute-start.4
  65.9 7.3 %all-to-all-start.2 = ((bf16[16,160,128]{2,1,0:T(8,128)(2,1)}), bf16[16,160,128]{2,1,0:T(8,128)(2,1)S(1)}, u32[]{:S(2)}, u32[]{:S(2)}) async-start(bf16[16,160,128]{2,1,0:T(8,128)(2,1)} %shard_map.130), calls=%async_computation.2 | async-start | bytes 1310720 | tf_op jit(solution)/shard_map/all_to_all | solution.py:258
  73.1 0.0 collective-permute-done.2
  73.2 0.0 collective-permute-done.3
  73.2 1.1 collective-permute-done.4
  74.3 0.1 fusion
  74.3 2.1 %collective-permute-start.5 = (bf16[32,1024]{1,0:T(8,128)(2,1)S(1)}, bf16[32,1024]{1,0:T(8,128)(2,1)S(1)}, u32[]{:S(2)}, u32[]{:S(2)}) collective-permute-start(bf16[32,1024]{1,0:T(8,128)(2,1)S(1)} %get-tuple-element.35), channel_id=1, source_target_pairs={{0,128},{16,144},{32,160},{48,176},{64,192},{80,208},{96,224},{112... | collective-permute-start | bytes 196616 | tf_op jit(solution)/shard_map/ppermute | solution.py:192
  76.4 1.0 collective-permute-start.7
  77.4 0.0 collective-permute-start.6
  77.4 3.4 %collective-permute-done.5 = bf16[32,1024]{1,0:T(8,128)(2,1)S(1)} collective-permute-done((bf16[32,1024]{1,0:T(8,128)(2,1)S(1)}, bf16[32,1024]{1,0:T(8,128)(2,1)S(1)}, u32[]{:S(2)}, u32[]{:S(2)}) %collective-permute-start.5) | collective-permute-done | bytes 65568 | tf_op jit(solution)/shard_map/ppermute | solution.py:192
  80.8 1.5 %collective-permute-done.7 = bf16[32,1024]{1,0:T(8,128)(2,1)S(1)} collective-permute-done((bf16[32,1024]{1,0:T(8,128)(2,1)S(1)}, bf16[32,1024]{1,0:T(8,128)(2,1)S(1)}, u32[]{:S(2)}, u32[]{:S(2)}) %collective-permute-start.7) | collective-permute-done | bytes 65568 | tf_op jit(solution)/shard_map/ppermute | solution.py:262
  82.3 1.7 %collective-permute-done.6 = bf16[32,1024]{1,0:T(8,128)(2,1)S(1)} collective-permute-done((bf16[32,1024]{1,0:T(8,128)(2,1)S(1)}, bf16[32,1024]{1,0:T(8,128)(2,1)S(1)}, u32[]{:S(2)}, u32[]{:S(2)}) %collective-permute-start.6) | collective-permute-done | bytes 65568 | tf_op jit(solution)/shard_map/ppermute | solution.py:192
  84.0 0.0 copy-start.1
  84.0 3.7 %collective-permute-start.10 = (bf16[32,1024]{1,0:T(8,128)(2,1)S(1)}, bf16[32,1024]{1,0:T(8,128)(2,1)S(1)}, u32[]{:S(2)}, u32[]{:S(2)}) collective-permute-start(bf16[32,1024]{1,0:T(8,128)(2,1)S(1)} %add_convert_fusion.1), channel_id=1, source_target_pairs={{0,48},{16,32},{32,16},{48,0},{64,112},{80,96},{96,80},{112,64},{1... | collective-permute-start | bytes 196616 | tf_op jit(solution)/shard_map/ppermute | solution.py:192
  87.7 0.0 collective-permute-start.9
  87.7 0.4 collective-permute-start.8
  88.1 3.7 %collective-permute-done.10 = bf16[32,1024]{1,0:T(8,128)(2,1)S(1)} collective-permute-done((bf16[32,1024]{1,0:T(8,128)(2,1)S(1)}, bf16[32,1024]{1,0:T(8,128)(2,1)S(1)}, u32[]{:S(2)}, u32[]{:S(2)}) %collective-permute-start.10) | collective-permute-done | bytes 65568 | tf_op jit(solution)/shard_map/ppermute | solution.py:192
  91.8 3.4 %collective-permute-done.9 = bf16[32,1024]{1,0:T(8,128)(2,1)S(1)} collective-permute-done((bf16[32,1024]{1,0:T(8,128)(2,1)S(1)}, bf16[32,1024]{1,0:T(8,128)(2,1)S(1)}, u32[]{:S(2)}, u32[]{:S(2)}) %collective-permute-start.9) | collective-permute-done | bytes 65568 | tf_op jit(solution)/shard_map/ppermute | solution.py:192
  95.2 0.0 collective-permute-done.8
  95.3 1.1 collective-permute-start.11
  96.4 4.2 %collective-permute-done.11 = bf16[32,1024]{1,0:T(8,128)(2,1)S(1)} collective-permute-done((bf16[32,1024]{1,0:T(8,128)(2,1)S(1)}, bf16[32,1024]{1,0:T(8,128)(2,1)S(1)}, u32[]{:S(2)}, u32[]{:S(2)}) %collective-permute-start.11) | collective-permute-done | bytes 65568 | tf_op jit(solution)/shard_map/ppermute | solution.py:192
  100.6 0.0 copy-done.1
  100.6 1.5 %multiply_add_fusion = (bf16[32,1024]{1,0:T(8,128)(2,1)S(1)}, f32[32,1024]{1,0:T(8,128)}) fusion(f32[32,1024]{1,0:T(8,128)S(1)} %copy-done.1, bf16[32,1024]{1,0:T(8,128)(2,1)S(1)} %collective-permute-done.11, bf16[32,1024]{1,0:T(8,128)(2,1)S(1)} %add_convert_fusion, bf16[512,1024]{1,0:T(8,128)(2,1)} %w_ref.1, s32[]{:T(128)S(6)} %select_n.22), kind=kLoop, calls=%fused_computation.3 | loop fusion | flops 327680 | bytes 524292 | tf_op jit(solution)/shard_map/add | solution.py:267
  102.1 0.0 all-to-all-done.2.in_ref
  102.2 10.9 %all_to_all.21 = bf16[8,32,1024]{2,1,0:T(8,128)(2,1)S(1)} all-to-all(bf16[8,32,1024]{2,1,0:T(8,128)(2,1)S(1)} %broadcast_in_dim.2), channel_id=1, replica_groups={{0,2,4,6,8,10,12,14},{1,3,5,7,9,11,13,15},{16,18,20,22,24,26,28,30},{17..., dimensions={0} | all-to-all | bytes 1048576 | tf_op jit(solution)/shard_map/all_to_all | solution.py:270
  113.1 4.2 %collective-permute-start.12 = (bf16[8,32,1024]{2,1,0:T(8,128)(2,1)S(1)}, bf16[8,32,1024]{2,1,0:T(8,128)(2,1)S(1)}, u32[]{:S(2)}, u32[]{:S(2)}) collective-permute-start(bf16[8,32,1024]{2,1,0:T(8,128)(2,1)S(1)} %all_to_all.21), channel_id=1, source_target_pairs={{0,1},{1,0},{2,3},{3,2},{4,5},{5,4},{6,7},{7,6},{8,9},{9,8},{10,11... | collective-permute-start | bytes 1572872 | tf_op jit(solution)/shard_map/ppermute | solution.py:192
  117.4 1.0 shard_map.132
  118.3 0.6 collective-permute-done.12
  118.9 0.1 select_bitcast_fusion.1
  119.0 1.1 pad_maximum_fusion
  (3 shorter events, 0.1 us)
Async XLA Ops:
  43.0 6.0 %copy-start = (bf16[2,64,1024]{2,1,0:T(8,128)(2,1)S(1)}, bf16[2,64,1024]{2,1,0:T(8,128)(2,1)}, u32[]{:S(2)}) copy-start(bf16[2,64,1024]{2,1,0:T(8,128)(2,1)} %param.12) | copy-start | bytes 786436
  43.0 15.0 %all-to-all-start.1 = ((bf16[16,32,128]{2,1,0:T(8,128)(2,1)}), bf16[16,32,128]{2,1,0:T(8,128)(2,1)S(1)}, u32[]{:S(2)}, u32[]{:S(2)}) async-start(bf16[16,32,128]{2,1,0:T(8,128)(2,1)} %get-tuple-element.18), calls=%async_computation.1 | async-start | bytes 262144 | tf_op jit(solution)/shard_map/all_to_all | solution.py:240
  49.0 11.4 %collective-permute-start.1 = (bf16[128,1024]{1,0:T(8,128)(2,1)S(1)}, bf16[128,1024]{1,0:T(8,128)(2,1)S(1)}, u32[]{:S(2)}, u32[]{:S(2)}) collective-permute-start(bf16[128,1024]{1,0:T(8,128)(2,1)S(1)} %bitcast.21), channel_id=1, source_target_pairs={{0,1},{1,0},{2,3},{3,2},{4,5},{5,4},{6,7},{7,6},{8,9},{9,8},{10,11... | collective-permute-start | bytes 786440 | tf_op jit(solution)/shard_map/ppermute | solution.py:192
  58.0 3.3 %collective-permute-start = (bf16[16,32,128]{2,1,0:T(8,128)(2,1)S(1)}, bf16[16,32,128]{2,1,0:T(8,128)(2,1)S(1)}, u32[]{:S(2)}, u32[]{:S(2)}) collective-permute-start(bf16[16,32,128]{2,1,0:T(8,128)(2,1)S(1)} %all-to-all-done.1.att_ref), channel_id=1, source_target_pairs={{0,1},{1,0},{2,3},{3,2},{4,5},{5,4},{6,7},{7,6},{8,9},{9,8},{10,11... | collective-permute-start | bytes 393224 | tf_op jit(solution)/shard_map/ppermute | solution.py:192
  61.9 11.2 %collective-permute-start.2 = (bf16[2,32,1024]{2,1,0:T(8,128)(2,1)S(1)}, bf16[2,32,1024]{2,1,0:T(8,128)(2,1)S(1)}, u32[]{:S(2)}, u32[]{:S(2)}) collective-permute-start(bf16[2,32,1024]{2,1,0:T(8,128)(2,1)S(1)} %get-tuple-element.22), channel_id=1, source_target_pairs={{0,4},{1,5},{2,6},{3,7},{4,0},{5,1},{6,2},{7,3},{8,12},{9,13},{10,... | collective-permute-start | bytes 393224 | tf_op jit(solution)/shard_map/ppermute | solution.py:192
  63.2 9.9 %collective-permute-start.3 = (bf16[2,32,1024]{2,1,0:T(8,128)(2,1)S(1)}, bf16[2,32,1024]{2,1,0:T(8,128)(2,1)S(1)}, u32[]{:S(2)}, u32[]{:S(2)}) collective-permute-start(bf16[2,32,1024]{2,1,0:T(8,128)(2,1)S(1)} %get-tuple-element.23), channel_id=1, source_target_pairs={{0,8},{1,9},{2,10},{3,11},{4,12},{5,13},{6,14},{7,15},{8,0},{9,1},... | collective-permute-start | bytes 393224 | tf_op jit(solution)/shard_map/ppermute | solution.py:192
  65.7 8.6 %collective-permute-start.4 = (bf16[2,32,1024]{2,1,0:T(8,128)(2,1)S(1)}, bf16[2,32,1024]{2,1,0:T(8,128)(2,1)S(1)}, u32[]{:S(2)}, u32[]{:S(2)}) collective-permute-start(bf16[2,32,1024]{2,1,0:T(8,128)(2,1)S(1)} %get-tuple-element.24), channel_id=1, source_target_pairs={{0,12},{1,13},{2,14},{3,15},{4,8},{5,9},{6,10},{7,11},{8,4},{9,5},... | collective-permute-start | bytes 393224 | tf_op jit(solution)/shard_map/ppermute | solution.py:192
  65.9 36.2 %all-to-all-start.2 = ((bf16[16,160,128]{2,1,0:T(8,128)(2,1)}), bf16[16,160,128]{2,1,0:T(8,128)(2,1)S(1)}, u32[]{:S(2)}, u32[]{:S(2)}) async-start(bf16[16,160,128]{2,1,0:T(8,128)(2,1)} %shard_map.130), calls=%async_computation.2 | async-start | bytes 1310720 | tf_op jit(solution)/shard_map/all_to_all | solution.py:258
  74.3 6.5 %collective-permute-start.5 = (bf16[32,1024]{1,0:T(8,128)(2,1)S(1)}, bf16[32,1024]{1,0:T(8,128)(2,1)S(1)}, u32[]{:S(2)}, u32[]{:S(2)}) collective-permute-start(bf16[32,1024]{1,0:T(8,128)(2,1)S(1)} %get-tuple-element.35), channel_id=1, source_target_pairs={{0,128},{16,144},{32,160},{48,176},{64,192},{80,208},{96,224},{112... | collective-permute-start | bytes 196616 | tf_op jit(solution)/shard_map/ppermute | solution.py:192
  76.4 5.9 %collective-permute-start.7 = (bf16[32,1024]{1,0:T(8,128)(2,1)S(1)}, bf16[32,1024]{1,0:T(8,128)(2,1)S(1)}, u32[]{:S(2)}, u32[]{:S(2)}) collective-permute-start(bf16[32,1024]{1,0:T(8,128)(2,1)S(1)} %get-tuple-element.36), channel_id=1, source_target_pairs={{0,130},{1,131},{2,128},{3,129},{4,134},{5,135},{6,132},{7,133},{8... | collective-permute-start | bytes 196616 | tf_op jit(solution)/shard_map/ppermute | solution.py:262
  77.4 6.6 %collective-permute-start.6 = (bf16[32,1024]{1,0:T(8,128)(2,1)S(1)}, bf16[32,1024]{1,0:T(8,128)(2,1)S(1)}, u32[]{:S(2)}, u32[]{:S(2)}) collective-permute-start(bf16[32,1024]{1,0:T(8,128)(2,1)S(1)} %get-tuple-element.36), channel_id=1, source_target_pairs={{0,2},{1,3},{2,0},{3,1},{4,6},{5,7},{6,4},{7,5},{8,10},{9,11},{10,... | collective-permute-start | bytes 196616 | tf_op jit(solution)/shard_map/ppermute | solution.py:192
  84.0 16.5 %copy-start.1 = (f32[32,1024]{1,0:T(8,128)S(1)}, f32[32,1024]{1,0:T(8,128)}, u32[]{:S(2)}) copy-start(f32[32,1024]{1,0:T(8,128)} %param.14) | copy-start | bytes 393220
  84.0 7.7 %collective-permute-start.10 = (bf16[32,1024]{1,0:T(8,128)(2,1)S(1)}, bf16[32,1024]{1,0:T(8,128)(2,1)S(1)}, u32[]{:S(2)}, u32[]{:S(2)}) collective-permute-start(bf16[32,1024]{1,0:T(8,128)(2,1)S(1)} %add_convert_fusion.1), channel_id=1, source_target_pairs={{0,48},{16,32},{32,16},{48,0},{64,112},{80,96},{96,80},{112,64},{1... | collective-permute-start | bytes 196616 | tf_op jit(solution)/shard_map/ppermute | solution.py:192
  87.7 7.5 %collective-permute-start.9 = (bf16[32,1024]{1,0:T(8,128)(2,1)S(1)}, bf16[32,1024]{1,0:T(8,128)(2,1)S(1)}, u32[]{:S(2)}, u32[]{:S(2)}) collective-permute-start(bf16[32,1024]{1,0:T(8,128)(2,1)S(1)} %add_convert_fusion.1), channel_id=1, source_target_pairs={{0,32},{16,48},{32,0},{48,16},{64,96},{80,112},{96,64},{112,80},{1... | collective-permute-start | bytes 196616 | tf_op jit(solution)/shard_map/ppermute | solution.py:192
  87.7 7.5 %collective-permute-start.8 = (bf16[32,1024]{1,0:T(8,128)(2,1)S(1)}, bf16[32,1024]{1,0:T(8,128)(2,1)S(1)}, u32[]{:S(2)}, u32[]{:S(2)}) collective-permute-start(bf16[32,1024]{1,0:T(8,128)(2,1)S(1)} %add_convert_fusion.1), channel_id=1, source_target_pairs={{0,16},{16,0},{32,48},{48,32},{64,80},{80,64},{96,112},{112,96},{1... | collective-permute-start | bytes 196616 | tf_op jit(solution)/shard_map/ppermute | solution.py:192
  95.3 5.3 %collective-permute-start.11 = (bf16[32,1024]{1,0:T(8,128)(2,1)S(1)}, bf16[32,1024]{1,0:T(8,128)(2,1)S(1)}, u32[]{:S(2)}, u32[]{:S(2)}) collective-permute-start(bf16[32,1024]{1,0:T(8,128)(2,1)S(1)} %add_convert_fusion), channel_id=1, source_target_pairs={{0,96},{16,112},{32,64},{48,80},{64,32},{80,48},{96,0},{112,16},{1... | collective-permute-start | bytes 196616 | tf_op jit(solution)/shard_map/ppermute | solution.py:192
  113.1 5.8 %collective-permute-start.12 = (bf16[8,32,1024]{2,1,0:T(8,128)(2,1)S(1)}, bf16[8,32,1024]{2,1,0:T(8,128)(2,1)S(1)}, u32[]{:S(2)}, u32[]{:S(2)}) collective-permute-start(bf16[8,32,1024]{2,1,0:T(8,128)(2,1)S(1)} %all_to_all.21), channel_id=1, source_target_pairs={{0,1},{1,0},{2,3},{3,2},{4,5},{5,4},{6,7},{7,6},{8,9},{9,8},{10,11... | collective-permute-start | bytes 1572872 | tf_op jit(solution)/shard_map/ppermute | solution.py:192

commit v5 on v4

--- a/solution.py
+++ b/solution.py
@@ -25,6 +25,7 @@
 F32 = jnp.float32
 VMEM_BYTES = 56 * 2**20
 SMALL_BYTES = 24 * 2**20
+MID_BYTES = 40 * 2**20
 SCALE = HEAD**-0.5
 
 
@@ -88,7 +89,7 @@
     x, kv = tiles_of(in_ref)
     keys, cells = score_ref.shape
     k_only = jnp.where(low_lanes(), kv * jnp.asarray(SCALE, BF), jnp.zeros((), BF))
-    v_t = kv.T[HEAD:]
+    v_t = jnp.concatenate([kv.T[HEAD:], jnp.ones((LISTS, keys), BF)], axis=0)
     seen = seen_blocks(in_ref)
     tops = []
     for g in range(0, keys, GROUP):
@@ -97,17 +98,15 @@
         tops += [jnp.max(scores[j : j + BLOCK], axis=0, keepdims=True) for j in range(0, GROUP, BLOCK)]
     top = jnp.max(jnp.where(seen, jnp.concatenate(tops, axis=0), -1e30), axis=0, keepdims=True)
     shift = jnp.where(seen, top, 1e30)
-    att = jnp.zeros((HEAD, cells), F32)
-    total = jnp.zeros((8, cells), F32)
+    att = jnp.zeros((v_t.shape[0], cells), F32)
     for g in range(0, keys, GROUP):
         probs = []
         for j in range(g, g + GROUP, BLOCK):
             prob = jnp.exp(score_ref[j : j + BLOCK, :] - shift[j // BLOCK : j // BLOCK + 1])
-            total = total + jnp.sum(prob.reshape(BLOCK // 8, 8, cells), axis=0)
             probs.append(prob.astype(BF))
         att = att + dot(v_t[:, g : g + GROUP], jnp.concatenate(probs, axis=0), (1, 0))
-    total = jnp.sum(total, axis=0, keepdims=True)
-    att = (att * (1.0 / total)).astype(BF)
+    total = att[HEAD : HEAD + 1]
+    att = (att[:HEAD] * (1.0 / total)).astype(BF)
     delta = jnp.sum(x.T[HEAD:].astype(F32) * att.astype(F32), axis=0, keepdims=True)
     row = lax.broadcasted_iota(jnp.int32, stat_ref.shape, 0)
     stat_ref[...] = jnp.where(row == 0, top + jnp.log(total), delta)
@@ -236,9 +235,10 @@
         (shape(lonb, HALF, PAIR), shape(8, cells, dtype=F32)),
         slabs,
         scratch=[pltpu.VMEM((lonb * CELLS, cells), F32)],
+        vmem=MID_BYTES,
     )
     att = lax.all_to_all(att, "lon", 0, 0, tiled=True)
-    grads = call(backward_kernel, shape(lonb, HALF + CELLS, PAIR), slabs, stats)
+    grads = call(backward_kernel, shape(lonb, HALF + CELLS, PAIR), slabs, stats, vmem=MID_BYTES)
     att, grads = lax.optimization_barrier((att, grads))
     rows = HD // lats
     quarters = lats // 4

time: 121 us -> 118 us (0.975)
  Pallas kernels: 17 us -> 14.4 us
  waiting for transfers between devices: 20.7 us -> 22.3 us
  starting transfers between devices: 33.3 us -> 31.8 us
    pallas_call x5, Pallas kernels: 17 us -> 14.4 us  [call(): pl.pallas_call(kernel, out_shape=outs, in_specs=on_chip, scratch_shapes=s...]
    ppermute x12, starting transfers between devices: 19.1 us -> 17.6 us  [pairwise(): lax.ppermute(x, axis, [(i, i ^ bit) for i in range(lax.axis_size(axis))])]
  transfers between devices with their start and end apart: 15 -> 15, of which waited for: 10 -> 10; matrix products, arithmetic and copies ran while one was open for 1% -> 1% of each run, Pallas kernels for 7% -> 6%
where the time goes in v5:
time: 118 us; the launch traced here: 117 us
  blocking collectives  45.2 us (38%)
  starting transfers between devices  31.8 us (27%)
  waiting for transfers between devices  22.3 us (19%)
  Pallas kernels  14.4 us (12%)
  other arithmetic  2.82 us (2%)
    all_to_all x1, blocking collectives, on_device(): slabs = lax.all_to_all(slabs, 'lon', 0, 0, tiled=True)  34.4 us
    ppermute x12, waiting for transfers between devices, pairwise(): lax.ppermute(x, axis, [(i, i ^ bit) for i in range(lax.axis_size(axis))])  18.3 us
    ppermute x12, starting transfers between devices, pairwise(): lax.ppermute(x, axis, [(i, i ^ bit) for i in range(lax.axis_size(axis))])  17.6 us
    pallas_call x5, Pallas kernels, call(): pl.pallas_call(kernel, out_shape=outs, in_specs=on_chip, scratch_shapes=s...  14.4 us
    all_to_all x1, blocking collectives, on_device(): lax.all_to_all(copies, 'lat', 0, 0, axis_index_groups=same_core, tiled=True)  10.8 us
    all_to_all x1, starting transfers between devices, on_device(): grads = lax.all_to_all(grads, 'lon', 0, 0, tiled=True)  6.14 us
    all_to_all x1, starting transfers between devices, on_device(): att = lax.all_to_all(att, 'lon', 0, 0, tiled=True)  5.98 us
    ppermute x1, waiting for transfers between devices, on_device(): lax.ppermute(far, ('lon', 'lat'), [(i * lats + j, (i ^ 8) * lats + (j ^ 2...  2.73 us
  transfers between devices with their start and end apart: 15, of which 10 were waited for; matrix products, arithmetic and copies ran while one was open for 1% of the time, Pallas kernels for 6%

profile of v5, /device:TPU:1, one launch (start us, length us, event | category | flops | bytes accessed | tf_op | source)
XLA Modules:
  0.0 117.3 jit_solution(9327002740491206014)
XLA Ops:
  0.6 3.0 %shard_map.128 = bf16[16,208,128]{2,1,0:T(8,128)(2,1)} custom-call(s32[2,1,8]{2,1,0:T(1,128)} %lon_ref.1, s32[2,1,8]{2,1,0:T(1,128)} %lat_ref.1, s32[2]{0:T(128)} %bitcast.27, bf16[128,512]{1,0:T(8,128)(2,1)} %bitcast.24, bf16[128,512]{1,0:T(8,128)(2,1)} %bitcast.25, bf16[128,512]{1,0:T(8,128)(2,1)} %bitcast.26, bf16[128,1024]{1,0:T(8,128)(2,1)} %bitcast.20, ...), custom_call_target="tpu_custom_call" | custom-call | tf_op jit(solution)/shard_map/pallas_call | solution.py:177
  3.6 34.4 %all_to_all.20.in_ref = bf16[16,208,128]{2,1,0:T(8,128)(2,1)S(1)} all-to-all(bf16[16,208,128]{2,1,0:T(8,128)(2,1)} %shard_map.128), channel_id=1, replica_groups=mesh['lon'=16,'lat'=16] {'lon'}, dimensions={0} | all-to-all | bytes 1703936 | tf_op jit(solution)/shard_map/all_to_all | solution.py:231
  38.0 3.5 %shard_map.129 = (bf16[16,32,128]{2,1,0:T(8,128)(2,1)}, f32[8,1024]{1,0:T(8,128)S(1)}) custom-call(bf16[16,208,128]{2,1,0:T(8,128)(2,1)S(1)} %all_to_all.20.in_ref), custom_call_target="tpu_custom_call" | custom-call | tf_op jit(solution)/shard_map/pallas_call | solution.py:177
  41.4 0.0 copy-start
  41.4 6.0 %all-to-all-start.1 = ((bf16[16,32,128]{2,1,0:T(8,128)(2,1)}), bf16[16,32,128]{2,1,0:T(8,128)(2,1)S(1)}, u32[]{:S(2)}, u32[]{:S(2)}) async-start(bf16[16,32,128]{2,1,0:T(8,128)(2,1)} %get-tuple-element.18), calls=%async_computation.1 | async-start | bytes 262144 | tf_op jit(solution)/shard_map/all_to_all | solution.py:240
  47.4 0.0 copy-done
  47.4 1.4 %collective-permute-start.1 = (bf16[128,1024]{1,0:T(8,128)(2,1)S(1)}, bf16[128,1024]{1,0:T(8,128)(2,1)S(1)}, u32[]{:S(2)}, u32[]{:S(2)}) collective-permute-start(bf16[128,1024]{1,0:T(8,128)(2,1)S(1)} %bitcast.21), channel_id=1, source_target_pairs={{0,1},{1,0},{2,3},{3,2},{4,5},{5,4},{6,7},{7,6},{8,9},{9,8},{10,11... | collective-permute-start | bytes 786440 | tf_op jit(solution)/shard_map/ppermute | solution.py:191
  48.8 6.4 %shard_map.130 = bf16[16,160,128]{2,1,0:T(8,128)(2,1)} custom-call(bf16[16,208,128]{2,1,0:T(8,128)(2,1)S(1)} %all_to_all.20.in_ref, f32[8,1024]{1,0:T(8,128)S(1)} %get-tuple-element.19.stat_ref), custom_call_target="tpu_custom_call" | custom-call | tf_op jit(solution)/shard_map/pallas_call | solution.py:177
  55.2 1.2 %all-to-all-done.1.att_ref = bf16[16,32,128]{2,1,0:T(8,128)(2,1)S(1)} async-done(((bf16[16,32,128]{2,1,0:T(8,128)(2,1)}), bf16[16,32,128]{2,1,0:T(8,128)(2,1)S(1)}, u32[]{:S(2)}, u32[]{:S(2)}) %all-to-all-start.1) | async-done | bytes 131104 | tf_op jit(solution)/shard_map/all_to_all | solution.py:240
  56.4 2.3 %collective-permute-start = (bf16[16,32,128]{2,1,0:T(8,128)(2,1)S(1)}, bf16[16,32,128]{2,1,0:T(8,128)(2,1)S(1)}, u32[]{:S(2)}, u32[]{:S(2)}) collective-permute-start(bf16[16,32,128]{2,1,0:T(8,128)(2,1)S(1)} %all-to-all-done.1.att_ref), channel_id=1, source_target_pairs={{0,1},{1,0},{2,3},{3,2},{4,5},{5,4},{6,7},{7,6},{8,9},{9,8},{10,11... | collective-permute-start | bytes 393224 | tf_op jit(solution)/shard_map/ppermute | solution.py:191
  58.8 0.0 collective-permute-done.1.other_up_ref
  58.8 1.0 collective-permute-done.other_att_ref
  59.8 0.6 shard_map.131
  60.4 1.3 %collective-permute-start.2 = (bf16[2,32,1024]{2,1,0:T(8,128)(2,1)S(1)}, bf16[2,32,1024]{2,1,0:T(8,128)(2,1)S(1)}, u32[]{:S(2)}, u32[]{:S(2)}) collective-permute-start(bf16[2,32,1024]{2,1,0:T(8,128)(2,1)S(1)} %get-tuple-element.22), channel_id=1, source_target_pairs={{0,4},{1,5},{2,6},{3,7},{4,0},{5,1},{6,2},{7,3},{8,12},{9,13},{10,... | collective-permute-start | bytes 393224 | tf_op jit(solution)/shard_map/ppermute | solution.py:191
  61.7 2.4 %collective-permute-start.3 = (bf16[2,32,1024]{2,1,0:T(8,128)(2,1)S(1)}, bf16[2,32,1024]{2,1,0:T(8,128)(2,1)S(1)}, u32[]{:S(2)}, u32[]{:S(2)}) collective-permute-start(bf16[2,32,1024]{2,1,0:T(8,128)(2,1)S(1)} %get-tuple-element.23), channel_id=1, source_target_pairs={{0,8},{1,9},{2,10},{3,11},{4,12},{5,13},{6,14},{7,15},{8,0},{9,1},... | collective-permute-start | bytes 393224 | tf_op jit(solution)/shard_map/ppermute | solution.py:191
  64.1 0.2 collective-permute-start.4
  64.3 6.1 %all-to-all-start.2 = ((bf16[16,160,128]{2,1,0:T(8,128)(2,1)}), bf16[16,160,128]{2,1,0:T(8,128)(2,1)S(1)}, u32[]{:S(2)}, u32[]{:S(2)}) async-start(bf16[16,160,128]{2,1,0:T(8,128)(2,1)} %shard_map.130), calls=%async_computation.2 | async-start | bytes 1310720 | tf_op jit(solution)/shard_map/all_to_all | solution.py:258
  70.5 0.0 collective-permute-done.2
  70.5 0.0 collective-permute-done.3
  70.5 2.2 %collective-permute-done.4 = bf16[2,32,1024]{2,1,0:T(8,128)(2,1)S(1)} collective-permute-done((bf16[2,32,1024]{2,1,0:T(8,128)(2,1)S(1)}, bf16[2,32,1024]{2,1,0:T(8,128)(2,1)S(1)}, u32[]{:S(2)}, u32[]{:S(2)}) %collective-permute-start.4) | collective-permute-done | bytes 131104 | tf_op jit(solution)/shard_map/ppermute | solution.py:191
  72.7 0.1 fusion
  72.8 0.9 collective-permute-start.5
  73.7 2.1 %collective-permute-start.7 = (bf16[32,1024]{1,0:T(8,128)(2,1)S(1)}, bf16[32,1024]{1,0:T(8,128)(2,1)S(1)}, u32[]{:S(2)}, u32[]{:S(2)}) collective-permute-start(bf16[32,1024]{1,0:T(8,128)(2,1)S(1)} %get-tuple-element.36), channel_id=1, source_target_pairs={{0,130},{1,131},{2,128},{3,129},{4,134},{5,135},{6,132},{7,133},{8... | collective-permute-start | bytes 196616 | tf_op jit(solution)/shard_map/ppermute | solution.py:262
  75.8 0.0 collective-permute-start.6
  75.8 2.5 %collective-permute-done.5 = bf16[32,1024]{1,0:T(8,128)(2,1)S(1)} collective-permute-done((bf16[32,1024]{1,0:T(8,128)(2,1)S(1)}, bf16[32,1024]{1,0:T(8,128)(2,1)S(1)}, u32[]{:S(2)}, u32[]{:S(2)}) %collective-permute-start.5) | collective-permute-done | bytes 65568 | tf_op jit(solution)/shard_map/ppermute | solution.py:191
  78.3 2.7 %collective-permute-done.7 = bf16[32,1024]{1,0:T(8,128)(2,1)S(1)} collective-permute-done((bf16[32,1024]{1,0:T(8,128)(2,1)S(1)}, bf16[32,1024]{1,0:T(8,128)(2,1)S(1)}, u32[]{:S(2)}, u32[]{:S(2)}) %collective-permute-start.7) | collective-permute-done | bytes 65568 | tf_op jit(solution)/shard_map/ppermute | solution.py:262
  81.1 0.5 collective-permute-done.6
  81.6 0.0 copy-start.1
  81.6 3.4 %collective-permute-start.10 = (bf16[32,1024]{1,0:T(8,128)(2,1)S(1)}, bf16[32,1024]{1,0:T(8,128)(2,1)S(1)}, u32[]{:S(2)}, u32[]{:S(2)}) collective-permute-start(bf16[32,1024]{1,0:T(8,128)(2,1)S(1)} %add_convert_fusion.1), channel_id=1, source_target_pairs={{0,48},{16,32},{32,16},{48,0},{64,112},{80,96},{96,80},{112,64},{1... | collective-permute-start | bytes 196616 | tf_op jit(solution)/shard_map/ppermute | solution.py:191
  85.0 0.0 collective-permute-start.9
  85.0 0.4 collective-permute-start.8
  85.4 3.7 %collective-permute-done.10 = bf16[32,1024]{1,0:T(8,128)(2,1)S(1)} collective-permute-done((bf16[32,1024]{1,0:T(8,128)(2,1)S(1)}, bf16[32,1024]{1,0:T(8,128)(2,1)S(1)}, u32[]{:S(2)}, u32[]{:S(2)}) %collective-permute-start.10) | collective-permute-done | bytes 65568 | tf_op jit(solution)/shard_map/ppermute | solution.py:191
  89.1 3.5 %collective-permute-done.9 = bf16[32,1024]{1,0:T(8,128)(2,1)S(1)} collective-permute-done((bf16[32,1024]{1,0:T(8,128)(2,1)S(1)}, bf16[32,1024]{1,0:T(8,128)(2,1)S(1)}, u32[]{:S(2)}, u32[]{:S(2)}) %collective-permute-start.9) | collective-permute-done | bytes 65568 | tf_op jit(solution)/shard_map/ppermute | solution.py:191
  92.6 0.0 collective-permute-done.8
  92.7 1.0 collective-permute-start.11
  93.7 4.3 %collective-permute-done.11 = bf16[32,1024]{1,0:T(8,128)(2,1)S(1)} collective-permute-done((bf16[32,1024]{1,0:T(8,128)(2,1)S(1)}, bf16[32,1024]{1,0:T(8,128)(2,1)S(1)}, u32[]{:S(2)}, u32[]{:S(2)}) %collective-permute-start.11) | collective-permute-done | bytes 65568 | tf_op jit(solution)/shard_map/ppermute | solution.py:191
  98.0 0.0 copy-done.1
  98.0 1.5 %multiply_add_fusion = (bf16[32,1024]{1,0:T(8,128)(2,1)S(1)}, f32[32,1024]{1,0:T(8,128)}) fusion(f32[32,1024]{1,0:T(8,128)S(1)} %copy-done.1, bf16[32,1024]{1,0:T(8,128)(2,1)S(1)} %collective-permute-done.11, bf16[32,1024]{1,0:T(8,128)(2,1)S(1)} %add_convert_fusion, bf16[512,1024]{1,0:T(8,128)(2,1)} %w_ref.1, s32[]{:T(128)S(6)} %select_n.22), kind=kLoop, calls=%fused_computation.3 | loop fusion | flops 327680 | bytes 524292 | tf_op jit(solution)/shard_map/add | solution.py:267
  99.5 0.0 all-to-all-done.2.in_ref
  99.6 10.8 %all_to_all.21 = bf16[8,32,1024]{2,1,0:T(8,128)(2,1)S(1)} all-to-all(bf16[8,32,1024]{2,1,0:T(8,128)(2,1)S(1)} %broadcast_in_dim.2), channel_id=1, replica_groups={{0,2,4,6,8,10,12,14},{1,3,5,7,9,11,13,15},{16,18,20,22,24,26,28,30},{17..., dimensions={0} | all-to-all | bytes 1048576 | tf_op jit(solution)/shard_map/all_to_all | solution.py:270
  110.4 4.2 %collective-permute-start.12 = (bf16[8,32,1024]{2,1,0:T(8,128)(2,1)S(1)}, bf16[8,32,1024]{2,1,0:T(8,128)(2,1)S(1)}, u32[]{:S(2)}, u32[]{:S(2)}) collective-permute-start(bf16[8,32,1024]{2,1,0:T(8,128)(2,1)S(1)} %all_to_all.21), channel_id=1, source_target_pairs={{0,1},{1,0},{2,3},{3,2},{4,5},{5,4},{6,7},{7,6},{8,9},{9,8},{10,11... | collective-permute-start | bytes 1572872 | tf_op jit(solution)/shard_map/ppermute | solution.py:191
  114.7 1.0 shard_map.132
  115.6 0.6 collective-permute-done.12
  116.2 0.1 select_bitcast_fusion.1
  116.3 1.1 pad_maximum_fusion
  (3 shorter events, 0.1 us)
Async XLA Ops:
  41.4 6.0 %copy-start = (bf16[2,64,1024]{2,1,0:T(8,128)(2,1)S(1)}, bf16[2,64,1024]{2,1,0:T(8,128)(2,1)}, u32[]{:S(2)}) copy-start(bf16[2,64,1024]{2,1,0:T(8,128)(2,1)} %param.12) | copy-start | bytes 786436
  41.4 15.0 %all-to-all-start.1 = ((bf16[16,32,128]{2,1,0:T(8,128)(2,1)}), bf16[16,32,128]{2,1,0:T(8,128)(2,1)S(1)}, u32[]{:S(2)}, u32[]{:S(2)}) async-start(bf16[16,32,128]{2,1,0:T(8,128)(2,1)} %get-tuple-element.18), calls=%async_computation.1 | async-start | bytes 262144 | tf_op jit(solution)/shard_map/all_to_all | solution.py:240
  47.4 11.4 %collective-permute-start.1 = (bf16[128,1024]{1,0:T(8,128)(2,1)S(1)}, bf16[128,1024]{1,0:T(8,128)(2,1)S(1)}, u32[]{:S(2)}, u32[]{:S(2)}) collective-permute-start(bf16[128,1024]{1,0:T(8,128)(2,1)S(1)} %bitcast.21), channel_id=1, source_target_pairs={{0,1},{1,0},{2,3},{3,2},{4,5},{5,4},{6,7},{7,6},{8,9},{9,8},{10,11... | collective-permute-start | bytes 786440 | tf_op jit(solution)/shard_map/ppermute | solution.py:191
  56.4 3.3 %collective-permute-start = (bf16[16,32,128]{2,1,0:T(8,128)(2,1)S(1)}, bf16[16,32,128]{2,1,0:T(8,128)(2,1)S(1)}, u32[]{:S(2)}, u32[]{:S(2)}) collective-permute-start(bf16[16,32,128]{2,1,0:T(8,128)(2,1)S(1)} %all-to-all-done.1.att_ref), channel_id=1, source_target_pairs={{0,1},{1,0},{2,3},{3,2},{4,5},{5,4},{6,7},{7,6},{8,9},{9,8},{10,11... | collective-permute-start | bytes 393224 | tf_op jit(solution)/shard_map/ppermute | solution.py:191
  60.4 10.1 %collective-permute-start.2 = (bf16[2,32,1024]{2,1,0:T(8,128)(2,1)S(1)}, bf16[2,32,1024]{2,1,0:T(8,128)(2,1)S(1)}, u32[]{:S(2)}, u32[]{:S(2)}) collective-permute-start(bf16[2,32,1024]{2,1,0:T(8,128)(2,1)S(1)} %get-tuple-element.22), channel_id=1, source_target_pairs={{0,4},{1,5},{2,6},{3,7},{4,0},{5,1},{6,2},{7,3},{8,12},{9,13},{10,... | collective-permute-start | bytes 393224 | tf_op jit(solution)/shard_map/ppermute | solution.py:191
  61.7 8.8 %collective-permute-start.3 = (bf16[2,32,1024]{2,1,0:T(8,128)(2,1)S(1)}, bf16[2,32,1024]{2,1,0:T(8,128)(2,1)S(1)}, u32[]{:S(2)}, u32[]{:S(2)}) collective-permute-start(bf16[2,32,1024]{2,1,0:T(8,128)(2,1)S(1)} %get-tuple-element.23), channel_id=1, source_target_pairs={{0,8},{1,9},{2,10},{3,11},{4,12},{5,13},{6,14},{7,15},{8,0},{9,1},... | collective-permute-start | bytes 393224 | tf_op jit(solution)/shard_map/ppermute | solution.py:191
  64.1 8.6 %collective-permute-start.4 = (bf16[2,32,1024]{2,1,0:T(8,128)(2,1)S(1)}, bf16[2,32,1024]{2,1,0:T(8,128)(2,1)S(1)}, u32[]{:S(2)}, u32[]{:S(2)}) collective-permute-start(bf16[2,32,1024]{2,1,0:T(8,128)(2,1)S(1)} %get-tuple-element.24), channel_id=1, source_target_pairs={{0,12},{1,13},{2,14},{3,15},{4,8},{5,9},{6,10},{7,11},{8,4},{9,5},... | collective-permute-start | bytes 393224 | tf_op jit(solution)/shard_map/ppermute | solution.py:191
  64.3 35.2 %all-to-all-start.2 = ((bf16[16,160,128]{2,1,0:T(8,128)(2,1)}), bf16[16,160,128]{2,1,0:T(8,128)(2,1)S(1)}, u32[]{:S(2)}, u32[]{:S(2)}) async-start(bf16[16,160,128]{2,1,0:T(8,128)(2,1)} %shard_map.130), calls=%async_computation.2 | async-start | bytes 1310720 | tf_op jit(solution)/shard_map/all_to_all | solution.py:258
  72.8 5.6 %collective-permute-start.5 = (bf16[32,1024]{1,0:T(8,128)(2,1)S(1)}, bf16[32,1024]{1,0:T(8,128)(2,1)S(1)}, u32[]{:S(2)}, u32[]{:S(2)}) collective-permute-start(bf16[32,1024]{1,0:T(8,128)(2,1)S(1)} %get-tuple-element.35), channel_id=1, source_target_pairs={{0,128},{16,144},{32,160},{48,176},{64,192},{80,208},{96,224},{112... | collective-permute-start | bytes 196616 | tf_op jit(solution)/shard_map/ppermute | solution.py:191
  73.7 7.4 %collective-permute-start.7 = (bf16[32,1024]{1,0:T(8,128)(2,1)S(1)}, bf16[32,1024]{1,0:T(8,128)(2,1)S(1)}, u32[]{:S(2)}, u32[]{:S(2)}) collective-permute-start(bf16[32,1024]{1,0:T(8,128)(2,1)S(1)} %get-tuple-element.36), channel_id=1, source_target_pairs={{0,130},{1,131},{2,128},{3,129},{4,134},{5,135},{6,132},{7,133},{8... | collective-permute-start | bytes 196616 | tf_op jit(solution)/shard_map/ppermute | solution.py:262
  75.8 5.7 %collective-permute-start.6 = (bf16[32,1024]{1,0:T(8,128)(2,1)S(1)}, bf16[32,1024]{1,0:T(8,128)(2,1)S(1)}, u32[]{:S(2)}, u32[]{:S(2)}) collective-permute-start(bf16[32,1024]{1,0:T(8,128)(2,1)S(1)} %get-tuple-element.36), channel_id=1, source_target_pairs={{0,2},{1,3},{2,0},{3,1},{4,6},{5,7},{6,4},{7,5},{8,10},{9,11},{10,... | collective-permute-start | bytes 196616 | tf_op jit(solution)/shard_map/ppermute | solution.py:191
  81.6 16.4 %copy-start.1 = (f32[32,1024]{1,0:T(8,128)S(1)}, f32[32,1024]{1,0:T(8,128)}, u32[]{:S(2)}) copy-start(f32[32,1024]{1,0:T(8,128)} %param.14) | copy-start | bytes 393220
  81.6 7.4 %collective-permute-start.10 = (bf16[32,1024]{1,0:T(8,128)(2,1)S(1)}, bf16[32,1024]{1,0:T(8,128)(2,1)S(1)}, u32[]{:S(2)}, u32[]{:S(2)}) collective-permute-start(bf16[32,1024]{1,0:T(8,128)(2,1)S(1)} %add_convert_fusion.1), channel_id=1, source_target_pairs={{0,48},{16,32},{32,16},{48,0},{64,112},{80,96},{96,80},{112,64},{1... | collective-permute-start | bytes 196616 | tf_op jit(solution)/shard_map/ppermute | solution.py:191
  85.0 7.6 %collective-permute-start.9 = (bf16[32,1024]{1,0:T(8,128)(2,1)S(1)}, bf16[32,1024]{1,0:T(8,128)(2,1)S(1)}, u32[]{:S(2)}, u32[]{:S(2)}) collective-permute-start(bf16[32,1024]{1,0:T(8,128)(2,1)S(1)} %add_convert_fusion.1), channel_id=1, source_target_pairs={{0,32},{16,48},{32,0},{48,16},{64,96},{80,112},{96,64},{112,80},{1... | collective-permute-start | bytes 196616 | tf_op jit(solution)/shard_map/ppermute | solution.py:191
  85.0 7.6 %collective-permute-start.8 = (bf16[32,1024]{1,0:T(8,128)(2,1)S(1)}, bf16[32,1024]{1,0:T(8,128)(2,1)S(1)}, u32[]{:S(2)}, u32[]{:S(2)}) collective-permute-start(bf16[32,1024]{1,0:T(8,128)(2,1)S(1)} %add_convert_fusion.1), channel_id=1, source_target_pairs={{0,16},{16,0},{32,48},{48,32},{64,80},{80,64},{96,112},{112,96},{1... | collective-permute-start | bytes 196616 | tf_op jit(solution)/shard_map/ppermute | solution.py:191
  92.7 5.3 %collective-permute-start.11 = (bf16[32,1024]{1,0:T(8,128)(2,1)S(1)}, bf16[32,1024]{1,0:T(8,128)(2,1)S(1)}, u32[]{:S(2)}, u32[]{:S(2)}) collective-permute-start(bf16[32,1024]{1,0:T(8,128)(2,1)S(1)} %add_convert_fusion), channel_id=1, source_target_pairs={{0,96},{16,112},{32,64},{48,80},{64,32},{80,48},{96,0},{112,16},{1... | collective-permute-start | bytes 196616 | tf_op jit(solution)/shard_map/ppermute | solution.py:191
  110.4 5.8 %collective-permute-start.12 = (bf16[8,32,1024]{2,1,0:T(8,128)(2,1)S(1)}, bf16[8,32,1024]{2,1,0:T(8,128)(2,1)S(1)}, u32[]{:S(2)}, u32[]{:S(2)}) collective-permute-start(bf16[8,32,1024]{2,1,0:T(8,128)(2,1)S(1)} %all_to_all.21), channel_id=1, source_target_pairs={{0,1},{1,0},{2,3},{3,2},{4,5},{5,4},{6,7},{7,6},{8,9},{9,8},{10,11... | collective-permute-start | bytes 1572872 | tf_op jit(solution)/shard_map/ppermute | solution.py:191

commit v6 on v5

--- a/solution.py
+++ b/solution.py
@@ -239,7 +239,11 @@
     )
     att = lax.all_to_all(att, "lon", 0, 0, tiled=True)
     grads = call(backward_kernel, shape(lonb, HALF + CELLS, PAIR), slabs, stats, vmem=MID_BYTES)
-    att, grads = lax.optimization_barrier((att, grads))
+    place = lax.axis_index("lat")
+    rows = HD // lats
+    own_weight = lax.dynamic_slice_in_dim(out_weight, place * rows, rows, 0).astype(F32)
+    kept = decay_rate * average
+    att, grads, own_weight, kept = lax.optimization_barrier((att, grads, own_weight, kept))
     rows = HD // lats
     quarters = lats // 4
     place = lax.axis_index("lat")
@@ -262,9 +266,8 @@
     across = lax.ppermute(far, ("lon", "lat"), [(i * lats + j, (i ^ 8) * lats + (j ^ 2)) for i, j in both])
     total = plus(near, pairwise(near, "lon", 8)) + plus(pairwise(far, "lat", 2), across)
     total = paired(joined(total, 1, 2, 3), 6)
-    own_weight = lax.dynamic_slice_in_dim(out_weight, place * rows, rows, 0).astype(F32)
     updated = own_weight - learn_rate * total
-    averaged = decay_rate * average + (1.0 - decay_rate) * updated
+    averaged = kept + (1.0 - decay_rate) * updated
     averaged, grads = lax.optimization_barrier((averaged, grads))
     copies = jnp.broadcast_to(averaged.astype(BF)[None], (lats // 2, rows, D))
     mine = lax.all_to_all(copies, "lat", 0, 0, axis_index_groups=same_core, tiled=True)

time: 118 us -> 118 us (level)
  blocking collectives: 45.2 us -> 10.6 us
  waiting for transfers between devices: 22.3 us -> 44.4 us
  starting transfers between devices: 31.8 us -> 44 us
    all_to_all x1 -> x0, blocking collectives: 34.4 us -> none  [on_device(): slabs = lax.all_to_all(slabs, 'lon', 0, 0, tiled=True)]
    all_to_all x0 -> x1, waiting for transfers between devices: none -> 21.1 us  [on_device(): slabs = lax.all_to_all(slabs, 'lon', 0, 0, tiled=True)]
    all_to_all x0 -> x1, starting transfers between devices: none -> 11.9 us  [on_device(): slabs = lax.all_to_all(slabs, 'lon', 0, 0, tiled=True)]
  transfers between devices with their start and end apart: 15 -> 16, of which waited for: 10 -> 10; matrix products, arithmetic and copies ran while one was open for 1% -> 1% of each run, Pallas kernels for 6% -> 9%
where the time goes in v6:
time: 118 us; the launch traced here: 117 us
  waiting for transfers between devices  44.4 us (38%)
  starting transfers between devices  44 us (37%)
  Pallas kernels  14.4 us (12%)
  blocking collectives  10.6 us (9%)
  other arithmetic  2.84 us (2%)
    all_to_all x1, waiting for transfers between devices, on_device(): slabs = lax.all_to_all(slabs, 'lon', 0, 0, tiled=True)  21.1 us
    ppermute x12, waiting for transfers between devices, pairwise(): lax.ppermute(x, axis, [(i, i ^ bit) for i in range(lax.axis_size(axis))])  18.1 us
    ppermute x12, starting transfers between devices, pairwise(): lax.ppermute(x, axis, [(i, i ^ bit) for i in range(lax.axis_size(axis))])  17 us
    pallas_call x5, Pallas kernels, call(): pl.pallas_call(kernel, out_shape=outs, in_specs=on_chip, scratch_shapes=s...  14.4 us
    all_to_all x1, starting transfers between devices, on_device(): slabs = lax.all_to_all(slabs, 'lon', 0, 0, tiled=True)  11.9 us
    all_to_all x1, blocking collectives, on_device(): lax.all_to_all(copies, 'lat', 0, 0, axis_index_groups=same_core, tiled=True)  10.6 us
    all_to_all x1, starting transfers between devices, on_device(): att = lax.all_to_all(att, 'lon', 0, 0, tiled=True)  6.88 us
    all_to_all x1, starting transfers between devices, on_device(): grads = lax.all_to_all(grads, 'lon', 0, 0, tiled=True)  6.38 us
  transfers between devices with their start and end apart: 16, of which 10 were waited for; matrix products, arithmetic and copies ran while one was open for 1% of the time, Pallas kernels for 9%

profile of v6, /device:TPU:1, one launch (start us, length us, event | category | flops | bytes accessed | tf_op | source)
XLA Modules:
  0.0 117.1 jit_solution(1885258618372551627)
XLA Ops:
  0.6 3.0 %shard_map.128 = bf16[16,208,128]{2,1,0:T(8,128)(2,1)} custom-call(s32[2,1,8]{2,1,0:T(1,128)} %lon_ref.1, s32[2,1,8]{2,1,0:T(1,128)} %lat_ref.1, s32[2]{0:T(128)} %bitcast.27, bf16[128,512]{1,0:T(8,128)(2,1)} %bitcast.24, bf16[128,512]{1,0:T(8,128)(2,1)} %bitcast.25, bf16[128,512]{1,0:T(8,128)(2,1)} %bitcast.26, bf16[128,1024]{1,0:T(8,128)(2,1)} %bitcast.20, ...), custom_call_target="tpu_custom_call" | custom-call | tf_op jit(solution)/shard_map/pallas_call | solution.py:177
  3.6 0.0 copy-start
  3.6 11.9 %all-to-all-start = ((bf16[16,208,128]{2,1,0:T(8,128)(2,1)}), bf16[16,208,128]{2,1,0:T(8,128)(2,1)S(1)}, u32[]{:S(2)}, u32[]{:S(2)}) async-start(bf16[16,208,128]{2,1,0:T(8,128)(2,1)} %shard_map.128), calls=%async_computation | async-start | bytes 1703936 | tf_op jit(solution)/shard_map/all_to_all | solution.py:231
  15.5 0.0 copy-done
  15.5 1.0 collective-permute-start.1
  16.5 21.1 %all-to-all-done.in_ref = bf16[16,208,128]{2,1,0:T(8,128)(2,1)S(1)} async-done(((bf16[16,208,128]{2,1,0:T(8,128)(2,1)}), bf16[16,208,128]{2,1,0:T(8,128)(2,1)S(1)}, u32[]{:S(2)}, u32[]{:S(2)}) %all-to-all-start) | async-done | bytes 852000 | tf_op jit(solution)/shard_map/all_to_all | solution.py:231
  37.7 3.5 %shard_map.129 = (bf16[16,32,128]{2,1,0:T(8,128)(2,1)}, f32[8,1024]{1,0:T(8,128)S(1)}) custom-call(bf16[16,208,128]{2,1,0:T(8,128)(2,1)S(1)} %all-to-all-done.in_ref), custom_call_target="tpu_custom_call" | custom-call | tf_op jit(solution)/shard_map/pallas_call | solution.py:177
  41.2 0.0 copy-start.1
  41.2 6.9 %all-to-all-start.1 = ((bf16[16,32,128]{2,1,0:T(8,128)(2,1)}), bf16[16,32,128]{2,1,0:T(8,128)(2,1)S(1)}, u32[]{:S(2)}, u32[]{:S(2)}) async-start(bf16[16,32,128]{2,1,0:T(8,128)(2,1)} %get-tuple-element.20), calls=%async_computation.1 | async-start | bytes 262144 | tf_op jit(solution)/shard_map/all_to_all | solution.py:240
  48.1 0.0 copy-done.1
  48.1 0.9 dynamic-slice_convert_fusion
  49.0 6.4 %shard_map.130 = bf16[16,160,128]{2,1,0:T(8,128)(2,1)} custom-call(bf16[16,208,128]{2,1,0:T(8,128)(2,1)S(1)} %all-to-all-done.in_ref, f32[8,1024]{1,0:T(8,128)S(1)} %get-tuple-element.21.stat_ref), custom_call_target="tpu_custom_call" | custom-call | tf_op jit(solution)/shard_map/pallas_call | solution.py:177
  55.4 1.6 %all-to-all-done.1.att_ref = bf16[16,32,128]{2,1,0:T(8,128)(2,1)S(1)} async-done(((bf16[16,32,128]{2,1,0:T(8,128)(2,1)}), bf16[16,32,128]{2,1,0:T(8,128)(2,1)S(1)}, u32[]{:S(2)}, u32[]{:S(2)}) %all-to-all-start.1) | async-done | bytes 131104 | tf_op jit(solution)/shard_map/all_to_all | solution.py:240
  57.0 2.1 %collective-permute-start = (bf16[16,32,128]{2,1,0:T(8,128)(2,1)S(1)}, bf16[16,32,128]{2,1,0:T(8,128)(2,1)S(1)}, u32[]{:S(2)}, u32[]{:S(2)}) collective-permute-start(bf16[16,32,128]{2,1,0:T(8,128)(2,1)S(1)} %all-to-all-done.1.att_ref), channel_id=1, source_target_pairs={{0,1},{1,0},{2,3},{3,2},{4,5},{5,4},{6,7},{7,6},{8,9},{9,8},{10,11... | collective-permute-start | bytes 393224 | tf_op jit(solution)/shard_map/ppermute | solution.py:191
  59.1 0.0 collective-permute-done.1.other_up_ref
  59.1 1.0 collective-permute-done.other_att_ref
  60.1 0.6 shard_map.131
  60.7 1.3 %collective-permute-start.2 = (bf16[2,32,1024]{2,1,0:T(8,128)(2,1)S(1)}, bf16[2,32,1024]{2,1,0:T(8,128)(2,1)S(1)}, u32[]{:S(2)}, u32[]{:S(2)}) collective-permute-start(bf16[2,32,1024]{2,1,0:T(8,128)(2,1)S(1)} %get-tuple-element.26), channel_id=1, source_target_pairs={{0,4},{1,5},{2,6},{3,7},{4,0},{5,1},{6,2},{7,3},{8,12},{9,13},{10,... | collective-permute-start | bytes 393224 | tf_op jit(solution)/shard_map/ppermute | solution.py:191
  62.0 2.4 %collective-permute-start.3 = (bf16[2,32,1024]{2,1,0:T(8,128)(2,1)S(1)}, bf16[2,32,1024]{2,1,0:T(8,128)(2,1)S(1)}, u32[]{:S(2)}, u32[]{:S(2)}) collective-permute-start(bf16[2,32,1024]{2,1,0:T(8,128)(2,1)S(1)} %get-tuple-element.27), channel_id=1, source_target_pairs={{0,8},{1,9},{2,10},{3,11},{4,12},{5,13},{6,14},{7,15},{8,0},{9,1},... | collective-permute-start | bytes 393224 | tf_op jit(solution)/shard_map/ppermute | solution.py:191
  64.4 0.2 collective-permute-start.4
  64.7 6.4 %all-to-all-start.2 = ((bf16[16,160,128]{2,1,0:T(8,128)(2,1)}), bf16[16,160,128]{2,1,0:T(8,128)(2,1)S(1)}, u32[]{:S(2)}, u32[]{:S(2)}) async-start(bf16[16,160,128]{2,1,0:T(8,128)(2,1)} %shard_map.130), calls=%async_computation.2 | async-start | bytes 1310720 | tf_op jit(solution)/shard_map/all_to_all | solution.py:262
  71.0 0.0 collective-permute-done.2
  71.1 0.0 collective-permute-done.3
  71.1 2.0 %collective-permute-done.4 = bf16[2,32,1024]{2,1,0:T(8,128)(2,1)S(1)} collective-permute-done((bf16[2,32,1024]{2,1,0:T(8,128)(2,1)S(1)}, bf16[2,32,1024]{2,1,0:T(8,128)(2,1)S(1)}, u32[]{:S(2)}, u32[]{:S(2)}) %collective-permute-start.4) | collective-permute-done | bytes 131104 | tf_op jit(solution)/shard_map/ppermute | solution.py:191
  73.0 0.1 fusion
  73.1 1.2 %collective-permute-start.5 = (bf16[32,1024]{1,0:T(8,128)(2,1)S(1)}, bf16[32,1024]{1,0:T(8,128)(2,1)S(1)}, u32[]{:S(2)}, u32[]{:S(2)}) collective-permute-start(bf16[32,1024]{1,0:T(8,128)(2,1)S(1)} %get-tuple-element.39), channel_id=1, source_target_pairs={{0,128},{16,144},{32,160},{48,176},{64,192},{80,208},{96,224},{112... | collective-permute-start | bytes 196616 | tf_op jit(solution)/shard_map/ppermute | solution.py:191
  74.3 1.9 %collective-permute-start.7 = (bf16[32,1024]{1,0:T(8,128)(2,1)S(1)}, bf16[32,1024]{1,0:T(8,128)(2,1)S(1)}, u32[]{:S(2)}, u32[]{:S(2)}) collective-permute-start(bf16[32,1024]{1,0:T(8,128)(2,1)S(1)} %get-tuple-element.40), channel_id=1, source_target_pairs={{0,130},{1,131},{2,128},{3,129},{4,134},{5,135},{6,132},{7,133},{8... | collective-permute-start | bytes 196616 | tf_op jit(solution)/shard_map/ppermute | solution.py:266
  76.2 0.0 collective-permute-start.6
  76.2 3.3 %collective-permute-done.5 = bf16[32,1024]{1,0:T(8,128)(2,1)S(1)} collective-permute-done((bf16[32,1024]{1,0:T(8,128)(2,1)S(1)}, bf16[32,1024]{1,0:T(8,128)(2,1)S(1)}, u32[]{:S(2)}, u32[]{:S(2)}) %collective-permute-start.5) | collective-permute-done | bytes 65568 | tf_op jit(solution)/shard_map/ppermute | solution.py:191
  79.4 3.6 %collective-permute-done.7 = bf16[32,1024]{1,0:T(8,128)(2,1)S(1)} collective-permute-done((bf16[32,1024]{1,0:T(8,128)(2,1)S(1)}, bf16[32,1024]{1,0:T(8,128)(2,1)S(1)}, u32[]{:S(2)}, u32[]{:S(2)}) %collective-permute-start.7) | collective-permute-done | bytes 65568 | tf_op jit(solution)/shard_map/ppermute | solution.py:266
  83.1 0.0 collective-permute-done.6
  83.1 2.6 %collective-permute-start.10 = (bf16[32,1024]{1,0:T(8,128)(2,1)S(1)}, bf16[32,1024]{1,0:T(8,128)(2,1)S(1)}, u32[]{:S(2)}, u32[]{:S(2)}) collective-permute-start(bf16[32,1024]{1,0:T(8,128)(2,1)S(1)} %add_convert_fusion.1), channel_id=1, source_target_pairs={{0,48},{16,32},{32,16},{48,0},{64,112},{80,96},{96,80},{112,64},{1... | collective-permute-start | bytes 196616 | tf_op jit(solution)/shard_map/ppermute | solution.py:191
  85.7 0.0 collective-permute-start.9
  85.7 1.0 collective-permute-start.8
  86.7 2.9 %collective-permute-done.10 = bf16[32,1024]{1,0:T(8,128)(2,1)S(1)} collective-permute-done((bf16[32,1024]{1,0:T(8,128)(2,1)S(1)}, bf16[32,1024]{1,0:T(8,128)(2,1)S(1)}, u32[]{:S(2)}, u32[]{:S(2)}) %collective-permute-start.10) | collective-permute-done | bytes 65568 | tf_op jit(solution)/shard_map/ppermute | solution.py:191
  89.6 3.8 %collective-permute-done.9 = bf16[32,1024]{1,0:T(8,128)(2,1)S(1)} collective-permute-done((bf16[32,1024]{1,0:T(8,128)(2,1)S(1)}, bf16[32,1024]{1,0:T(8,128)(2,1)S(1)}, u32[]{:S(2)}, u32[]{:S(2)}) %collective-permute-start.9) | collective-permute-done | bytes 65568 | tf_op jit(solution)/shard_map/ppermute | solution.py:191
  93.4 0.0 collective-permute-done.8
  93.5 0.8 collective-permute-start.11
  94.3 4.6 %collective-permute-done.11 = bf16[32,1024]{1,0:T(8,128)(2,1)S(1)} collective-permute-done((bf16[32,1024]{1,0:T(8,128)(2,1)S(1)}, bf16[32,1024]{1,0:T(8,128)(2,1)S(1)}, u32[]{:S(2)}, u32[]{:S(2)}) %collective-permute-start.11) | collective-permute-done | bytes 65568 | tf_op jit(solution)/shard_map/ppermute | solution.py:191
  98.8 0.7 multiply_add_fusion
  99.5 0.0 all-to-all-done.2.in_ref
  99.6 10.6 %all_to_all.20 = bf16[8,32,1024]{2,1,0:T(8,128)(2,1)S(1)} all-to-all(bf16[8,32,1024]{2,1,0:T(8,128)(2,1)S(1)} %broadcast_in_dim.2), channel_id=1, replica_groups={{0,2,4,6,8,10,12,14},{1,3,5,7,9,11,13,15},{16,18,20,22,24,26,28,30},{17..., dimensions={0} | all-to-all | bytes 1048576 | tf_op jit(solution)/shard_map/all_to_all | solution.py:273
  110.1 4.2 %collective-permute-start.12 = (bf16[8,32,1024]{2,1,0:T(8,128)(2,1)S(1)}, bf16[8,32,1024]{2,1,0:T(8,128)(2,1)S(1)}, u32[]{:S(2)}, u32[]{:S(2)}) collective-permute-start(bf16[8,32,1024]{2,1,0:T(8,128)(2,1)S(1)} %all_to_all.20), channel_id=1, source_target_pairs={{0,1},{1,0},{2,3},{3,2},{4,5},{5,4},{6,7},{7,6},{8,9},{9,8},{10,11... | collective-permute-start | bytes 1572872 | tf_op jit(solution)/shard_map/ppermute | solution.py:191
  114.4 1.0 shard_map.132
  115.4 0.6 collective-permute-done.12
  115.9 0.1 select_bitcast_fusion.1
  116.0 1.1 pad_maximum_fusion
  (4 shorter events, 0.1 us)
Async XLA Ops:
  3.6 11.9 %copy-start = (bf16[2,64,1024]{2,1,0:T(8,128)(2,1)S(1)}, bf16[2,64,1024]{2,1,0:T(8,128)(2,1)}, u32[]{:S(2)}) copy-start(bf16[2,64,1024]{2,1,0:T(8,128)(2,1)} %param.12) | copy-start | bytes 786436
  3.6 34.1 %all-to-all-start = ((bf16[16,208,128]{2,1,0:T(8,128)(2,1)}), bf16[16,208,128]{2,1,0:T(8,128)(2,1)S(1)}, u32[]{:S(2)}, u32[]{:S(2)}) async-start(bf16[16,208,128]{2,1,0:T(8,128)(2,1)} %shard_map.128), calls=%async_computation | async-start | bytes 1703936 | tf_op jit(solution)/shard_map/all_to_all | solution.py:231
  15.5 43.6 %collective-permute-start.1 = (bf16[128,1024]{1,0:T(8,128)(2,1)S(1)}, bf16[128,1024]{1,0:T(8,128)(2,1)S(1)}, u32[]{:S(2)}, u32[]{:S(2)}) collective-permute-start(bf16[128,1024]{1,0:T(8,128)(2,1)S(1)} %bitcast.21), channel_id=1, source_target_pairs={{0,1},{1,0},{2,3},{3,2},{4,5},{5,4},{6,7},{7,6},{8,9},{9,8},{10,11... | collective-permute-start | bytes 786440 | tf_op jit(solution)/shard_map/ppermute | solution.py:191
  41.2 6.9 %copy-start.1 = (f32[32,1024]{1,0:T(8,128)S(1)}, f32[32,1024]{1,0:T(8,128)}, u32[]{:S(2)}) copy-start(f32[32,1024]{1,0:T(8,128)} %param.14) | copy-start | bytes 393220
  41.2 15.8 %all-to-all-start.1 = ((bf16[16,32,128]{2,1,0:T(8,128)(2,1)}), bf16[16,32,128]{2,1,0:T(8,128)(2,1)S(1)}, u32[]{:S(2)}, u32[]{:S(2)}) async-start(bf16[16,32,128]{2,1,0:T(8,128)(2,1)} %get-tuple-element.20), calls=%async_computation.1 | async-start | bytes 262144 | tf_op jit(solution)/shard_map/all_to_all | solution.py:240
  57.0 3.1 %collective-permute-start = (bf16[16,32,128]{2,1,0:T(8,128)(2,1)S(1)}, bf16[16,32,128]{2,1,0:T(8,128)(2,1)S(1)}, u32[]{:S(2)}, u32[]{:S(2)}) collective-permute-start(bf16[16,32,128]{2,1,0:T(8,128)(2,1)S(1)} %all-to-all-done.1.att_ref), channel_id=1, source_target_pairs={{0,1},{1,0},{2,3},{3,2},{4,5},{5,4},{6,7},{7,6},{8,9},{9,8},{10,11... | collective-permute-start | bytes 393224 | tf_op jit(solution)/shard_map/ppermute | solution.py:191
  60.7 10.3 %collective-permute-start.2 = (bf16[2,32,1024]{2,1,0:T(8,128)(2,1)S(1)}, bf16[2,32,1024]{2,1,0:T(8,128)(2,1)S(1)}, u32[]{:S(2)}, u32[]{:S(2)}) collective-permute-start(bf16[2,32,1024]{2,1,0:T(8,128)(2,1)S(1)} %get-tuple-element.26), channel_id=1, source_target_pairs={{0,4},{1,5},{2,6},{3,7},{4,0},{5,1},{6,2},{7,3},{8,12},{9,13},{10,... | collective-permute-start | bytes 393224 | tf_op jit(solution)/shard_map/ppermute | solution.py:191
  62.0 9.1 %collective-permute-start.3 = (bf16[2,32,1024]{2,1,0:T(8,128)(2,1)S(1)}, bf16[2,32,1024]{2,1,0:T(8,128)(2,1)S(1)}, u32[]{:S(2)}, u32[]{:S(2)}) collective-permute-start(bf16[2,32,1024]{2,1,0:T(8,128)(2,1)S(1)} %get-tuple-element.27), channel_id=1, source_target_pairs={{0,8},{1,9},{2,10},{3,11},{4,12},{5,13},{6,14},{7,15},{8,0},{9,1},... | collective-permute-start | bytes 393224 | tf_op jit(solution)/shard_map/ppermute | solution.py:191
  64.4 8.6 %collective-permute-start.4 = (bf16[2,32,1024]{2,1,0:T(8,128)(2,1)S(1)}, bf16[2,32,1024]{2,1,0:T(8,128)(2,1)S(1)}, u32[]{:S(2)}, u32[]{:S(2)}) collective-permute-start(bf16[2,32,1024]{2,1,0:T(8,128)(2,1)S(1)} %get-tuple-element.28), channel_id=1, source_target_pairs={{0,12},{1,13},{2,14},{3,15},{4,8},{5,9},{6,10},{7,11},{8,4},{9,5},... | collective-permute-start | bytes 393224 | tf_op jit(solution)/shard_map/ppermute | solution.py:191
  64.7 34.9 %all-to-all-start.2 = ((bf16[16,160,128]{2,1,0:T(8,128)(2,1)}), bf16[16,160,128]{2,1,0:T(8,128)(2,1)S(1)}, u32[]{:S(2)}, u32[]{:S(2)}) async-start(bf16[16,160,128]{2,1,0:T(8,128)(2,1)} %shard_map.130), calls=%async_computation.2 | async-start | bytes 1310720 | tf_op jit(solution)/shard_map/all_to_all | solution.py:262
  73.1 6.3 %collective-permute-start.5 = (bf16[32,1024]{1,0:T(8,128)(2,1)S(1)}, bf16[32,1024]{1,0:T(8,128)(2,1)S(1)}, u32[]{:S(2)}, u32[]{:S(2)}) collective-permute-start(bf16[32,1024]{1,0:T(8,128)(2,1)S(1)} %get-tuple-element.39), channel_id=1, source_target_pairs={{0,128},{16,144},{32,160},{48,176},{64,192},{80,208},{96,224},{112... | collective-permute-start | bytes 196616 | tf_op jit(solution)/shard_map/ppermute | solution.py:191
  74.3 8.8 %collective-permute-start.7 = (bf16[32,1024]{1,0:T(8,128)(2,1)S(1)}, bf16[32,1024]{1,0:T(8,128)(2,1)S(1)}, u32[]{:S(2)}, u32[]{:S(2)}) collective-permute-start(bf16[32,1024]{1,0:T(8,128)(2,1)S(1)} %get-tuple-element.40), channel_id=1, source_target_pairs={{0,130},{1,131},{2,128},{3,129},{4,134},{5,135},{6,132},{7,133},{8... | collective-permute-start | bytes 196616 | tf_op jit(solution)/shard_map/ppermute | solution.py:266
  76.2 6.9 %collective-permute-start.6 = (bf16[32,1024]{1,0:T(8,128)(2,1)S(1)}, bf16[32,1024]{1,0:T(8,128)(2,1)S(1)}, u32[]{:S(2)}, u32[]{:S(2)}) collective-permute-start(bf16[32,1024]{1,0:T(8,128)(2,1)S(1)} %get-tuple-element.40), channel_id=1, source_target_pairs={{0,2},{1,3},{2,0},{3,1},{4,6},{5,7},{6,4},{7,5},{8,10},{9,11},{10,... | collective-permute-start | bytes 196616 | tf_op jit(solution)/shard_map/ppermute | solution.py:191
  83.1 6.5 %collective-permute-start.10 = (bf16[32,1024]{1,0:T(8,128)(2,1)S(1)}, bf16[32,1024]{1,0:T(8,128)(2,1)S(1)}, u32[]{:S(2)}, u32[]{:S(2)}) collective-permute-start(bf16[32,1024]{1,0:T(8,128)(2,1)S(1)} %add_convert_fusion.1), channel_id=1, source_target_pairs={{0,48},{16,32},{32,16},{48,0},{64,112},{80,96},{96,80},{112,64},{1... | collective-permute-start | bytes 196616 | tf_op jit(solution)/shard_map/ppermute | solution.py:191
  85.7 7.7 %collective-permute-start.9 = (bf16[32,1024]{1,0:T(8,128)(2,1)S(1)}, bf16[32,1024]{1,0:T(8,128)(2,1)S(1)}, u32[]{:S(2)}, u32[]{:S(2)}) collective-permute-start(bf16[32,1024]{1,0:T(8,128)(2,1)S(1)} %add_convert_fusion.1), channel_id=1, source_target_pairs={{0,32},{16,48},{32,0},{48,16},{64,96},{80,112},{96,64},{112,80},{1... | collective-permute-start | bytes 196616 | tf_op jit(solution)/shard_map/ppermute | solution.py:191
  85.7 7.7 %collective-permute-start.8 = (bf16[32,1024]{1,0:T(8,128)(2,1)S(1)}, bf16[32,1024]{1,0:T(8,128)(2,1)S(1)}, u32[]{:S(2)}, u32[]{:S(2)}) collective-permute-start(bf16[32,1024]{1,0:T(8,128)(2,1)S(1)} %add_convert_fusion.1), channel_id=1, source_target_pairs={{0,16},{16,0},{32,48},{48,32},{64,80},{80,64},{96,112},{112,96},{1... | collective-permute-start | bytes 196616 | tf_op jit(solution)/shard_map/ppermute | solution.py:191
  93.5 5.3 %collective-permute-start.11 = (bf16[32,1024]{1,0:T(8,128)(2,1)S(1)}, bf16[32,1024]{1,0:T(8,128)(2,1)S(1)}, u32[]{:S(2)}, u32[]{:S(2)}) collective-permute-start(bf16[32,1024]{1,0:T(8,128)(2,1)S(1)} %add_convert_fusion), channel_id=1, source_target_pairs={{0,96},{16,112},{32,64},{48,80},{64,32},{80,48},{96,0},{112,16},{1... | collective-permute-start | bytes 196616 | tf_op jit(solution)/shard_map/ppermute | solution.py:191
  110.1 5.8 %collective-permute-start.12 = (bf16[8,32,1024]{2,1,0:T(8,128)(2,1)S(1)}, bf16[8,32,1024]{2,1,0:T(8,128)(2,1)S(1)}, u32[]{:S(2)}, u32[]{:S(2)}) collective-permute-start(bf16[8,32,1024]{2,1,0:T(8,128)(2,1)S(1)} %all_to_all.20), channel_id=1, source_target_pairs={{0,1},{1,0},{2,3},{3,2},{4,5},{5,4},{6,7},{7,6},{8,9},{9,8},{10,11... | collective-permute-start | bytes 1572872 | tf_op jit(solution)/shard_map/ppermute | solution.py:191
